TPU v7x, 256 devices: a whole 4x4x8 slice. The times are simulated.
256 devices in a mesh: hst: 4 (over x), local: 64 (over z, y, core).
Axes of the slice: x: 4, y: 4, z: 8, core: 2. Of those that a mesh axis runs over, the one named last changes fastest.
Arguments:
- table_rows: float32 [4, 8192, 128], P('hst', 'local'), may hold values from -2.5 to 2.5
- row_accum: float32 [4, 8192], P('hst', 'local'), may hold values from 0.1 to 1
- row_ids: int32 [4, 8, 32768], P('hst'), may hold values from 0 to 8191
- sketch_bits: int32 [4, 8, 32768], P('hst'), may hold values from 0 to 1
- cross_u: bfloat16 [512, 512], replicated, may hold values from -0.25 to 0.25
- cross_v: bfloat16 [512, 512], replicated, may hold values from -0.25 to 0.25
- cross_bias: float32 [512], replicated, may hold values from -3 to 3
- cotangent: bfloat16 [32768, 512], P(('hst', 'local')), may hold values from -6 to 6
Outputs:
- crossed: bfloat16 [32768, 512], P(('hst', 'local'))
- new_rows: float32 [4, 8192, 128], P('hst', 'local')
- new_accum: float32 [4, 8192], P('hst', 'local')
All inputs are finite; a program needn't handle non-finite values.
Results may differ from a plain program's by a relative error of at most 0.0023.
The roundings to bfloat16 on the way count: a program that leaves them out, or rounds other values in their place, can miss the bound.
Values sent between devices are 32-bit elements; how exact they have to be, the bound alone decides.
No kernel may reach another device: no remote copies, remote signals or barrier semaphores. Data moves between devices by JAX's collectives and lax.ppermute only.
A program may use at most 128 MiB of HBM per device.

v0:
```python
import jax
import jax.numpy as jnp
from jax import lax
from jax.sharding import PartitionSpec as P

learn_rate = 0.1


def sketch_counts(id_block, sign_block, row_count):
    row_numbers = jnp.arange(row_count, dtype=jnp.int32)
    total = jnp.zeros((row_count, id_block.shape[1]), jnp.float32)
    for entry in range(id_block.shape[0]):
        hits = id_block[entry][None, :] == row_numbers[:, None]
        total = total + jnp.where(hits, sign_block[entry][None, :], 0.0)
    return total


def contract_rows(counts, table):
    return lax.dot_general(
        counts,
        table,
        (((0,), (0,)), ((), ())),
        precision=lax.Precision.HIGHEST,
        preferred_element_type=jnp.float32,
    )


def per_device(
    table_rows, row_accum, row_ids, sketch_bits, cross_u, cross_v, cross_bias, cotangent
):
    n_hosts = lax.axis_size("hst")
    n_local = lax.axis_size("local")
    local_index = lax.axis_index("local")
    my_rows = table_rows[0]
    row_count = my_rows.shape[0]
    width = my_rows.shape[1]
    all_ids = row_ids[0]
    all_signs = (2 * sketch_bits[0] - 1).astype(jnp.float32)
    bag_size = all_ids.shape[0]
    batch_total = all_ids.shape[1]
    per_owner = batch_total // (n_hosts * n_local)
    own_ids = lax.dynamic_index_in_dim(
        all_ids.reshape(bag_size, n_hosts, n_local, per_owner), local_index, 2, keepdims=False
    ).reshape(bag_size, n_hosts * per_owner)
    own_signs = lax.dynamic_index_in_dim(
        all_signs.reshape(bag_size, n_hosts, n_local, per_owner), local_index, 2, keepdims=False
    ).reshape(bag_size, n_hosts * per_owner)
    piece = lax.all_gather(my_rows, "local", axis=0, tiled=True)
    pooled = contract_rows(sketch_counts(own_ids, own_signs, piece.shape[0]), piece).reshape(
        n_hosts, per_owner, width
    )
    features = lax.all_to_all(pooled, "hst", split_axis=0, concat_axis=0, tiled=True)
    base_x = features.transpose(1, 0, 2).reshape(per_owner, -1)
    low = jnp.dot(base_x.astype(jnp.bfloat16), cross_u, preferred_element_type=jnp.float32).astype(
        jnp.bfloat16
    )
    scale = jnp.dot(low, cross_v, preferred_element_type=jnp.float32) + cross_bias
    crossed = (base_x * scale + base_x).astype(jnp.bfloat16)
    upstream = cotangent.astype(jnp.float32)
    mixed = (upstream * base_x).astype(jnp.bfloat16)
    back_low = jnp.dot(mixed, cross_v.T, preferred_element_type=jnp.float32).astype(jnp.bfloat16)
    grad_x = upstream * (scale + 1.0) + jnp.dot(
        back_low, cross_u.T, preferred_element_type=jnp.float32
    )
    grad_tables = grad_x.reshape(per_owner, -1, width).transpose(1, 0, 2)
    grad_back = lax.all_to_all(grad_tables, "hst", split_axis=0, concat_axis=0, tiled=True)
    flat_grads = grad_back.reshape(-1, width)
    counts = sketch_counts(own_ids, own_signs, row_count * lax.axis_size("local"))
    row_grads = lax.psum_scatter(
        jnp.dot(
            counts, flat_grads, precision=lax.Precision.HIGHEST, preferred_element_type=jnp.float32
        ),
        "local",
        scatter_dimension=0,
        tiled=True,
    )
    new_accum = row_accum[0] + jnp.mean(row_grads * row_grads, axis=1)
    new_rows = my_rows - learn_rate * row_grads / jnp.sqrt(new_accum)[:, None]
    return (crossed, new_rows[None], new_accum[None])


def solution(mesh):
    in_specs = (
        P("hst", "local", None),
        P("hst", "local"),
        P("hst", None, None),
        P("hst", None, None),
        P(),
        P(),
        P(),
        P(("hst", "local"), None),
    )
    out_specs = (P(("hst", "local"), None), P("hst", "local", None), P("hst", "local"))
    return jax.shard_map(
        per_device, mesh=mesh, in_specs=in_specs, out_specs=out_specs, check_vma=False
    )
```

profile of v0, /device:TPU:1, one launch (start us, length us, event | category | flops | bytes accessed | tf_op | source)
XLA Modules:
  0.0 330.9 jit_solution(12187337444011199317)
XLA Ops:
  7.2 0.0 copy-start
  7.2 0.0 all-gather.3.cloned.1.call-start
  7.2 0.7 all-gather.3.cloned.1.call-update
  7.9 0.0 reduce-scatter.2.cloned.1.call-start
  8.0 1.3 add_convert_fusion
  9.3 1.2 constant_dynamic-slice_fusion.13
  10.5 83.5 %all-gather.3.cloned.1.call-done = f32[1,8192,128]{2,1,0:T(8,128)} async-done(((f32[1,128,128]{2,1,0:T(8,128)}), f32[1,8192,128]{2,1,0:T(8,128)}) %all-gather.3.cloned.1.call-update) | async-done | bytes 4194320 | tf_op jit(solution)/shard_map/all_gather | solution.py:48
  94.1 41.2 %fusion.1 = f32[512,128]{1,0:T(8,128)S(1)} fusion(f32[512]{0:T(512)S(1)} %bitcast.87, s32[512]{0:T(512)S(1)} %bitcast.103, f32[512]{0:T(512)S(1)} %bitcast.75, s32[512]{0:T(512)S(1)} %bitcast.91, f32[512]{0:T(512)S(1)} %bitcast.77, s32[512]{0:T(512)S(1)} %bitcast.93, f32[512]{0:T(512)S(1)} %bitcast.79, s32[512]{0:T(512)S(1)} %bitcast.95, ...), kind=kOutput, calls=%fused_computation.10 | convolution fusion | flops 6538919936 | bytes 4489216 | tf_op jit(solution)/shard_map/dot_general | solution.py:19
  135.3 10.0 %all_to_all.10 = f32[4,128,128]{2,1,0:T(8,128)S(1)} all-to-all(f32[4,128,128]{2,1,0:T(8,128)S(1)} %bitcast.72), channel_id=1, replica_groups=mesh['hst'=4,'local'=64] {'hst'}, dimensions={0} | all-to-all | bytes 524288 | tf_op jit(solution)/shard_map/all_to_all | solution.py:52
  145.3 0.0 copy-done
  145.3 0.0 copy-done.1
  145.3 0.0 copy-done.4
  145.3 1.1 fusion.5
  146.4 0.0 copy-done.3
  146.4 0.5 fusion.3
  147.0 7.9 %all_to_all.11 = f32[4,128,128]{2,1,0:T(8,128)S(1)} all-to-all(f32[4,128,128]{2,1,0:T(8,128)S(1)} %bitcast.70), channel_id=1, replica_groups=mesh['hst'=4,'local'=64] {'hst'}, dimensions={0} | all-to-all | bytes 524288 | tf_op jit(solution)/shard_map/all_to_all | solution.py:66
  154.9 29.9 %fusion = f32[8192,128]{1,0:T(8,128)} fusion(f32[512,128]{1,0:T(8,128)S(1)} %bitcast.71, f32[512]{0:T(512)S(1)} %bitcast.88, s32[512]{0:T(512)S(1)} %bitcast.104, f32[512]{0:T(512)S(1)} %bitcast.76, s32[512]{0:T(512)S(1)} %bitcast.92, f32[512]{0:T(512)S(1)} %bitcast.78, s32[512]{0:T(512)S(1)} %bitcast.94, f32[512]{0:T(512)S(1)} %bitcast.80, ...), kind=kOutput, calls=%fused_computation.9 | convolution fusion | flops 6538919936 | bytes 4489216 | tf_op jit(solution)/shard_map/dot_general | solution.py:70
  184.8 0.0 reduce-scatter.2.cloned.1.call-update
  184.8 136.2 %reduce-scatter.2.cloned.1.call-done = f32[128,128]{1,0:T(8,128)} async-done(((f32[8192,128]{1,0:T(8,128)}), f32[128,128]{1,0:T(8,128)}) %reduce-scatter.2.cloned.1.call-update) | async-done | bytes 65552 | tf_op jit(solution)/shard_map/reduce_scatter | solution.py:69
  321.1 0.9 multiply_reduce_fusion
  322.0 0.0 copy-done.5
  322.0 0.5 bitcast_add_fusion
  322.5 0.0 copy-done.2
  322.5 1.6 fusion.8
  (8 shorter events, 0.1 us)
Async XLA Ops:
  7.2 138.2 %copy-start = (bf16[512,512]{1,0:T(8,128)(2,1)S(1)}, bf16[512,512]{1,0:T(8,128)(2,1)}, u32[]{:S(2)}) copy-start(bf16[512,512]{1,0:T(8,128)(2,1)} %param.13) | copy-start | bytes 1572868
  7.2 86.9 %all-gather.3.cloned.1.call-start = ((), (), s32[]{:S(2)}) async-start(), calls=%async_computation.4 | async-start | bytes 4259840 | tf_op jit(solution)/shard_map/all_gather | solution.py:48
  7.9 313.1 %reduce-scatter.2.cloned.1.call-start = ((), (), s32[]{:S(2)}) async-start(), calls=%async_computation.3 | async-start | bytes 4259840 | tf_op jit(solution)/shard_map/reduce_scatter | solution.py:69
  94.1 51.3 %copy-start.1 = (bf16[512,512]{1,0:T(8,128)(2,1)S(1)}, bf16[512,512]{1,0:T(8,128)(2,1)}, u32[]{:S(2)}) copy-start(bf16[512,512]{1,0:T(8,128)(2,1)} %param.12) | copy-start | bytes 1572868
  94.1 51.3 %copy-start.4 = (f32[512]{0:T(512)S(1)}, f32[512]{0:T(512)}, u32[]{:S(2)}) copy-start(f32[512]{0:T(512)} %param.14) | copy-start | bytes 6148
  94.1 52.3 %copy-start.3 = (bf16[128,512]{1,0:T(8,128)(2,1)S(1)}, bf16[128,512]{1,0:T(8,128)(2,1)}, u32[]{:S(2)}) copy-start(bf16[128,512]{1,0:T(8,128)(2,1)} %param.15) | copy-start | bytes 393220
  184.8 137.2 %copy-start.5 = (f32[1,128]{1,0:T(1,128)S(1)}, f32[1,128]{1,0:T(1,128)}, u32[]{:S(2)}) copy-start(f32[1,128]{1,0:T(1,128)} %param.9) | copy-start | bytes 1540
  184.8 137.7 %copy-start.2 = (f32[1,128,128]{2,1,0:T(8,128)S(1)}, f32[1,128,128]{2,1,0:T(8,128)}, u32[]{:S(2)}) copy-start(f32[1,128,128]{2,1,0:T(8,128)} %param.8) | copy-start | bytes 196612
Sparse Core Ops, SparseCore 0:
  10.8 83.2 all-gather.2
  185.0 136.0 reduce-scatter.1
where the time goes:
time: 336 us; the launch traced here: 331 us
  waiting for transfers between devices  220 us (65%)
  matrix products  72.8 us (22%)
  blocking collectives  17.9 us (5%)
  between operations  14.1 us (4%)
  other arithmetic  4.35 us (1%)
    reduce_scatter x1, waiting for transfers between devices, per_device(): lax.psum_scatter(jnp.dot(counts, flat_grads, precision=lax.Precision.HIGH...  136 us
    all_gather x1, waiting for transfers between devices, per_device(): piece = lax.all_gather(my_rows, 'local', axis=0, tiled=True)  83.5 us
    dot_general x1, matrix products, contract_rows(): lax.dot_general(counts, table, (((0,), (0,)), ((), ())), precision=lax.Pr...  41.2 us
    dot_general x1, matrix products, per_device(): jnp.dot(counts, flat_grads, precision=lax.Precision.HIGHEST, preferred_el...  29.9 us
    all_to_all x1, blocking collectives, per_device(): lax.all_to_all(pooled, 'hst', split_axis=0, concat_axis=0, tiled=True)  10 us
    all_to_all x1, blocking collectives, per_device(): lax.all_to_all(grad_tables, 'hst', split_axis=0, concat_axis=0, tiled=True)  7.92 us
  transfers between devices with their start and end apart: 2, of which 2 were waited for; matrix products, arithmetic and copies ran while one was open for 1% of the time, Pallas kernels for 0%

commit v1 on v0

v1 whole, which is shorter than its diff:
```python
import functools

import jax
import jax.numpy as jnp
from jax import lax
from jax.experimental import pallas as pl
from jax.experimental.pallas import tpu as pltpu
from jax.sharding import Mesh, PartitionSpec as P

learn_rate = 0.1
NX, NZ, NY, NC = 4, 8, 4, 2
RB, SB, E, BAG = 128, 128, 128, 8
SIZES = {"hst": NX, "z": NZ, "y": NY, "core": NC}
HALF_ROWS = NZ * RB
SAMPLES_Y = NX * SB
F32, BF16 = jnp.float32, jnp.bfloat16
VMEM = pltpu.CompilerParams(vmem_limit_bytes=40 << 20)


def move(array, axis, step):
    n = SIZES[axis]
    return lax.ppermute(array, axis, [(i, (i + step) % n) for i in range(n)])


def call(kernel, out_shapes, *operands, flops=0, moved=0):
    shapes = [jax.ShapeDtypeStruct(s, d) for s, d in out_shapes]
    return pl.pallas_call(
        kernel,
        out_shape=shapes,
        compiler_params=VMEM,
        cost_estimate=pl.CostEstimate(flops=flops, bytes_accessed=moved or 1 << 20, transcendentals=0),
    )(*operands)


def split_terms(value):
    high = value.astype(BF16)
    return jnp.concatenate([high, (value - high.astype(F32)).astype(BF16)], axis=1)


def counts_kernel(pos, ids_ref, bits_ref, out_ref):
    z, y, c = pos[1], pos[2], pos[3]
    rows16 = lax.broadcasted_iota(jnp.int32, (16, SB), 0).astype(jnp.int16)
    for dx in range(NX):
        x = (pos[0] + dx) & (NX - 1)
        ids = ids_ref[x, 0, 0, 0]
        rel = (((ids >> 7) & 1) ^ c) * HALF_ROWS + (((ids >> 10) - z) & (NZ - 1)) * RB + (ids & (RB - 1))
        rel = jnp.where(((ids >> 8) & (NY - 1)) == y, rel, -1)
        sign = (2 * bits_ref[x, 0, 0, 0] - 1).astype(F32)
        rels = [jnp.broadcast_to(rel[k : k + 1], (16, SB)).astype(jnp.int16) for k in range(BAG)]
        signs = [jnp.broadcast_to(sign[k : k + 1], (16, SB)).astype(BF16) for k in range(BAG)]

        def step(r, carry):
            here = rows16 + (r * 16).astype(jnp.int16)
            total = jnp.where(rels[0] == here, signs[0], BF16(0))
            for k in range(1, BAG):
                total = total + jnp.where(rels[k] == here, signs[k], BF16(0))
            out_ref[pl.ds(pl.multiple_of(r * 16, 16), 16), dx * SB : (dx + 1) * SB] = total
            return carry

        lax.fori_loop(0, NC * HALF_ROWS // 16, step, 0, unroll=16)


def counts_of(pos, ids, bits, dy):
    spec = pl.BlockSpec(
        (NX, 1, 1, 1, BAG, SB), lambda i, p: (0, p[1], (p[2] + dy) & (NY - 1), p[3], 0, 0)
    )
    return pl.pallas_call(
        counts_kernel,
        grid_spec=pltpu.PrefetchScalarGridSpec(
            num_scalar_prefetch=1,
            grid=(1,),
            in_specs=[spec, spec],
            out_specs=pl.BlockSpec((NC * HALF_ROWS, SAMPLES_Y), lambda i, p: (0, 0)),
        ),
        out_shape=jax.ShapeDtypeStruct((NC * HALF_ROWS, SAMPLES_Y), BF16),
        compiler_params=VMEM,
        cost_estimate=pl.CostEstimate(
            flops=3 * BAG * NC * HALF_ROWS * SAMPLES_Y, bytes_accessed=4 << 20, transcendentals=0
        ),
    )(pos, ids, bits)


def forward_kernel(own, p1, m1, p2, m2, up, down):
    up[:RB] = p1[...]
    up[RB:] = p2[: RB // 2]
    down[:RB] = m1[...]
    down[RB:] = m2[RB // 2 :]


def gather_kernel(own, p1, m1, p2, m2, p3, m3, out):
    h = RB // 2
    out[0:RB] = own[...]
    out[RB : 2 * RB] = m1[...]
    out[2 * RB : 3 * RB] = m2[...]
    out[3 * RB : 4 * RB] = m3[:RB]
    out[4 * RB : 4 * RB + h] = p3[RB:]
    out[4 * RB + h : 5 * RB] = m3[RB:]
    out[5 * RB : 6 * RB] = p3[:RB]
    out[6 * RB : 7 * RB] = p2[...]
    out[7 * RB : 8 * RB] = p1[...]


def pool_kernel(with_base, rows, c0, c1, c2, c3, *refs):
    base, outs, (totals,) = (refs[:4], refs[4:8], refs[8:]) if with_base else (None, refs[:4], refs[4:])
    step = pl.program_id(0)
    terms = split_terms(rows[...])
    for d, c in enumerate((c0, c1, c2, c3)):
        part = lax.dot_general(terms, c[...], (((0,), (0,)), ((), ())), preferred_element_type=F32)
        part = part[:E] + part[E:]

        @pl.when(step == 0)
        def _():
            totals[d] = part

        @pl.when(step == pl.num_programs(0) - 1)
        def _():
            for i in range(NX):
                s = slice(i * SB, (i + 1) * SB)
                value = (totals[d, :, s] + part[:, s]).T
                if with_base:
                    value = value + base[d][s]
                outs[d][s] = value


def pool(rows, counts, half, base=()):
    kb = HALF_ROWS // 2
    whole = pl.BlockSpec((SAMPLES_Y, E), lambda i: (0, 0))
    return pl.pallas_call(
        functools.partial(pool_kernel, len(base) > 0),
        grid=(2,),
        in_specs=[pl.BlockSpec((kb, E), lambda i: (i, 0))]
        + [pl.BlockSpec((kb, SAMPLES_Y), lambda i: (2 * half + i, 0))] * NY
        + [whole] * len(base),
        out_specs=[whole] * NY,
        out_shape=[jax.ShapeDtypeStruct((SAMPLES_Y, E), F32)] * NY,
        scratch_shapes=[pltpu.VMEM((NY, E, SAMPLES_Y), F32)],
        compiler_params=VMEM,
        cost_estimate=pl.CostEstimate(
            flops=4 * HALF_ROWS * NY * SAMPLES_Y * E, bytes_accessed=6 << 20, transcendentals=0
        ),
    )(rows, *counts, *base)


def owners_kernel(a, b, c, d, o0, o1, o2, o3):
    for i, out in enumerate((o0, o1, o2, o3)):
        s = slice(i * SB, (i + 1) * SB)
        out[...] = (a[s] + b[s]) + (c[s] + d[s])


def cross_kernel(pos, b0, b1, b2, b3, u, v, bias, cot, crossed, g0, g1, g2, g3, x_ref):
    def columns(d):
        return pl.ds(pl.multiple_of(((pos[0] - d) & (NX - 1)) * E, E), E)

    for d, b in enumerate((b0, b1, b2, b3)):
        x_ref[:, columns(d)] = b[...]
    base_x = x_ref[...]
    low = jnp.dot(base_x.astype(BF16), u[...], preferred_element_type=F32).astype(BF16)
    scale = jnp.dot(low, v[...], preferred_element_type=F32) + bias[...]
    crossed[...] = (base_x * scale + base_x).astype(BF16)
    upstream = cot[...].astype(F32)
    mixed = (upstream * base_x).astype(BF16)
    last = (((1,), (1,)), ((), ()))
    back_low = lax.dot_general(mixed, v[...], last, preferred_element_type=F32).astype(BF16)
    x_ref[...] = upstream * (scale + 1.0) + lax.dot_general(
        back_low, u[...], last, preferred_element_type=F32
    )
    for d, g in enumerate((g0, g1, g2, g3)):
        g[...] = x_ref[:, columns(d)]


def cross(pos, parts, u, v, bias, cot):
    vm = pl.BlockSpec(memory_space=pltpu.VMEM)
    return pl.pallas_call(
        cross_kernel,
        in_specs=[pl.BlockSpec(memory_space=pltpu.SMEM)] + [vm] * 8,
        out_specs=[vm] * 5,
        out_shape=[jax.ShapeDtypeStruct(cot.shape, BF16)] + [jax.ShapeDtypeStruct((SB, E), F32)] * NX,
        scratch_shapes=[pltpu.VMEM(cot.shape, F32)],
        compiler_params=VMEM,
        cost_estimate=pl.CostEstimate(flops=8 * SB * 512 * 512, bytes_accessed=2 << 20, transcendentals=0),
    )(pos, *parts, u, v, bias, cot)


def stack_kernel(a, b, c, d, out):
    for i, ref in enumerate((a, b, c, d)):
        out[i * SB : (i + 1) * SB] = ref[...]


def grads_kernel(c0, c1, c2, c3, g0, g1, g2, g3, out, terms):
    @pl.when(pl.program_id(0) == 0)
    def _():
        for d, g in enumerate((g0, g1, g2, g3)):
            terms[d] = split_terms(g[...])

    total = None
    for d, c in enumerate((c0, c1, c2, c3)):
        part = jnp.dot(c[...], terms[d], preferred_element_type=F32)
        total = part if total is None else total + part
    out[...] = total[:, :E] + total[:, E:]


def grads(counts, parts, half):
    rows = 256
    steps = HALF_ROWS // rows
    return pl.pallas_call(
        grads_kernel,
        grid=(steps,),
        in_specs=[pl.BlockSpec((rows, SAMPLES_Y), lambda i: (steps * half + i, 0))] * NY
        + [pl.BlockSpec((SAMPLES_Y, E), lambda i: (0, 0))] * NY,
        out_specs=pl.BlockSpec((rows, E), lambda i: (i, 0)),
        out_shape=jax.ShapeDtypeStruct((HALF_ROWS, E), F32),
        scratch_shapes=[pltpu.VMEM((NY, SAMPLES_Y, 2 * E), BF16)],
        compiler_params=VMEM,
        cost_estimate=pl.CostEstimate(
            flops=4 * HALF_ROWS * NY * SAMPLES_Y * E, bytes_accessed=6 << 20, transcendentals=0
        ),
    )(*counts, *parts)


def far_kernel(a, b, up, down, keep):
    h = RB // 2
    up[...] = a[3 * RB : 4 * RB + h] + b[3 * RB : 4 * RB + h]
    down[:RB] = a[5 * RB : 6 * RB] + b[5 * RB : 6 * RB]
    down[RB:] = a[4 * RB + h : 5 * RB] + b[4 * RB + h : 5 * RB]
    keep[: 3 * RB] = a[: 3 * RB] + b[: 3 * RB]
    keep[3 * RB :] = a[6 * RB :] + b[6 * RB :]


def near_kernel(keep, up, down, p1, p2, m2, m1):
    h = RB // 2
    p1[...] = keep[RB : 2 * RB] + up[:RB]
    p2[:h] = keep[2 * RB : 2 * RB + h] + up[RB:]
    p2[h:] = keep[2 * RB + h : 3 * RB]
    m2[:h] = keep[3 * RB : 3 * RB + h]
    m2[h:] = keep[3 * RB + h : 4 * RB] + down[RB:]
    m1[...] = keep[4 * RB :] + down[:RB]


def update_kernel(keep, a, b, c, d, rows, accum, new_rows, new_accum):
    grad = keep[:RB] + ((a[...] + b[...]) + (c[...] + d[...]))
    mean = jnp.sum(grad * grad, axis=1, keepdims=True) * (1.0 / E)
    mean_row = jnp.broadcast_to(mean, (RB, E)).T[:1]
    total = accum[...] + mean_row
    new_accum[...] = total
    total_column = jnp.broadcast_to(total, (E, RB)).T
    new_rows[...] = rows[...] - learn_rate * grad / jnp.sqrt(total_column)


def per_device(
    table_rows, row_accum, row_ids, sketch_bits, cross_u, cross_v, cross_bias, cotangent
):
    pos = jnp.stack([lax.axis_index(a) for a in ("hst", "z", "y", "core")]).astype(jnp.int32)
    own = table_rows[0]

    def by_owner(entries):
        return entries[0].reshape(BAG, -1, SB).transpose(1, 0, 2).reshape(NX, NZ, NY, NC, BAG, SB)

    ids, bits = by_owner(row_ids), by_owner(sketch_bits)
    p1, m1 = move(own, "z", 1), move(own, "z", -1)
    p2, m2 = move(own, "z", 2), move(own, "z", -2)
    counts = [counts_of(pos, ids, bits, d) for d in range(NY)]
    third = (RB + RB // 2, E)
    up, down = call(forward_kernel, [(third, F32)] * 2, own, p1, m1, p2, m2)
    p3, m3 = move(up, "z", 2), move(down, "z", -2)
    (rows,) = call(gather_kernel, [((HALF_ROWS, E), F32)], own, p1, m1, p2, m2, p3, m3)
    other_rows = move(rows, "core", 1)
    pooled = pool(rows, counts, 0)
    pooled = pool(other_rows, counts, 1, pooled)
    block = ((SB, E), F32)
    mine = call(
        owners_kernel,
        [block] * NX,
        pooled[0],
        move(pooled[1], "y", 1),
        move(pooled[2], "y", 2),
        move(pooled[3], "y", -1),
    )
    parts = [mine[0]] + [move(mine[d], "hst", d) for d in range(1, NX)]
    crossed, *grad_parts = cross(
        pos, parts, cross_u, cross_v, cross_bias.reshape(1, -1), cotangent
    )
    back = [grad_parts[0]] + [move(grad_parts[d], "hst", -d) for d in range(1, NX)]
    (bag_grads,) = call(stack_kernel, [((SAMPLES_Y, E), F32)], *back)
    all_grads = [bag_grads] + [move(bag_grads, "y", -d) for d in range(1, NY)]
    other_half = grads(counts, all_grads, 1)
    from_other = move(other_half, "core", 1)
    own_half = grads(counts, all_grads, 0)
    up, down, keep = call(
        far_kernel, [(third, F32)] * 2 + [((5 * RB, E), F32)], own_half, from_other
    )
    near = call(near_kernel, [block] * 4, keep, move(up, "z", 2), move(down, "z", -2))
    sums = [move(a, "z", s) for a, s in zip(near, (1, 2, -2, -1))]
    new_rows, new_accum = call(
        update_kernel, [block, ((1, RB), F32)], keep, *sums, own, row_accum
    )
    return (crossed, new_rows[None], new_accum)


def solution(mesh):
    grid = Mesh(mesh.devices.reshape(NX, NZ, NY, NC), ("hst", "z", "y", "core"))
    local = ("z", "y", "core")
    in_specs = (
        P("hst", local, None),
        P("hst", local),
        P("hst", None, None),
        P("hst", None, None),
        P(),
        P(),
        P(),
        P(("hst",) + local, None),
    )
    out_specs = (P(("hst",) + local, None), P("hst", local, None), P("hst", local))
    return jax.shard_map(
        per_device, mesh=grid, in_specs=in_specs, out_specs=out_specs, check_vma=False
    )
```

time: 336 us -> 117 us (0.35); the launches traced: 331 us -> 116 us
  waiting for transfers between devices: 220 us -> 41.3 us
  matrix products: 72.8 us -> 0 us
  starting transfers between devices: 0.08 us -> 48.5 us
  Pallas kernels: 0 us -> 23.5 us
  blocking collectives: 17.9 us -> 0 us
  between operations: 14.1 us -> 0.87 us
  other arithmetic: 4.35 us -> 0.08 us
    reduce_scatter x1 -> x0, waiting for transfers between devices: 136 us -> none  [per_device(): lax.psum_scatter(jnp.dot(counts, flat_grads, precision=lax.Precision.HIGH...]
    all_gather x1 -> x0, waiting for transfers between devices: 83.5 us -> none  [per_device(): piece = lax.all_gather(my_rows, 'local', axis=0, tiled=True)]
    dot_general x4 -> x0, matrix products: 72.8 us -> none  [the longest x1 41.2 us: contract_rows(): lax.dot_general(counts, table, (((0,), (0,)), ((), ())), precision=lax.Pr...]
    ppermute x0 -> x26, starting transfers between devices: none -> 48.5 us  [move(): return lax.ppermute(array, axis, [(i, (i + step) % n) for i in range(n)])]
    ppermute x0 -> x26, waiting for transfers between devices: none -> 41.3 us  [move(): return lax.ppermute(array, axis, [(i, (i + step) % n) for i in range(n)])]
    pallas_call x0 -> x16, Pallas kernels: none -> 23.5 us  [the longest x4 10.6 us: counts_of(): pl.pallas_call(counts_kernel, grid_spec=pltpu.PrefetchScalarGridSpec(num_...]
    all_to_all x2 -> x0, blocking collectives: 17.9 us -> none  [the longest x1 10 us: per_device(): lax.all_to_all(pooled, 'hst', split_axis=0, concat_axis=0, tiled=True)]
  transfers between devices with their start and end apart: 2 -> 26, of which waited for: 2 -> 16; matrix products, arithmetic and copies ran while one was open for 1% -> 0% of each run, Pallas kernels for 0% -> 13%
where the time goes in v1:
time: 117 us; the launch traced here: 116 us
  starting transfers between devices  48.5 us (41%)
  waiting for transfers between devices  41.3 us (35%)
  Pallas kernels  23.5 us (20%)
  local copies, waits for them, and re-layouts  2.11 us (2%)
    ppermute x26, starting transfers between devices, move(): return lax.ppermute(array, axis, [(i, (i + step) % n) for i in range(n)])  48.5 us
    ppermute x26, waiting for transfers between devices, move(): return lax.ppermute(array, axis, [(i, (i + step) % n) for i in range(n)])  41.3 us
    pallas_call x4, Pallas kernels, counts_of(): pl.pallas_call(counts_kernel, grid_spec=pltpu.PrefetchScalarGridSpec(num_...  10.6 us
    pallas_call x2, Pallas kernels, pool(): pl.pallas_call(functools.partial(pool_kernel, len(base) > 0), grid=(2,),...  6.11 us
    pallas_call x2, Pallas kernels, grads(): pl.pallas_call(grads_kernel, grid=(steps,), in_specs=[pl.BlockSpec((rows,...  3.85 us
  transfers between devices with their start and end apart: 26, of which 16 were waited for; matrix products, arithmetic and copies ran while one was open for 0% of the time, Pallas kernels for 13%

profile of v1, /device:TPU:1, one launch (start us, length us, event | category | flops | bytes accessed | tf_op | source)
XLA Modules:
  0.0 116.3 jit_solution(3634647227848616)
XLA Ops:
  0.6 6.9 %collective-permute-start.3 = (f32[128,128]{1,0:T(8,128)}, f32[128,128]{1,0:T(8,128)S(1)}, u32[]{:S(2)}, u32[]{:S(2)}) collective-permute-start(f32[128,128]{1,0:T(8,128)} %bitcast.25), channel_id=1, source_target_pairs={{0,48},{8,56},{16,0},{24,8},{32,16},{40,24},{48,32},{56,40},{1,49}... | collective-permute-start | bytes 196616 | tf_op jit(solution)/shard_map/ppermute | solution.py:22
  7.6 3.1 %collective-permute-start.1 = (f32[128,128]{1,0:T(8,128)}, f32[128,128]{1,0:T(8,128)S(1)}, u32[]{:S(2)}, u32[]{:S(2)}) collective-permute-start(f32[128,128]{1,0:T(8,128)} %bitcast.27), channel_id=1, source_target_pairs={{0,56},{8,0},{16,8},{24,16},{32,24},{40,32},{48,40},{56,48},{1,57}... | collective-permute-start | bytes 196616 | tf_op jit(solution)/shard_map/ppermute | solution.py:22
  10.7 3.0 %collective-permute-done.2.p2 = f32[128,128]{1,0:T(8,128)S(1)} collective-permute-done((f32[128,128]{1,0:T(8,128)}, f32[128,128]{1,0:T(8,128)S(1)}, u32[]{:S(2)}, u32[]{:S(2)}) %collective-permute-start.2) | collective-permute-done | bytes 65568 | tf_op jit(solution)/shard_map/ppermute | solution.py:22
  16.5 3.6 %collective-permute-start.5 = (f32[192,128]{1,0:T(8,128)S(1)}, f32[192,128]{1,0:T(8,128)S(1)}, u32[]{:S(2)}, u32[]{:S(2)}) collective-permute-start(f32[192,128]{1,0:T(8,128)S(1)} %get-tuple-element.32), channel_id=1, source_target_pairs={{0,48},{8,56},{16,0},{24,8},{32,16},{40,24},{48,32},{56,40},{1,49}... | collective-permute-start | bytes 294920 | tf_op jit(solution)/shard_map/ppermute | solution.py:22
  20.1 2.5 %collective-permute-done.4.p3 = f32[192,128]{1,0:T(8,128)S(1)} collective-permute-done((f32[192,128]{1,0:T(8,128)S(1)}, f32[192,128]{1,0:T(8,128)S(1)}, u32[]{:S(2)}, u32[]{:S(2)}) %collective-permute-start.4) | collective-permute-done | bytes 98336 | tf_op jit(solution)/shard_map/ppermute | solution.py:22
  22.7 3.1 %collective-permute-start.6 = (f32[1024,128]{1,0:T(8,128)S(1)}, f32[1024,128]{1,0:T(8,128)S(1)}, u32[]{:S(2)}, u32[]{:S(2)}) collective-permute-start(f32[1024,128]{1,0:T(8,128)S(1)} %shard_map.104.rows), channel_id=1, source_target_pairs={{0,1},{1,0},{2,3},{3,2},{4,5},{5,4},{6,7},{7,6},{8,9},{9,8},{10,11... | collective-permute-start | bytes 1572872 | tf_op jit(solution)/shard_map/ppermute | solution.py:22
  27.1 2.6 %shard_map.108.c3 = bf16[2048,512]{1,0:T(8,128)(2,1)S(1)} custom-call(s32[4]{0:T(128)S(1)} %pad_add_fusion.pos, s32[4,8,4,2,8,128]{5,4,3,2,1,0:T(8,128)S(1)} %bitcast.17, s32[4,8,4,2,8,128]{5,4,3,2,1,0:T(8,128)S(1)} %bitcast.21), custom_call_target="tpu_custom_call" | custom-call | flops 25165824 | bytes 4194304 | tf_op jit(solution)/shard_map/pallas_call | solution.py:67
  29.7 2.6 %shard_map.107.c2 = bf16[2048,512]{1,0:T(8,128)(2,1)S(1)} custom-call(s32[4]{0:T(128)S(1)} %pad_add_fusion.pos, s32[4,8,4,2,8,128]{5,4,3,2,1,0:T(8,128)S(1)} %bitcast.18, s32[4,8,4,2,8,128]{5,4,3,2,1,0:T(8,128)S(1)} %bitcast.22), custom_call_target="tpu_custom_call" | custom-call | flops 25165824 | bytes 4194304 | tf_op jit(solution)/shard_map/pallas_call | solution.py:67
  32.4 2.6 %shard_map.106.c1 = bf16[2048,512]{1,0:T(8,128)(2,1)S(1)} custom-call(s32[4]{0:T(128)S(1)} %pad_add_fusion.pos, s32[4,8,4,2,8,128]{5,4,3,2,1,0:T(8,128)S(1)} %bitcast.19, s32[4,8,4,2,8,128]{5,4,3,2,1,0:T(8,128)S(1)} %bitcast.23), custom_call_target="tpu_custom_call" | custom-call | flops 25165824 | bytes 4194304 | tf_op jit(solution)/shard_map/pallas_call | solution.py:67
  35.1 2.6 %shard_map.105.c0 = bf16[2048,512]{1,0:T(8,128)(2,1)S(1)} custom-call(s32[4]{0:T(128)S(1)} %pad_add_fusion.pos, s32[4,8,4,2,8,128]{5,4,3,2,1,0:T(8,128)S(1)} %bitcast.20, s32[4,8,4,2,8,128]{5,4,3,2,1,0:T(8,128)S(1)} %bitcast.24), custom_call_target="tpu_custom_call" | custom-call | flops 25165824 | bytes 4194304 | tf_op jit(solution)/shard_map/pallas_call | solution.py:67
  37.7 3.0 %shard_map.109 = (f32[512,128]{1,0:T(8,128)S(1)}, f32[512,128]{1,0:T(8,128)S(1)}, f32[512,128]{1,0:T(8,128)S(1)}, f32[512,128]{1,0:T(8,128)S(1)}) custom-call(f32[1024,128]{1,0:T(8,128)S(1)} %shard_map.104.rows, bf16[2048,512]{1,0:T(8,128)(2,1)S(1)} %shard_map.105.c0, bf16[2048,512]{1,0:T(8,128)(2,1)S(1)} %shard_map.106.c1, ...), custom_call_target="tpu_custom_call" | custom-call | flops 1073741824 | bytes 6291456 | tf_op jit(solution)/shard_map/pallas_call | solution.py:128
  40.8 3.1 %shard_map.110 = (f32[512,128]{1,0:T(8,128)S(1)}, f32[512,128]{1,0:T(8,128)S(1)}, f32[512,128]{1,0:T(8,128)S(1)}, f32[512,128]{1,0:T(8,128)S(1)}) custom-call(f32[1024,128]{1,0:T(8,128)S(1)} %collective-permute-done.6.rows, bf16[2048,512]{1,0:T(8,128)(2,1)S(1)} %shard_map.105.c0, bf16[2048,512]{1,0:T(8,128)(2,1)S(1)} %shard_map.106.c1, ...), custom_call_target="tpu_custom_call" | custom-call | flops 1073741824 | bytes 6291456 | tf_op jit(solution)/shard_map/pallas_call | solution.py:128
  45.3 2.6 %collective-permute-start.8 = (f32[512,128]{1,0:T(8,128)S(1)}, f32[512,128]{1,0:T(8,128)S(1)}, u32[]{:S(2)}, u32[]{:S(2)}) collective-permute-start(f32[512,128]{1,0:T(8,128)S(1)} %get-tuple-element.39), channel_id=1, source_target_pairs={{0,4},{2,6},{4,0},{6,2},{1,5},{3,7},{5,1},{7,3},{8,12},{10,14},{12... | collective-permute-start | bytes 786440 | tf_op jit(solution)/shard_map/ppermute | solution.py:22
  48.9 4.3 %collective-permute-done.7.b = f32[512,128]{1,0:T(8,128)S(1)} collective-permute-done((f32[512,128]{1,0:T(8,128)S(1)}, f32[512,128]{1,0:T(8,128)S(1)}, u32[]{:S(2)}, u32[]{:S(2)}) %collective-permute-start.7) | collective-permute-done | bytes 262176 | tf_op jit(solution)/shard_map/ppermute | solution.py:22
  53.2 6.7 %collective-permute-done.8.c = f32[512,128]{1,0:T(8,128)S(1)} collective-permute-done((f32[512,128]{1,0:T(8,128)S(1)}, f32[512,128]{1,0:T(8,128)S(1)}, u32[]{:S(2)}, u32[]{:S(2)}) %collective-permute-start.8) | collective-permute-done | bytes 262176 | tf_op jit(solution)/shard_map/ppermute | solution.py:22
  61.3 2.4 %collective-permute-start.11 = (f32[128,128]{1,0:T(8,128)S(1)}, f32[128,128]{1,0:T(8,128)S(1)}, u32[]{:S(2)}, u32[]{:S(2)}) collective-permute-start(f32[128,128]{1,0:T(8,128)S(1)} %get-tuple-element.43), channel_id=1, source_target_pairs={{0,128},{64,192},{128,0},{192,64},{1,129},{65,193},{129,1},{193,65... | collective-permute-start | bytes 196616 | tf_op jit(solution)/shard_map/ppermute | solution.py:22
  69.4 2.1 %collective-permute-start.13 = (f32[128,128]{1,0:T(8,128)S(1)}, f32[128,128]{1,0:T(8,128)S(1)}, u32[]{:S(2)}, u32[]{:S(2)}) collective-permute-start(f32[128,128]{1,0:T(8,128)S(1)} %get-tuple-element.47), channel_id=1, source_target_pairs={{0,192},{64,0},{128,64},{192,128},{1,193},{65,1},{129,65},{193,129... | collective-permute-start | bytes 196616 | tf_op jit(solution)/shard_map/ppermute | solution.py:22
  73.4 2.8 %collective-permute-done.14.c = f32[128,128]{1,0:T(8,128)S(1)} collective-permute-done((f32[128,128]{1,0:T(8,128)S(1)}, f32[128,128]{1,0:T(8,128)S(1)}, u32[]{:S(2)}, u32[]{:S(2)}) %collective-permute-start.14) | collective-permute-done | bytes 65568 | tf_op jit(solution)/shard_map/ppermute | solution.py:22
  77.8 1.9 %collective-permute-start.17 = (f32[512,128]{1,0:T(8,128)S(1)}, f32[512,128]{1,0:T(8,128)S(1)}, u32[]{:S(2)}, u32[]{:S(2)}) collective-permute-start(f32[512,128]{1,0:T(8,128)S(1)} %shard_map.113.g0), channel_id=1, source_target_pairs={{0,4},{2,6},{4,0},{6,2},{1,5},{3,7},{5,1},{7,3},{8,12},{10,14},{12... | collective-permute-start | bytes 786440 | tf_op jit(solution)/shard_map/ppermute | solution.py:22
  83.0 4.7 %collective-permute-done.17.g2 = f32[512,128]{1,0:T(8,128)S(1)} collective-permute-done((f32[512,128]{1,0:T(8,128)S(1)}, f32[512,128]{1,0:T(8,128)S(1)}, u32[]{:S(2)}, u32[]{:S(2)}) %collective-permute-start.17) | collective-permute-done | bytes 262176 | tf_op jit(solution)/shard_map/ppermute | solution.py:22
  90.0 4.9 %collective-permute-start.19 = (f32[1024,128]{1,0:T(8,128)S(1)}, f32[1024,128]{1,0:T(8,128)S(1)}, u32[]{:S(2)}, u32[]{:S(2)}) collective-permute-start(f32[1024,128]{1,0:T(8,128)S(1)} %shard_map.115), channel_id=1, source_target_pairs={{0,1},{1,0},{2,3},{3,2},{4,5},{5,4},{6,7},{7,6},{8,9},{9,8},{10,11... | collective-permute-start | bytes 1572872 | tf_op jit(solution)/shard_map/ppermute | solution.py:22
  96.8 2.4 %collective-permute-start.20 = (f32[192,128]{1,0:T(8,128)S(1)}, f32[192,128]{1,0:T(8,128)S(1)}, u32[]{:S(2)}, u32[]{:S(2)}) collective-permute-start(f32[192,128]{1,0:T(8,128)S(1)} %get-tuple-element.51), channel_id=1, source_target_pairs={{0,16},{8,24},{16,32},{24,40},{32,48},{40,56},{48,0},{56,8},{1,17}... | collective-permute-start | bytes 294920 | tf_op jit(solution)/shard_map/ppermute | solution.py:22
  101.2 5.2 %collective-permute-done.20.up = f32[192,128]{1,0:T(8,128)S(1)} collective-permute-done((f32[192,128]{1,0:T(8,128)S(1)}, f32[192,128]{1,0:T(8,128)S(1)}, u32[]{:S(2)}, u32[]{:S(2)}) %collective-permute-start.20) | collective-permute-done | bytes 98336 | tf_op jit(solution)/shard_map/ppermute | solution.py:22
  112.9 2.5 %collective-permute-done.25.d = f32[128,128]{1,0:T(8,128)S(1)} collective-permute-done((f32[128,128]{1,0:T(8,128)S(1)}, f32[128,128]{1,0:T(8,128)S(1)}, u32[]{:S(2)}, u32[]{:S(2)}) %collective-permute-start.25) | collective-permute-done | bytes 65568 | tf_op jit(solution)/shard_map/ppermute | solution.py:22
  (65 shorter events, 33.9 us)
Async XLA Ops:
  0.6 10.1 %collective-permute-start.3 = (f32[128,128]{1,0:T(8,128)}, f32[128,128]{1,0:T(8,128)S(1)}, u32[]{:S(2)}, u32[]{:S(2)}) collective-permute-start(f32[128,128]{1,0:T(8,128)} %bitcast.25), channel_id=1, source_target_pairs={{0,48},{8,56},{16,0},{24,8},{32,16},{40,24},{48,32},{56,40},{1,49}... | collective-permute-start | bytes 196616 | tf_op jit(solution)/shard_map/ppermute | solution.py:22
  7.6 6.1 %collective-permute-start.2 = (f32[128,128]{1,0:T(8,128)}, f32[128,128]{1,0:T(8,128)S(1)}, u32[]{:S(2)}, u32[]{:S(2)}) collective-permute-start(f32[128,128]{1,0:T(8,128)} %bitcast.26), channel_id=1, source_target_pairs={{0,16},{8,24},{16,32},{24,40},{32,48},{40,56},{48,0},{56,8},{1,17}... | collective-permute-start | bytes 196616 | tf_op jit(solution)/shard_map/ppermute | solution.py:22
  7.6 6.1 %collective-permute-start.1 = (f32[128,128]{1,0:T(8,128)}, f32[128,128]{1,0:T(8,128)S(1)}, u32[]{:S(2)}, u32[]{:S(2)}) collective-permute-start(f32[128,128]{1,0:T(8,128)} %bitcast.27), channel_id=1, source_target_pairs={{0,56},{8,0},{16,8},{24,16},{32,24},{40,32},{48,40},{56,48},{1,57}... | collective-permute-start | bytes 196616 | tf_op jit(solution)/shard_map/ppermute | solution.py:22
  10.7 4.9 %collective-permute-start = (f32[128,128]{1,0:T(8,128)}, f32[128,128]{1,0:T(8,128)S(1)}, u32[]{:S(2)}, u32[]{:S(2)}) collective-permute-start(f32[128,128]{1,0:T(8,128)} %bitcast.28), channel_id=1, source_target_pairs={{0,8},{8,16},{16,24},{24,32},{32,40},{40,48},{48,56},{56,0},{1,9},... | collective-permute-start | bytes 196616 | tf_op jit(solution)/shard_map/ppermute | solution.py:22
  16.5 6.2 %collective-permute-start.4 = (f32[192,128]{1,0:T(8,128)S(1)}, f32[192,128]{1,0:T(8,128)S(1)}, u32[]{:S(2)}, u32[]{:S(2)}) collective-permute-start(f32[192,128]{1,0:T(8,128)S(1)} %get-tuple-element.31), channel_id=1, source_target_pairs={{0,16},{8,24},{16,32},{24,40},{32,48},{40,56},{48,0},{56,8},{1,17}... | collective-permute-start | bytes 294920 | tf_op jit(solution)/shard_map/ppermute | solution.py:22
  16.5 6.1 %collective-permute-start.5 = (f32[192,128]{1,0:T(8,128)S(1)}, f32[192,128]{1,0:T(8,128)S(1)}, u32[]{:S(2)}, u32[]{:S(2)}) collective-permute-start(f32[192,128]{1,0:T(8,128)S(1)} %get-tuple-element.32), channel_id=1, source_target_pairs={{0,48},{8,56},{16,0},{24,8},{32,16},{40,24},{48,32},{56,40},{1,49}... | collective-permute-start | bytes 294920 | tf_op jit(solution)/shard_map/ppermute | solution.py:22
  22.7 18.1 %collective-permute-start.6 = (f32[1024,128]{1,0:T(8,128)S(1)}, f32[1024,128]{1,0:T(8,128)S(1)}, u32[]{:S(2)}, u32[]{:S(2)}) collective-permute-start(f32[1024,128]{1,0:T(8,128)S(1)} %shard_map.104.rows), channel_id=1, source_target_pairs={{0,1},{1,0},{2,3},{3,2},{4,5},{5,4},{6,7},{7,6},{8,9},{9,8},{10,11... | collective-permute-start | bytes 1572872 | tf_op jit(solution)/shard_map/ppermute | solution.py:22
  43.9 9.3 %collective-permute-start.7 = (f32[512,128]{1,0:T(8,128)S(1)}, f32[512,128]{1,0:T(8,128)S(1)}, u32[]{:S(2)}, u32[]{:S(2)}) collective-permute-start(f32[512,128]{1,0:T(8,128)S(1)} %get-tuple-element.38), channel_id=1, source_target_pairs={{0,2},{2,4},{4,6},{6,0},{1,3},{3,5},{5,7},{7,1},{8,10},{10,12},{12... | collective-permute-start | bytes 786440 | tf_op jit(solution)/shard_map/ppermute | solution.py:22
  45.3 14.7 %collective-permute-start.8 = (f32[512,128]{1,0:T(8,128)S(1)}, f32[512,128]{1,0:T(8,128)S(1)}, u32[]{:S(2)}, u32[]{:S(2)}) collective-permute-start(f32[512,128]{1,0:T(8,128)S(1)} %get-tuple-element.39), channel_id=1, source_target_pairs={{0,4},{2,6},{4,0},{6,2},{1,5},{3,7},{5,1},{7,3},{8,12},{10,14},{12... | collective-permute-start | bytes 786440 | tf_op jit(solution)/shard_map/ppermute | solution.py:22
  47.9 12.1 %collective-permute-start.9 = (f32[512,128]{1,0:T(8,128)S(1)}, f32[512,128]{1,0:T(8,128)S(1)}, u32[]{:S(2)}, u32[]{:S(2)}) collective-permute-start(f32[512,128]{1,0:T(8,128)S(1)} %get-tuple-element.40), channel_id=1, source_target_pairs={{0,6},{2,0},{4,2},{6,4},{1,7},{3,1},{5,3},{7,5},{8,14},{10,8},{12,... | collective-permute-start | bytes 786440 | tf_op jit(solution)/shard_map/ppermute | solution.py:22
  60.0 4.9 %collective-permute-start.10 = (f32[128,128]{1,0:T(8,128)S(1)}, f32[128,128]{1,0:T(8,128)S(1)}, u32[]{:S(2)}, u32[]{:S(2)}) collective-permute-start(f32[128,128]{1,0:T(8,128)S(1)} %get-tuple-element.42), channel_id=1, source_target_pairs={{0,64},{64,128},{128,192},{192,0},{1,65},{65,129},{129,193},{193,1... | collective-permute-start | bytes 196616 | tf_op jit(solution)/shard_map/ppermute | solution.py:22
  61.3 4.9 %collective-permute-start.11 = (f32[128,128]{1,0:T(8,128)S(1)}, f32[128,128]{1,0:T(8,128)S(1)}, u32[]{:S(2)}, u32[]{:S(2)}) collective-permute-start(f32[128,128]{1,0:T(8,128)S(1)} %get-tuple-element.43), channel_id=1, source_target_pairs={{0,128},{64,192},{128,0},{192,64},{1,129},{65,193},{129,1},{193,65... | collective-permute-start | bytes 196616 | tf_op jit(solution)/shard_map/ppermute | solution.py:22
  71.5 4.7 %collective-permute-start.14 = (f32[128,128]{1,0:T(8,128)S(1)}, f32[128,128]{1,0:T(8,128)S(1)}, u32[]{:S(2)}, u32[]{:S(2)}) collective-permute-start(f32[128,128]{1,0:T(8,128)S(1)} %get-tuple-element.48), channel_id=1, source_target_pairs={{0,128},{64,192},{128,0},{192,64},{1,129},{65,193},{129,1},{193,65... | collective-permute-start | bytes 196616 | tf_op jit(solution)/shard_map/ppermute | solution.py:22
  71.5 5.0 %collective-permute-start.15 = (f32[128,128]{1,0:T(8,128)S(1)}, f32[128,128]{1,0:T(8,128)S(1)}, u32[]{:S(2)}, u32[]{:S(2)}) collective-permute-start(f32[128,128]{1,0:T(8,128)S(1)} %get-tuple-element.49), channel_id=1, source_target_pairs={{0,64},{64,128},{128,192},{192,0},{1,65},{65,129},{129,193},{193,1... | collective-permute-start | bytes 196616 | tf_op jit(solution)/shard_map/ppermute | solution.py:22
  76.5 6.5 %collective-permute-start.18 = (f32[512,128]{1,0:T(8,128)S(1)}, f32[512,128]{1,0:T(8,128)S(1)}, u32[]{:S(2)}, u32[]{:S(2)}) collective-permute-start(f32[512,128]{1,0:T(8,128)S(1)} %shard_map.113.g0), channel_id=1, source_target_pairs={{0,2},{2,4},{4,6},{6,0},{1,3},{3,5},{5,7},{7,1},{8,10},{10,12},{12... | collective-permute-start | bytes 786440 | tf_op jit(solution)/shard_map/ppermute | solution.py:22
  77.8 10.0 %collective-permute-start.17 = (f32[512,128]{1,0:T(8,128)S(1)}, f32[512,128]{1,0:T(8,128)S(1)}, u32[]{:S(2)}, u32[]{:S(2)}) collective-permute-start(f32[512,128]{1,0:T(8,128)S(1)} %shard_map.113.g0), channel_id=1, source_target_pairs={{0,4},{2,6},{4,0},{6,2},{1,5},{3,7},{5,1},{7,3},{8,12},{10,14},{12... | collective-permute-start | bytes 786440 | tf_op jit(solution)/shard_map/ppermute | solution.py:22
  79.7 8.3 %collective-permute-start.16 = (f32[512,128]{1,0:T(8,128)S(1)}, f32[512,128]{1,0:T(8,128)S(1)}, u32[]{:S(2)}, u32[]{:S(2)}) collective-permute-start(f32[512,128]{1,0:T(8,128)S(1)} %shard_map.113.g0), channel_id=1, source_target_pairs={{0,6},{2,0},{4,2},{6,4},{1,7},{3,1},{5,3},{7,5},{8,14},{10,8},{12,... | collective-permute-start | bytes 786440 | tf_op jit(solution)/shard_map/ppermute | solution.py:22
  90.0 6.8 %collective-permute-start.19 = (f32[1024,128]{1,0:T(8,128)S(1)}, f32[1024,128]{1,0:T(8,128)S(1)}, u32[]{:S(2)}, u32[]{:S(2)}) collective-permute-start(f32[1024,128]{1,0:T(8,128)S(1)} %shard_map.115), channel_id=1, source_target_pairs={{0,1},{1,0},{2,3},{3,2},{4,5},{5,4},{6,7},{7,6},{8,9},{9,8},{10,11... | collective-permute-start | bytes 1572872 | tf_op jit(solution)/shard_map/ppermute | solution.py:22
  96.8 9.5 %collective-permute-start.20 = (f32[192,128]{1,0:T(8,128)S(1)}, f32[192,128]{1,0:T(8,128)S(1)}, u32[]{:S(2)}, u32[]{:S(2)}) collective-permute-start(f32[192,128]{1,0:T(8,128)S(1)} %get-tuple-element.51), channel_id=1, source_target_pairs={{0,16},{8,24},{16,32},{24,40},{32,48},{40,56},{48,0},{56,8},{1,17}... | collective-permute-start | bytes 294920 | tf_op jit(solution)/shard_map/ppermute | solution.py:22
  99.3 7.1 %collective-permute-start.21 = (f32[192,128]{1,0:T(8,128)S(1)}, f32[192,128]{1,0:T(8,128)S(1)}, u32[]{:S(2)}, u32[]{:S(2)}) collective-permute-start(f32[192,128]{1,0:T(8,128)S(1)} %get-tuple-element.52), channel_id=1, source_target_pairs={{0,48},{8,56},{16,0},{24,8},{32,16},{40,24},{48,32},{56,40},{1,49}... | collective-permute-start | bytes 294920 | tf_op jit(solution)/shard_map/ppermute | solution.py:22
  106.4 5.1 %collective-permute-start.22 = (f32[128,128]{1,0:T(8,128)S(1)}, f32[128,128]{1,0:T(8,128)S(1)}, u32[]{:S(2)}, u32[]{:S(2)}) collective-permute-start(f32[128,128]{1,0:T(8,128)S(1)} %get-tuple-element.53), channel_id=1, source_target_pairs={{0,8},{8,16},{16,24},{24,32},{32,40},{40,48},{48,56},{56,0},{1,9},... | collective-permute-start | bytes 196616 | tf_op jit(solution)/shard_map/ppermute | solution.py:22
  106.5 6.4 %collective-permute-start.23 = (f32[128,128]{1,0:T(8,128)S(1)}, f32[128,128]{1,0:T(8,128)S(1)}, u32[]{:S(2)}, u32[]{:S(2)}) collective-permute-start(f32[128,128]{1,0:T(8,128)S(1)} %get-tuple-element.54), channel_id=1, source_target_pairs={{0,16},{8,24},{16,32},{24,40},{32,48},{40,56},{48,0},{56,8},{1,17}... | collective-permute-start | bytes 196616 | tf_op jit(solution)/shard_map/ppermute | solution.py:22
  108.4 4.5 %collective-permute-start.24 = (f32[128,128]{1,0:T(8,128)S(1)}, f32[128,128]{1,0:T(8,128)S(1)}, u32[]{:S(2)}, u32[]{:S(2)}) collective-permute-start(f32[128,128]{1,0:T(8,128)S(1)} %get-tuple-element.55), channel_id=1, source_target_pairs={{0,48},{8,56},{16,0},{24,8},{32,16},{40,24},{48,32},{56,40},{1,49}... | collective-permute-start | bytes 196616 | tf_op jit(solution)/shard_map/ppermute | solution.py:22
  110.2 5.2 %collective-permute-start.25 = (f32[128,128]{1,0:T(8,128)S(1)}, f32[128,128]{1,0:T(8,128)S(1)}, u32[]{:S(2)}, u32[]{:S(2)}) collective-permute-start(f32[128,128]{1,0:T(8,128)S(1)} %get-tuple-element.56), channel_id=1, source_target_pairs={{0,56},{8,0},{16,8},{24,16},{32,24},{40,32},{48,40},{56,48},{1,57}... | collective-permute-start | bytes 196616 | tf_op jit(solution)/shard_map/ppermute | solution.py:22
  (12 other events, 195.6 us)

commit v2 on v1

v2 whole, which is shorter than its diff:
```python
import functools

import jax
import jax.numpy as jnp
from jax import lax
from jax.experimental import pallas as pl
from jax.experimental.pallas import tpu as pltpu
from jax.sharding import Mesh, PartitionSpec as P

learn_rate = 0.1
NX, NZ, NY, NC = 4, 8, 4, 2
RB, SB, E, BAG = 128, 128, 128, 8
SIZES = {"hst": NX, "z": NZ, "y": NY, "core": NC}
HALF_ROWS = NZ * RB
NEAR = 5 * RB
RADIX = 17
SAMPLES_Y = NX * SB
F32, BF16 = jnp.float32, jnp.bfloat16
VMEM = pltpu.CompilerParams(vmem_limit_bytes=40 << 20)


def move(array, axis, step):
    n = SIZES[axis]
    return lax.ppermute(array, axis, [(i, (i + step) % n) for i in range(n)])


def call(kernel, out_shapes, *operands, flops=0, moved=0):
    shapes = [jax.ShapeDtypeStruct(s, d) for s, d in out_shapes]
    return pl.pallas_call(
        kernel,
        out_shape=shapes,
        compiler_params=VMEM,
        cost_estimate=pl.CostEstimate(flops=flops, bytes_accessed=moved or 1 << 20, transcendentals=0),
    )(*operands)


def split_terms(value):
    high = value.astype(BF16)
    return jnp.concatenate([high, (value - high.astype(F32)).astype(BF16)], axis=1)


def entries_kernel(pos, ids_hbm, bits_hbm, spot_ref, value_ref, ids, bits, sems):
    z, y, c = pos[1], pos[2], pos[3]
    copies = [
        pltpu.make_async_copy(source.at[:, z, :, c], target, sems.at[i])
        for i, (source, target) in enumerate(((ids_hbm, ids), (bits_hbm, bits)))
    ]
    for copy in copies:
        copy.start()
    for copy in copies:
        copy.wait()
    for dy in range(NY):
        for dx in range(NX):
            at = (pos[0] + dx) & (NX - 1), (y + dy) & (NY - 1)
            row = ids[at]
            spot = (((row >> 10) - z + 2) & (NZ - 1)) * RB + (row & (RB - 1))
            spot_ref[dy, dx] = jnp.where(((row >> 8) & (NY - 1)) == y, spot, -1)
            other = (((row >> 7) & 1) ^ c).astype(F32)
            value_ref[dy, dx] = (2 * bits[at] - 1).astype(F32) * (1.0 + (RADIX - 1) * other)


def entries_of(pos, ids, bits):
    shape = (NX, NY, BAG, SB)
    return pl.pallas_call(
        entries_kernel,
        in_specs=[pl.BlockSpec(memory_space=pltpu.SMEM)] + [pl.BlockSpec(memory_space=pltpu.HBM)] * 2,
        out_specs=[pl.BlockSpec(memory_space=pltpu.VMEM)] * 2,
        out_shape=[jax.ShapeDtypeStruct(shape, jnp.int32), jax.ShapeDtypeStruct(shape, F32)],
        scratch_shapes=[pltpu.VMEM(shape, jnp.int32)] * 2 + [pltpu.SemaphoreType.DMA((2,))],
        compiler_params=VMEM,
        cost_estimate=pl.CostEstimate(flops=1 << 20, bytes_accessed=1 << 19, transcendentals=0),
    )(pos, ids, bits)


def counts_kernel(spot_ref, value_ref, out_ref):
    rows16 = lax.broadcasted_iota(jnp.int32, (16, SB), 0).astype(jnp.int16)
    for dx in range(NX):
        spots = [jnp.broadcast_to(spot_ref[dx, k : k + 1], (16, SB)).astype(jnp.int16) for k in range(BAG)]
        values = [jnp.broadcast_to(value_ref[dx, k : k + 1], (16, SB)).astype(BF16) for k in range(BAG)]
        columns = slice(dx * SB, (dx + 1) * SB)

        def step(r, carry):
            here = rows16 + (r * 16).astype(jnp.int16)
            terms = [jnp.where(s == here, v, BF16(0)) for s, v in zip(spots, values)]
            while len(terms) > 1:
                terms = [a + b for a, b in zip(terms[::2], terms[1::2])]
            high = (terms[0] * BF16(1.0 / RADIX) + BF16(192)) - BF16(192)
            at = pl.multiple_of(r * 16, 16)
            out_ref[pl.ds(at, 16), columns] = terms[0] - high * BF16(RADIX)
            out_ref[pl.ds(HALF_ROWS + at, 16), columns] = high
            return carry

        lax.fori_loop(0, HALF_ROWS // 16, step, 0, unroll=16)


def counts_of(entries, dy, *after):
    vm = pl.BlockSpec(memory_space=pltpu.VMEM)
    spec = pl.BlockSpec((None, NX, BAG, SB), lambda i: (dy, 0, 0, 0))
    return pl.pallas_call(
        lambda s, v, *rest: counts_kernel(s, v, rest[-1]),
        grid=(1,),
        in_specs=[spec, spec] + [pl.BlockSpec(memory_space=pl.ANY)] * len(after),
        out_specs=pl.BlockSpec(memory_space=pltpu.VMEM),
        out_shape=jax.ShapeDtypeStruct((NC * HALF_ROWS, SAMPLES_Y), BF16),
        compiler_params=VMEM,
        cost_estimate=pl.CostEstimate(flops=1 << 28, bytes_accessed=2 << 20, transcendentals=0),
    )(*entries, *after)


def forward_kernel(own, p1, m1, p2, m2, *refs):
    near, up, down = refs[-3:]
    for i, ref in enumerate((p2, p1, own, m1, m2)):
        near[i * RB : (i + 1) * RB] = ref[...]
    up[:RB] = p1[...]
    up[RB:] = p2[: RB // 2]
    down[:RB] = m1[...]
    down[RB:] = m2[RB // 2 :]


def far_rows_kernel(p3, m3, *refs):
    far = refs[-1]
    h = RB // 2
    far[:RB] = m3[:RB]
    far[RB : RB + h] = p3[RB:]
    far[RB + h : 2 * RB] = m3[RB:]
    far[2 * RB :] = p3[:RB]


def call_after(kernel, out_shapes, operands, after):
    vm, anywhere = pl.BlockSpec(memory_space=pltpu.VMEM), pl.BlockSpec(memory_space=pl.ANY)
    return pl.pallas_call(
        kernel,
        in_specs=[vm] * len(operands) + [anywhere] * len(after),
        out_specs=[vm] * len(out_shapes),
        out_shape=[jax.ShapeDtypeStruct(s, F32) for s in out_shapes],
        compiler_params=VMEM,
        cost_estimate=pl.CostEstimate(flops=0, bytes_accessed=1 << 18, transcendentals=0),
    )(*operands, *after)


def turned_terms(rows):
    turned = rows.T
    high = turned.astype(BF16)
    return jnp.concatenate([high, (turned - high.astype(F32)).astype(BF16)], axis=0)


def pool_part(terms, count_rows):
    part = jnp.dot(terms, count_rows, preferred_element_type=F32)
    return part[:E] + part[E:]


def pool_near_kernel(own, other, c0, c1, c2, c3, out):
    a, b = turned_terms(own[...]), turned_terms(other[...])
    for d, c in enumerate((c0, c1, c2, c3)):
        out[d] = pool_part(a, c[:NEAR]) + pool_part(b, c[HALF_ROWS : HALF_ROWS + NEAR])


def pool_far_kernel(own, base, c0, c1, c2, c3, out):
    a = turned_terms(own[...])
    for d, c in enumerate((c0, c1, c2, c3)):
        out[d] = base[d] + pool_part(a, c[NEAR:HALF_ROWS])


def pool_last_kernel(d, other, base, c, out):
    b = turned_terms(other[...])
    total = base[d] + pool_part(b, c[HALF_ROWS + NEAR :])
    for i in range(NX):
        s = slice(i * SB, (i + 1) * SB)
        out[s] = total[:, s].T


def owners_kernel(a, b, c, d, o0, o1, o2, o3):
    for i, out in enumerate((o0, o1, o2, o3)):
        s = slice(i * SB, (i + 1) * SB)
        out[...] = (a[s] + b[s]) + (c[s] + d[s])


def cross_kernel(pos, b0, b1, b2, b3, u, v, bias, cot, crossed, g0, g1, g2, g3, x_ref):
    def columns(d):
        return pl.ds(pl.multiple_of(((pos[0] - d) & (NX - 1)) * E, E), E)

    for d, b in enumerate((b0, b1, b2, b3)):
        x_ref[:, columns(d)] = b[...]
    base_x = x_ref[...]
    low = jnp.dot(base_x.astype(BF16), u[...], preferred_element_type=F32).astype(BF16)
    scale = jnp.dot(low, v[...], preferred_element_type=F32) + bias[...]
    crossed[...] = (base_x * scale + base_x).astype(BF16)
    upstream = cot[...].astype(F32)
    mixed = (upstream * base_x).astype(BF16)
    last = (((1,), (1,)), ((), ()))
    back_low = lax.dot_general(mixed, v[...], last, preferred_element_type=F32).astype(BF16)
    x_ref[...] = upstream * (scale + 1.0) + lax.dot_general(
        back_low, u[...], last, preferred_element_type=F32
    )
    for d, g in enumerate((g0, g1, g2, g3)):
        g[...] = x_ref[:, columns(d)]


def cross(pos, parts, u, v, bias, cot):
    vm = pl.BlockSpec(memory_space=pltpu.VMEM)
    return pl.pallas_call(
        cross_kernel,
        in_specs=[pl.BlockSpec(memory_space=pltpu.SMEM)] + [vm] * 8,
        out_specs=[vm] * 5,
        out_shape=[jax.ShapeDtypeStruct(cot.shape, BF16)] + [jax.ShapeDtypeStruct((SB, E), F32)] * NX,
        scratch_shapes=[pltpu.VMEM(cot.shape, F32)],
        compiler_params=VMEM,
        cost_estimate=pl.CostEstimate(flops=8 * SB * 512 * 512, bytes_accessed=2 << 20, transcendentals=0),
    )(pos, *parts, u, v, bias, cot)


def stack_kernel(a, b, c, d, out):
    for i, ref in enumerate((a, b, c, d)):
        out[i * SB : (i + 1) * SB] = ref[...]


def grad_terms_kernel(g0, g1, g2, g3, c0, c1, c2, c3, out, terms):
    for d, g in enumerate((g0, g1, g2, g3)):
        terms[d] = split_terms(g[...])
    grads_kernel(slice(HALF_ROWS + NEAR, NC * HALF_ROWS), terms, c0, c1, c2, c3, out)


def grads_kernel(rows, terms, c0, c1, c2, c3, *refs):
    out = refs[-1]
    total = None
    for d, c in enumerate((c0, c1, c2, c3)):
        part = jnp.dot(c[rows], terms[d], preferred_element_type=F32)
        total = part if total is None else total + part
    out[...] = total[:, :E] + total[:, E:]


def grads(counts, terms, rows, *after):
    vm = pl.BlockSpec(memory_space=pltpu.VMEM)
    amount = rows.stop - rows.start
    return pl.pallas_call(
        functools.partial(grads_kernel, rows),
        in_specs=[vm] * 5 + [pl.BlockSpec(memory_space=pl.ANY)] * len(after),
        out_specs=vm,
        out_shape=jax.ShapeDtypeStruct((amount, E), F32),
        compiler_params=VMEM,
        cost_estimate=pl.CostEstimate(
            flops=4 * amount * NY * SAMPLES_Y * E, bytes_accessed=1 << 20, transcendentals=0
        ),
    )(terms, *counts, *after)


def far_sums_kernel(a, b, up, down):
    h = RB // 2
    total = a[...] + b[...]
    up[...] = total[: RB + h]
    down[:RB] = total[2 * RB :]
    down[RB:] = total[RB + h : 2 * RB]


def near_sums_kernel(a, b, up, down, keep, p1, p2, m2, m1):
    h = RB // 2
    m2[...] = a[:RB] + b[:RB]
    m2[h:] += down[RB:]
    m1[...] = a[RB : 2 * RB] + b[RB : 2 * RB] + down[:RB]
    keep[...] = a[2 * RB : 3 * RB] + b[2 * RB : 3 * RB]
    p1[...] = a[3 * RB : 4 * RB] + b[3 * RB : 4 * RB] + up[:RB]
    p2[...] = a[4 * RB :] + b[4 * RB :]
    p2[:h] += up[RB:]


def update_kernel(keep, a, b, c, d, rows, accum, new_rows, new_accum):
    grad = keep[...] + ((a[...] + b[...]) + (c[...] + d[...]))
    mean = jnp.sum(grad * grad, axis=1, keepdims=True) * (1.0 / E)
    mean_row = jnp.broadcast_to(mean, (RB, E)).T[:1]
    total = accum[...] + mean_row
    new_accum[...] = total
    total_column = jnp.broadcast_to(total, (E, RB)).T
    new_rows[...] = rows[...] - learn_rate * grad / jnp.sqrt(total_column)


def per_device(
    table_rows, row_accum, row_ids, sketch_bits, cross_u, cross_v, cross_bias, cotangent
):
    pos = jnp.stack([lax.axis_index(a) for a in ("hst", "z", "y", "core")]).astype(jnp.int32)
    own = table_rows[0]

    def by_owner(entries):
        return entries[0].reshape(BAG, -1, SB).transpose(1, 0, 2).reshape(NX, NZ, NY, NC, BAG, SB)

    ids, bits = by_owner(row_ids), by_owner(sketch_bits)
    third = (RB + RB // 2, E)
    p1, m1 = move(own, "z", 1), move(own, "z", -1)
    p2, m2 = move(own, "z", 2), move(own, "z", -2)
    entries = entries_of(pos, ids, bits)
    first = [counts_of(entries, d) for d in (2, 1)]
    near, up, down = call_after(forward_kernel, [(NEAR, E), third, third], (own, p1, m1, p2, m2), first)
    p3, m3 = move(up, "z", 2), move(down, "z", -2)
    other_near = move(near, "core", 1)
    last = [counts_of(entries, d, near) for d in (3, 0)]
    counts = [last[1], first[1], first[0], last[0]]
    turned = (NY, E, SAMPLES_Y)
    bags = call(pool_near_kernel, [(turned, F32)], near, other_near, *counts, flops=1 << 30)[0]
    far = call_after(far_rows_kernel, [(HALF_ROWS - NEAR, E)], (p3, m3), [bags])[0]
    other_far = move(far, "core", 1)
    bags = call(pool_far_kernel, [(turned, F32)], far, bags, *counts, flops=1 << 28)[0]
    pooled = [None] * NY
    for d in (2, 1, 3, 0):
        (pooled[d],) = call(
            functools.partial(pool_last_kernel, d),
            [((SAMPLES_Y, E), F32)],
            other_far,
            bags,
            counts[d],
            flops=1 << 27,
        )
    block = ((SB, E), F32)
    mine = call(
        owners_kernel,
        [block] * NX,
        pooled[0],
        move(pooled[1], "y", 1),
        move(pooled[2], "y", 2),
        move(pooled[3], "y", -1),
    )
    parts = [mine[0]] + [move(mine[d], "hst", d) for d in range(1, NX)]
    crossed, *grad_parts = cross(
        pos, parts, cross_u, cross_v, cross_bias.reshape(1, -1), cotangent
    )
    back = [grad_parts[0]] + [move(grad_parts[d], "hst", -d) for d in range(1, NX)]
    (bag_grads,) = call(stack_kernel, [((SAMPLES_Y, E), F32)], *back)
    all_grads = [bag_grads] + [move(bag_grads, "y", -d) for d in range(1, NY)]
    far_shape = (HALF_ROWS - NEAR, E)
    other_far, terms = call(
        grad_terms_kernel,
        [(far_shape, F32), ((NY, SAMPLES_Y, 2 * E), BF16)],
        *all_grads,
        *counts,
        flops=1 << 29,
    )
    from_far = move(other_far, "core", 1)
    own_far = grads(counts, terms, slice(NEAR, HALF_ROWS))
    up, down = call(far_sums_kernel, [(third, F32)] * 2, own_far, from_far)
    up_in, down_in = move(up, "z", 2), move(down, "z", -2)
    other_near = grads(counts, terms, slice(HALF_ROWS, HALF_ROWS + NEAR), up)
    from_near = move(other_near, "core", 1)
    own_near = grads(counts, terms, slice(0, NEAR), up)
    keep, *near = call(near_sums_kernel, [block] * 5, own_near, from_near, up_in, down_in)
    sums = [move(a, "z", s) for a, s in zip(near, (1, 2, -2, -1))]
    new_rows, new_accum = call(
        update_kernel, [block, ((1, RB), F32)], keep, *sums, own, row_accum
    )
    return (crossed, new_rows[None], new_accum)


def solution(mesh):
    grid = Mesh(mesh.devices.reshape(NX, NZ, NY, NC), ("hst", "z", "y", "core"))
    local = ("z", "y", "core")
    in_specs = (
        P("hst", local, None),
        P("hst", local),
        P("hst", None, None),
        P("hst", None, None),
        P(),
        P(),
        P(),
        P(("hst",) + local, None),
    )
    out_specs = (P(("hst",) + local, None), P("hst", local, None), P("hst", local))
    return jax.shard_map(
        per_device, mesh=grid, in_specs=in_specs, out_specs=out_specs, check_vma=False
    )
```

time: 117 us -> 102 us (0.87)
  waiting for transfers between devices: 41.3 us -> 33.5 us
  Pallas kernels: 23.5 us -> 16 us
    pallas_call x8 -> x10, Pallas kernels: 20.5 us -> 8.17 us  [the longest x4 5.24 us: counts_of(): pl.pallas_call(lambda s, v, *rest: counts_kernel(s, v, rest[-1]), grid=(1...]
    ppermute x26 -> x28, waiting for transfers between devices: 41.3 us -> 33.5 us  [move(): return lax.ppermute(array, axis, [(i, (i + step) % n) for i in range(n)])]
    pallas_call x7 -> x12, Pallas kernels: 1.1 us -> 5.96 us  [call(): pl.pallas_call(kernel, out_shape=shapes, compiler_params=VMEM, cost_estim...]
    unnamed x20 -> x16, local copies, waits for them, and re-layouts: 2.11 us -> 2.49 us
    ppermute x26 -> x28, starting transfers between devices: 48.5 us -> 48.4 us  [move(): return lax.ppermute(array, axis, [(i, (i + step) % n) for i in range(n)])]
  transfers between devices with their start and end apart: 26 -> 28, of which waited for: 16 -> 16; matrix products, arithmetic and copies ran while one was open for 0% -> 0% of each run, Pallas kernels for 13% -> 11%
where the time goes in v2:
time: 102 us; the launch traced here: 101 us
  starting transfers between devices  48.4 us (47%)
  waiting for transfers between devices  33.5 us (33%)
  Pallas kernels  16 us (16%)
  local copies, waits for them, and re-layouts  2.49 us (2%)
    ppermute x28, starting transfers between devices, move(): return lax.ppermute(array, axis, [(i, (i + step) % n) for i in range(n)])  48.4 us
    ppermute x28, waiting for transfers between devices, move(): return lax.ppermute(array, axis, [(i, (i + step) % n) for i in range(n)])  33.5 us
    pallas_call x12, Pallas kernels, call(): pl.pallas_call(kernel, out_shape=shapes, compiler_params=VMEM, cost_estim...  5.96 us
    pallas_call x4, Pallas kernels, counts_of(): pl.pallas_call(lambda s, v, *rest: counts_kernel(s, v, rest[-1]), grid=(1...  5.24 us
    unnamed x16, local copies, waits for them, and re-layouts  2.49 us
    pallas_call x3, Pallas kernels, grads(): pl.pallas_call(functools.partial(grads_kernel, rows), in_specs=[vm] * 5 +...  2.25 us
  transfers between devices with their start and end apart: 28, of which 16 were waited for; matrix products, arithmetic and copies ran while one was open for 0% of the time, Pallas kernels for 11%

profile of v2, /device:TPU:1, one launch (start us, length us, event | category | flops | bytes accessed | tf_op | source)
XLA Modules:
  0.0 101.4 jit_solution(15668262939192482323)
XLA Ops:
  0.6 6.9 %collective-permute-start.3 = (f32[128,128]{1,0:T(8,128)}, f32[128,128]{1,0:T(8,128)S(1)}, u32[]{:S(2)}, u32[]{:S(2)}) collective-permute-start(f32[128,128]{1,0:T(8,128)} %bitcast.19), channel_id=1, source_target_pairs={{0,48},{8,56},{16,0},{24,8},{32,16},{40,24},{48,32},{56,40},{1,49}... | collective-permute-start | bytes 196616 | tf_op jit(solution)/shard_map/ppermute | solution.py:24
  7.6 3.1 %collective-permute-start.1 = (f32[128,128]{1,0:T(8,128)}, f32[128,128]{1,0:T(8,128)S(1)}, u32[]{:S(2)}, u32[]{:S(2)}) collective-permute-start(f32[128,128]{1,0:T(8,128)} %bitcast.21), channel_id=1, source_target_pairs={{0,56},{8,0},{16,8},{24,16},{32,24},{40,32},{48,40},{56,48},{1,57}... | collective-permute-start | bytes 196616 | tf_op jit(solution)/shard_map/ppermute | solution.py:24
  16.6 1.6 %collective-permute-start.6 = (f32[640,128]{1,0:T(8,128)S(1)}, f32[640,128]{1,0:T(8,128)S(1)}, u32[]{:S(2)}, u32[]{:S(2)}) collective-permute-start(f32[640,128]{1,0:T(8,128)S(1)} %get-tuple-element.32.rest_0_.own), channel_id=1, source_target_pairs={{0,1},{1,0},{2,3},{3,2},{4,5},{5,4},{6,7},{7,6},{8,9},{9,8},{10,11... | collective-permute-start | bytes 983048 | tf_op jit(solution)/shard_map/ppermute | solution.py:24
  18.2 3.6 %collective-permute-start.5 = (f32[192,128]{1,0:T(8,128)S(1)}, f32[192,128]{1,0:T(8,128)S(1)}, u32[]{:S(2)}, u32[]{:S(2)}) collective-permute-start(f32[192,128]{1,0:T(8,128)S(1)} %get-tuple-element.31), channel_id=1, source_target_pairs={{0,48},{8,56},{16,0},{24,8},{32,16},{40,24},{48,32},{56,40},{1,49}... | collective-permute-start | bytes 294920 | tf_op jit(solution)/shard_map/ppermute | solution.py:24
  24.4 1.8 %shard_map.109.refs_0_.base = f32[4,128,512]{2,1,0:T(8,128)S(1)} custom-call(f32[640,128]{1,0:T(8,128)S(1)} %get-tuple-element.32.rest_0_.own, f32[640,128]{1,0:T(8,128)S(1)} %collective-permute-done.6.other, bf16[2048,512]{1,0:T(8,128)(2,1)S(1)} %shard_map.107.c0.c, bf16[2048,512]{1,0:T(8,128)(2,1)S(1)} %shard_map.105.refs_1_.c1.c, ...), custom_call_target="tpu_custom_call" | custom-call | flops 1073741824 | bytes 1048576 | tf_op jit(solution)/shard_map/pallas_call | solution.py:29
  30.4 2.7 %collective-permute-start.9 = (f32[512,128]{1,0:T(8,128)S(1)}, f32[512,128]{1,0:T(8,128)S(1)}, u32[]{:S(2)}, u32[]{:S(2)}) collective-permute-start(f32[512,128]{1,0:T(8,128)S(1)} %shard_map.114), channel_id=1, source_target_pairs={{0,4},{2,6},{4,0},{6,2},{1,5},{3,7},{5,1},{7,3},{8,12},{10,14},{12... | collective-permute-start | bytes 786440 | tf_op jit(solution)/shard_map/ppermute | solution.py:24
  35.2 2.3 %collective-permute-done.8.b = f32[512,128]{1,0:T(8,128)S(1)} collective-permute-done((f32[512,128]{1,0:T(8,128)S(1)}, f32[512,128]{1,0:T(8,128)S(1)}, u32[]{:S(2)}, u32[]{:S(2)}) %collective-permute-start.8) | collective-permute-done | bytes 262176 | tf_op jit(solution)/shard_map/ppermute | solution.py:24
  37.5 6.7 %collective-permute-done.9.c = f32[512,128]{1,0:T(8,128)S(1)} collective-permute-done((f32[512,128]{1,0:T(8,128)S(1)}, f32[512,128]{1,0:T(8,128)S(1)}, u32[]{:S(2)}, u32[]{:S(2)}) %collective-permute-start.9) | collective-permute-done | bytes 262176 | tf_op jit(solution)/shard_map/ppermute | solution.py:24
  44.3 1.5 %collective-permute-start.11 = (f32[128,128]{1,0:T(8,128)S(1)}, f32[128,128]{1,0:T(8,128)S(1)}, u32[]{:S(2)}, u32[]{:S(2)}) collective-permute-start(f32[128,128]{1,0:T(8,128)S(1)} %get-tuple-element.34), channel_id=1, source_target_pairs={{0,64},{64,128},{128,192},{192,0},{1,65},{65,129},{129,193},{193,1... | collective-permute-start | bytes 196616 | tf_op jit(solution)/shard_map/ppermute | solution.py:24
  45.8 2.5 %collective-permute-start.12 = (f32[128,128]{1,0:T(8,128)S(1)}, f32[128,128]{1,0:T(8,128)S(1)}, u32[]{:S(2)}, u32[]{:S(2)}) collective-permute-start(f32[128,128]{1,0:T(8,128)S(1)} %get-tuple-element.35), channel_id=1, source_target_pairs={{0,128},{64,192},{128,0},{192,64},{1,129},{65,193},{129,1},{193,65... | collective-permute-start | bytes 196616 | tf_op jit(solution)/shard_map/ppermute | solution.py:24
  50.7 1.6 %collective-permute-done.13.b3 = f32[128,128]{1,0:T(8,128)S(1)} collective-permute-done((f32[128,128]{1,0:T(8,128)S(1)}, f32[128,128]{1,0:T(8,128)S(1)}, u32[]{:S(2)}, u32[]{:S(2)}) %collective-permute-start.13) | collective-permute-done | bytes 65568 | tf_op jit(solution)/shard_map/ppermute | solution.py:24
  52.3 1.8 %shard_map.117 = (bf16[128,512]{1,0:T(8,128)(2,1)}, f32[128,128]{1,0:T(8,128)S(1)}, f32[128,128]{1,0:T(8,128)S(1)}, f32[128,128]{1,0:T(8,128)S(1)}, f32[128,128]{1,0:T(8,128)S(1)}) custom-call(s32[4]{0:T(128)S(1)} %pad_add_fusion.pos, f32[128,128]{1,0:T(8,128)S(1)} %get-tuple-element.33.b0, f32[128,128]{1,0:T(8,128)S(1)} %collective-permute-done.11.b1, ...), custom_call_target="tpu_custom_call" | custom-call | flops 268435456 | bytes 2097152 | tf_op jit(solution)/shard_map/pallas_call | solution.py:201
  54.1 2.3 %collective-permute-start.14 = (f32[128,128]{1,0:T(8,128)S(1)}, f32[128,128]{1,0:T(8,128)S(1)}, u32[]{:S(2)}, u32[]{:S(2)}) collective-permute-start(f32[128,128]{1,0:T(8,128)S(1)} %get-tuple-element.39), channel_id=1, source_target_pairs={{0,192},{64,0},{128,64},{192,128},{1,193},{65,1},{129,65},{193,129... | collective-permute-start | bytes 196616 | tf_op jit(solution)/shard_map/ppermute | solution.py:24
  58.4 2.8 %collective-permute-done.15.c = f32[128,128]{1,0:T(8,128)S(1)} collective-permute-done((f32[128,128]{1,0:T(8,128)S(1)}, f32[128,128]{1,0:T(8,128)S(1)}, u32[]{:S(2)}, u32[]{:S(2)}) %collective-permute-start.15) | collective-permute-done | bytes 65568 | tf_op jit(solution)/shard_map/ppermute | solution.py:24
  61.5 2.0 %collective-permute-start.19 = (f32[512,128]{1,0:T(8,128)S(1)}, f32[512,128]{1,0:T(8,128)S(1)}, u32[]{:S(2)}, u32[]{:S(2)}) collective-permute-start(f32[512,128]{1,0:T(8,128)S(1)} %shard_map.118.g0), channel_id=1, source_target_pairs={{0,2},{2,4},{4,6},{6,0},{1,3},{3,5},{5,7},{7,1},{8,10},{10,12},{12... | collective-permute-start | bytes 786440 | tf_op jit(solution)/shard_map/ppermute | solution.py:24
  63.5 1.5 %collective-permute-start.18 = (f32[512,128]{1,0:T(8,128)S(1)}, f32[512,128]{1,0:T(8,128)S(1)}, u32[]{:S(2)}, u32[]{:S(2)}) collective-permute-start(f32[512,128]{1,0:T(8,128)S(1)} %shard_map.118.g0), channel_id=1, source_target_pairs={{0,4},{2,6},{4,0},{6,2},{1,5},{3,7},{5,1},{7,3},{8,12},{10,14},{12... | collective-permute-start | bytes 786440 | tf_op jit(solution)/shard_map/ppermute | solution.py:24
  66.0 2.0 %collective-permute-done.19.g3 = f32[512,128]{1,0:T(8,128)S(1)} collective-permute-done((f32[512,128]{1,0:T(8,128)S(1)}, f32[512,128]{1,0:T(8,128)S(1)}, u32[]{:S(2)}, u32[]{:S(2)}) %collective-permute-start.19) | collective-permute-done | bytes 262176 | tf_op jit(solution)/shard_map/ppermute | solution.py:24
  68.0 5.1 %collective-permute-done.18.g2 = f32[512,128]{1,0:T(8,128)S(1)} collective-permute-done((f32[512,128]{1,0:T(8,128)S(1)}, f32[512,128]{1,0:T(8,128)S(1)}, u32[]{:S(2)}, u32[]{:S(2)}) %collective-permute-start.18) | collective-permute-done | bytes 262176 | tf_op jit(solution)/shard_map/ppermute | solution.py:24
  73.7 4.8 %collective-permute-start.20 = (f32[384,128]{1,0:T(8,128)S(1)}, f32[384,128]{1,0:T(8,128)S(1)}, u32[]{:S(2)}, u32[]{:S(2)}) collective-permute-start(f32[384,128]{1,0:T(8,128)S(1)} %get-tuple-element.43), channel_id=1, source_target_pairs={{0,1},{1,0},{2,3},{3,2},{4,5},{5,4},{6,7},{7,6},{8,9},{9,8},{10,11... | collective-permute-start | bytes 589832 | tf_op jit(solution)/shard_map/ppermute | solution.py:24
  81.0 4.3 %collective-permute-start.23 = (f32[192,128]{1,0:T(8,128)S(1)}, f32[192,128]{1,0:T(8,128)S(1)}, u32[]{:S(2)}, u32[]{:S(2)}) collective-permute-start(f32[192,128]{1,0:T(8,128)S(1)} %get-tuple-element.45), channel_id=1, source_target_pairs={{0,48},{8,56},{16,0},{24,8},{32,16},{40,24},{48,32},{56,40},{1,49}... | collective-permute-start | bytes 294920 | tf_op jit(solution)/shard_map/ppermute | solution.py:24
  86.1 2.5 %collective-permute-done.23.down = f32[192,128]{1,0:T(8,128)S(1)} collective-permute-done((f32[192,128]{1,0:T(8,128)S(1)}, f32[192,128]{1,0:T(8,128)S(1)}, u32[]{:S(2)}, u32[]{:S(2)}) %collective-permute-start.23) | collective-permute-done | bytes 98336 | tf_op jit(solution)/shard_map/ppermute | solution.py:24
  88.5 4.3 %collective-permute-done.22.up = f32[192,128]{1,0:T(8,128)S(1)} collective-permute-done((f32[192,128]{1,0:T(8,128)S(1)}, f32[192,128]{1,0:T(8,128)S(1)}, u32[]{:S(2)}, u32[]{:S(2)}) %collective-permute-start.22) | collective-permute-done | bytes 98336 | tf_op jit(solution)/shard_map/ppermute | solution.py:24
  93.3 3.4 %collective-permute-start.26 = (f32[128,128]{1,0:T(8,128)S(1)}, f32[128,128]{1,0:T(8,128)S(1)}, u32[]{:S(2)}, u32[]{:S(2)}) collective-permute-start(f32[128,128]{1,0:T(8,128)S(1)} %get-tuple-element.49), channel_id=1, source_target_pairs={{0,48},{8,56},{16,0},{24,8},{32,16},{40,24},{48,32},{56,40},{1,49}... | collective-permute-start | bytes 196616 | tf_op jit(solution)/shard_map/ppermute | solution.py:24
  96.7 1.4 %collective-permute-start.27 = (f32[128,128]{1,0:T(8,128)S(1)}, f32[128,128]{1,0:T(8,128)S(1)}, u32[]{:S(2)}, u32[]{:S(2)}) collective-permute-start(f32[128,128]{1,0:T(8,128)S(1)} %get-tuple-element.50), channel_id=1, source_target_pairs={{0,56},{8,0},{16,8},{24,16},{32,24},{40,32},{48,40},{56,48},{1,57}... | collective-permute-start | bytes 196616 | tf_op jit(solution)/shard_map/ppermute | solution.py:24
  (72 shorter events, 28.0 us)
Async XLA Ops:
  0.6 15.9 %collective-permute-start.3 = (f32[128,128]{1,0:T(8,128)}, f32[128,128]{1,0:T(8,128)S(1)}, u32[]{:S(2)}, u32[]{:S(2)}) collective-permute-start(f32[128,128]{1,0:T(8,128)} %bitcast.19), channel_id=1, source_target_pairs={{0,48},{8,56},{16,0},{24,8},{32,16},{40,24},{48,32},{56,40},{1,49}... | collective-permute-start | bytes 196616 | tf_op jit(solution)/shard_map/ppermute | solution.py:24
  7.6 9.0 %collective-permute-start.2 = (f32[128,128]{1,0:T(8,128)}, f32[128,128]{1,0:T(8,128)S(1)}, u32[]{:S(2)}, u32[]{:S(2)}) collective-permute-start(f32[128,128]{1,0:T(8,128)} %bitcast.20), channel_id=1, source_target_pairs={{0,16},{8,24},{16,32},{24,40},{32,48},{40,56},{48,0},{56,8},{1,17}... | collective-permute-start | bytes 196616 | tf_op jit(solution)/shard_map/ppermute | solution.py:24
  7.6 9.0 %collective-permute-start.1 = (f32[128,128]{1,0:T(8,128)}, f32[128,128]{1,0:T(8,128)S(1)}, u32[]{:S(2)}, u32[]{:S(2)}) collective-permute-start(f32[128,128]{1,0:T(8,128)} %bitcast.21), channel_id=1, source_target_pairs={{0,56},{8,0},{16,8},{24,16},{32,24},{40,32},{48,40},{56,48},{1,57}... | collective-permute-start | bytes 196616 | tf_op jit(solution)/shard_map/ppermute | solution.py:24
  10.7 5.9 %collective-permute-start = (f32[128,128]{1,0:T(8,128)}, f32[128,128]{1,0:T(8,128)S(1)}, u32[]{:S(2)}, u32[]{:S(2)}) collective-permute-start(f32[128,128]{1,0:T(8,128)} %bitcast.22), channel_id=1, source_target_pairs={{0,8},{8,16},{16,24},{24,32},{32,40},{40,48},{48,56},{56,0},{1,9},... | collective-permute-start | bytes 196616 | tf_op jit(solution)/shard_map/ppermute | solution.py:24
  16.6 7.8 %collective-permute-start.6 = (f32[640,128]{1,0:T(8,128)S(1)}, f32[640,128]{1,0:T(8,128)S(1)}, u32[]{:S(2)}, u32[]{:S(2)}) collective-permute-start(f32[640,128]{1,0:T(8,128)S(1)} %get-tuple-element.32.rest_0_.own), channel_id=1, source_target_pairs={{0,1},{1,0},{2,3},{3,2},{4,5},{5,4},{6,7},{7,6},{8,9},{9,8},{10,11... | collective-permute-start | bytes 983048 | tf_op jit(solution)/shard_map/ppermute | solution.py:24
  18.2 8.1 %collective-permute-start.4 = (f32[192,128]{1,0:T(8,128)S(1)}, f32[192,128]{1,0:T(8,128)S(1)}, u32[]{:S(2)}, u32[]{:S(2)}) collective-permute-start(f32[192,128]{1,0:T(8,128)S(1)} %get-tuple-element.30), channel_id=1, source_target_pairs={{0,16},{8,24},{16,32},{24,40},{32,48},{40,56},{48,0},{56,8},{1,17}... | collective-permute-start | bytes 294920 | tf_op jit(solution)/shard_map/ppermute | solution.py:24
  18.2 8.1 %collective-permute-start.5 = (f32[192,128]{1,0:T(8,128)S(1)}, f32[192,128]{1,0:T(8,128)S(1)}, u32[]{:S(2)}, u32[]{:S(2)}) collective-permute-start(f32[192,128]{1,0:T(8,128)S(1)} %get-tuple-element.31), channel_id=1, source_target_pairs={{0,48},{8,56},{16,0},{24,8},{32,16},{40,24},{48,32},{56,40},{1,49}... | collective-permute-start | bytes 294920 | tf_op jit(solution)/shard_map/ppermute | solution.py:24
  28.6 8.9 %collective-permute-start.8 = (f32[512,128]{1,0:T(8,128)S(1)}, f32[512,128]{1,0:T(8,128)S(1)}, u32[]{:S(2)}, u32[]{:S(2)}) collective-permute-start(f32[512,128]{1,0:T(8,128)S(1)} %shard_map.113), channel_id=1, source_target_pairs={{0,2},{2,4},{4,6},{6,0},{1,3},{3,5},{5,7},{7,1},{8,10},{10,12},{12... | collective-permute-start | bytes 786440 | tf_op jit(solution)/shard_map/ppermute | solution.py:24
  30.4 13.9 %collective-permute-start.9 = (f32[512,128]{1,0:T(8,128)S(1)}, f32[512,128]{1,0:T(8,128)S(1)}, u32[]{:S(2)}, u32[]{:S(2)}) collective-permute-start(f32[512,128]{1,0:T(8,128)S(1)} %shard_map.114), channel_id=1, source_target_pairs={{0,4},{2,6},{4,0},{6,2},{1,5},{3,7},{5,1},{7,3},{8,12},{10,14},{12... | collective-permute-start | bytes 786440 | tf_op jit(solution)/shard_map/ppermute | solution.py:24
  33.6 10.6 %collective-permute-start.10 = (f32[512,128]{1,0:T(8,128)S(1)}, f32[512,128]{1,0:T(8,128)S(1)}, u32[]{:S(2)}, u32[]{:S(2)}) collective-permute-start(f32[512,128]{1,0:T(8,128)S(1)} %shard_map.115), channel_id=1, source_target_pairs={{0,6},{2,0},{4,2},{6,4},{1,7},{3,1},{5,3},{7,5},{8,14},{10,8},{12,... | collective-permute-start | bytes 786440 | tf_op jit(solution)/shard_map/ppermute | solution.py:24
  44.3 5.1 %collective-permute-start.11 = (f32[128,128]{1,0:T(8,128)S(1)}, f32[128,128]{1,0:T(8,128)S(1)}, u32[]{:S(2)}, u32[]{:S(2)}) collective-permute-start(f32[128,128]{1,0:T(8,128)S(1)} %get-tuple-element.34), channel_id=1, source_target_pairs={{0,64},{64,128},{128,192},{192,0},{1,65},{65,129},{129,193},{193,1... | collective-permute-start | bytes 196616 | tf_op jit(solution)/shard_map/ppermute | solution.py:24
  45.8 4.9 %collective-permute-start.12 = (f32[128,128]{1,0:T(8,128)S(1)}, f32[128,128]{1,0:T(8,128)S(1)}, u32[]{:S(2)}, u32[]{:S(2)}) collective-permute-start(f32[128,128]{1,0:T(8,128)S(1)} %get-tuple-element.35), channel_id=1, source_target_pairs={{0,128},{64,192},{128,0},{192,64},{1,129},{65,193},{129,1},{193,65... | collective-permute-start | bytes 196616 | tf_op jit(solution)/shard_map/ppermute | solution.py:24
  56.5 4.7 %collective-permute-start.15 = (f32[128,128]{1,0:T(8,128)S(1)}, f32[128,128]{1,0:T(8,128)S(1)}, u32[]{:S(2)}, u32[]{:S(2)}) collective-permute-start(f32[128,128]{1,0:T(8,128)S(1)} %get-tuple-element.40), channel_id=1, source_target_pairs={{0,128},{64,192},{128,0},{192,64},{1,129},{65,193},{129,1},{193,65... | collective-permute-start | bytes 196616 | tf_op jit(solution)/shard_map/ppermute | solution.py:24
  56.5 5.0 %collective-permute-start.16 = (f32[128,128]{1,0:T(8,128)S(1)}, f32[128,128]{1,0:T(8,128)S(1)}, u32[]{:S(2)}, u32[]{:S(2)}) collective-permute-start(f32[128,128]{1,0:T(8,128)S(1)} %get-tuple-element.41), channel_id=1, source_target_pairs={{0,64},{64,128},{128,192},{192,0},{1,65},{65,129},{129,193},{193,1... | collective-permute-start | bytes 196616 | tf_op jit(solution)/shard_map/ppermute | solution.py:24
  61.5 6.5 %collective-permute-start.19 = (f32[512,128]{1,0:T(8,128)S(1)}, f32[512,128]{1,0:T(8,128)S(1)}, u32[]{:S(2)}, u32[]{:S(2)}) collective-permute-start(f32[512,128]{1,0:T(8,128)S(1)} %shard_map.118.g0), channel_id=1, source_target_pairs={{0,2},{2,4},{4,6},{6,0},{1,3},{3,5},{5,7},{7,1},{8,10},{10,12},{12... | collective-permute-start | bytes 786440 | tf_op jit(solution)/shard_map/ppermute | solution.py:24
  63.5 9.6 %collective-permute-start.18 = (f32[512,128]{1,0:T(8,128)S(1)}, f32[512,128]{1,0:T(8,128)S(1)}, u32[]{:S(2)}, u32[]{:S(2)}) collective-permute-start(f32[512,128]{1,0:T(8,128)S(1)} %shard_map.118.g0), channel_id=1, source_target_pairs={{0,4},{2,6},{4,0},{6,2},{1,5},{3,7},{5,1},{7,3},{8,12},{10,14},{12... | collective-permute-start | bytes 786440 | tf_op jit(solution)/shard_map/ppermute | solution.py:24
  65.0 8.1 %collective-permute-start.17 = (f32[512,128]{1,0:T(8,128)S(1)}, f32[512,128]{1,0:T(8,128)S(1)}, u32[]{:S(2)}, u32[]{:S(2)}) collective-permute-start(f32[512,128]{1,0:T(8,128)S(1)} %shard_map.118.g0), channel_id=1, source_target_pairs={{0,6},{2,0},{4,2},{6,4},{1,7},{3,1},{5,3},{7,5},{8,14},{10,8},{12,... | collective-permute-start | bytes 786440 | tf_op jit(solution)/shard_map/ppermute | solution.py:24
  73.7 5.9 %collective-permute-start.20 = (f32[384,128]{1,0:T(8,128)S(1)}, f32[384,128]{1,0:T(8,128)S(1)}, u32[]{:S(2)}, u32[]{:S(2)}) collective-permute-start(f32[384,128]{1,0:T(8,128)S(1)} %get-tuple-element.43), channel_id=1, source_target_pairs={{0,1},{1,0},{2,3},{3,2},{4,5},{5,4},{6,7},{7,6},{8,9},{9,8},{10,11... | collective-permute-start | bytes 589832 | tf_op jit(solution)/shard_map/ppermute | solution.py:24
  80.5 12.4 %collective-permute-start.21 = (f32[640,128]{1,0:T(8,128)S(1)}, f32[640,128]{1,0:T(8,128)S(1)}, u32[]{:S(2)}, u32[]{:S(2)}) collective-permute-start(f32[640,128]{1,0:T(8,128)S(1)} %shard_map.123), channel_id=1, source_target_pairs={{0,1},{1,0},{2,3},{3,2},{4,5},{5,4},{6,7},{7,6},{8,9},{9,8},{10,11... | collective-permute-start | bytes 983048 | tf_op jit(solution)/shard_map/ppermute | solution.py:24
  81.0 7.6 %collective-permute-start.23 = (f32[192,128]{1,0:T(8,128)S(1)}, f32[192,128]{1,0:T(8,128)S(1)}, u32[]{:S(2)}, u32[]{:S(2)}) collective-permute-start(f32[192,128]{1,0:T(8,128)S(1)} %get-tuple-element.45), channel_id=1, source_target_pairs={{0,48},{8,56},{16,0},{24,8},{32,16},{40,24},{48,32},{56,40},{1,49}... | collective-permute-start | bytes 294920 | tf_op jit(solution)/shard_map/ppermute | solution.py:24
  85.2 7.6 %collective-permute-start.22 = (f32[192,128]{1,0:T(8,128)S(1)}, f32[192,128]{1,0:T(8,128)S(1)}, u32[]{:S(2)}, u32[]{:S(2)}) collective-permute-start(f32[192,128]{1,0:T(8,128)S(1)} %get-tuple-element.44.refs_0_), channel_id=1, source_target_pairs={{0,16},{8,24},{16,32},{24,40},{32,48},{40,56},{48,0},{56,8},{1,17}... | collective-permute-start | bytes 294920 | tf_op jit(solution)/shard_map/ppermute | solution.py:24
  92.9 5.1 %collective-permute-start.24 = (f32[128,128]{1,0:T(8,128)S(1)}, f32[128,128]{1,0:T(8,128)S(1)}, u32[]{:S(2)}, u32[]{:S(2)}) collective-permute-start(f32[128,128]{1,0:T(8,128)S(1)} %get-tuple-element.47), channel_id=1, source_target_pairs={{0,8},{8,16},{16,24},{24,32},{32,40},{40,48},{48,56},{56,0},{1,9},... | collective-permute-start | bytes 196616 | tf_op jit(solution)/shard_map/ppermute | solution.py:24
  93.0 5.4 %collective-permute-start.25 = (f32[128,128]{1,0:T(8,128)S(1)}, f32[128,128]{1,0:T(8,128)S(1)}, u32[]{:S(2)}, u32[]{:S(2)}) collective-permute-start(f32[128,128]{1,0:T(8,128)S(1)} %get-tuple-element.48), channel_id=1, source_target_pairs={{0,16},{8,24},{16,32},{24,40},{32,48},{40,56},{48,0},{56,8},{1,17}... | collective-permute-start | bytes 196616 | tf_op jit(solution)/shard_map/ppermute | solution.py:24
  93.3 6.1 %collective-permute-start.26 = (f32[128,128]{1,0:T(8,128)S(1)}, f32[128,128]{1,0:T(8,128)S(1)}, u32[]{:S(2)}, u32[]{:S(2)}) collective-permute-start(f32[128,128]{1,0:T(8,128)S(1)} %get-tuple-element.49), channel_id=1, source_target_pairs={{0,48},{8,56},{16,0},{24,8},{32,16},{40,24},{48,32},{56,40},{1,49}... | collective-permute-start | bytes 196616 | tf_op jit(solution)/shard_map/ppermute | solution.py:24
  (12 other events, 113.5 us)

commit v3 on v0

v3 whole, which is shorter than its diff:
```python
import functools

import jax
import jax.numpy as jnp
from jax import lax
from jax.experimental import pallas as pl
from jax.experimental.pallas import tpu as pltpu
from jax.sharding import Mesh, PartitionSpec as P

learn_rate = 0.1
NX, NZ, NY, NC = 4, 8, 4, 2
RB, SB, E, BAG = 128, 128, 128, 8
SIZES = {"hst": NX, "z": NZ, "y": NY, "core": NC}
HALF_ROWS = NZ * RB
RADIX = 17
SAMPLES_Y = NX * SB
F32, BF16 = jnp.float32, jnp.bfloat16
VMEM = pltpu.CompilerParams(vmem_limit_bytes=40 << 20)
SMALL = pl.CostEstimate(flops=0, bytes_accessed=1024, transcendentals=0)


def move(array, axis, step):
    n = SIZES[axis]
    return lax.ppermute(array, axis, [(i, (i + step) % n) for i in range(n)])


def move_ways(array, axis, step):
    n = SIZES[axis]
    pairs = [
        (i * NC + c, (i + (step if c == 0 else -step)) % n * NC + c) for i in range(n) for c in range(NC)
    ]
    return lax.ppermute(array, (axis, "core"), pairs)


def call(kernel, out_shapes, *operands):
    vm = pl.BlockSpec(memory_space=pltpu.VMEM)
    return pl.pallas_call(
        kernel,
        in_specs=[vm] * len(operands),
        out_specs=[vm] * len(out_shapes),
        out_shape=[jax.ShapeDtypeStruct(s, d) for s, d in out_shapes],
        compiler_params=VMEM,
        cost_estimate=SMALL,
    )(*operands)


def split_terms(value):
    high = value.astype(BF16)
    return jnp.concatenate([high, (value - high.astype(F32)).astype(BF16)], axis=1)


def entries_kernel(pos, ids, bits, spot_ref, value_ref):
    z, y, c = pos[1], pos[2], pos[3]
    for x in range(NX):
        for at_y in range(NY):
            row = ids[x, at_y, c]
            steps = ((z - (row >> 10)) * (1 - 2 * c)) & (NZ - 1)
            crossed = ((row >> 7) & 1) ^ c
            beyond = steps > NZ // 2
            ends = (steps & (NZ // 2 - 1)) == 0
            other = jnp.where(ends, crossed, jnp.where(beyond, 1, 0))
            near_core = jnp.where(ends, 0, crossed ^ other)
            k = jnp.where(beyond, NZ - steps, steps)
            spot = jnp.where(k == 0, 0, (2 * k - 1 + near_core) * RB) + (row & (RB - 1))
            spot_ref[x, at_y] = jnp.where(((row >> 8) & (NY - 1)) == y, spot, -1)
            value_ref[x, at_y] = (2 * bits[x, at_y, c] - 1).astype(F32) * (1 + (RADIX - 1) * other).astype(F32)


def entries_of(pos, ids, bits):
    shape = (4, NX, BAG, SB)
    vm = pl.BlockSpec(memory_space=pltpu.VMEM)
    return pl.pallas_call(
        entries_kernel,
        in_specs=[pl.BlockSpec(memory_space=pltpu.SMEM), vm, vm],
        out_specs=[vm] * 2,
        out_shape=[jax.ShapeDtypeStruct(shape, jnp.int32), jax.ShapeDtypeStruct(shape, F32)],
        compiler_params=VMEM,
        cost_estimate=SMALL,
    )(pos, ids, bits)


def counts_kernel(spot_ref, value_ref, out_ref):
    rows16 = lax.broadcasted_iota(jnp.int32, (16, SB), 0).astype(jnp.int16)
    for dx in range(NX):
        spots = [jnp.broadcast_to(spot_ref[dx, k : k + 1], (16, SB)).astype(jnp.int16) for k in range(BAG)]
        values = [jnp.broadcast_to(value_ref[dx, k : k + 1], (16, SB)).astype(BF16) for k in range(BAG)]
        columns = slice(dx * SB, (dx + 1) * SB)

        def step(r, carry):
            here = rows16 + (r * 16).astype(jnp.int16)
            terms = [jnp.where(s == here, v, BF16(0)) for s, v in zip(spots, values)]
            while len(terms) > 1:
                terms = [a + b for a, b in zip(terms[::2], terms[1::2])]
            high = (terms[0] * BF16(1.0 / RADIX) + BF16(192)) - BF16(192)
            at = pl.multiple_of(r * 16, 16)
            out_ref[pl.ds(at, 16), columns] = terms[0] - high * BF16(RADIX)
            out_ref[pl.ds(HALF_ROWS + at, 16), columns] = high
            return carry

        lax.fori_loop(0, HALF_ROWS // 16, step, 0, unroll=16)


def counts_of(entries, group, *after):
    vm = pl.BlockSpec(memory_space=pltpu.VMEM)
    spec = pl.BlockSpec((None, NX, BAG, SB), lambda i: (group, 0, 0, 0))
    return pl.pallas_call(
        lambda s, v, *rest: counts_kernel(s, v, rest[-1]),
        grid=(1,),
        in_specs=[spec, spec] + [pl.BlockSpec(memory_space=pl.ANY)] * len(after),
        out_specs=pl.BlockSpec(memory_space=pltpu.VMEM),
        out_shape=jax.ShapeDtypeStruct((NC * HALF_ROWS, SAMPLES_Y), BF16),
        compiler_params=VMEM,
        cost_estimate=SMALL,
    )(*entries, *after)


def pair_kernel(own, other, *refs):
    out, sem = refs[-2:]
    copy = pltpu.make_async_copy(own, out.at[:RB], sem)
    copy.start()
    out[RB:] = other[...]
    copy.wait()


def rows_kernel(own, one, two, three, four, *refs):
    out = refs[-1]
    out[:RB] = own[...]
    for i, ref in enumerate((one, two, three)):
        out[(2 * i + 1) * RB : (2 * i + 3) * RB] = ref[...]
    out[7 * RB :] = four[...]


def call_after(kernel, out_shapes, operands, after, first=pltpu.VMEM, scratch=()):
    vm, anywhere = pl.BlockSpec(memory_space=pltpu.VMEM), pl.BlockSpec(memory_space=pl.ANY)
    return pl.pallas_call(
        kernel,
        in_specs=[pl.BlockSpec(memory_space=first)] + [vm] * (len(operands) - 1) + [anywhere] * len(after),
        out_specs=[vm] * len(out_shapes),
        out_shape=[jax.ShapeDtypeStruct(s, F32) for s in out_shapes],
        scratch_shapes=scratch,
        compiler_params=VMEM,
        cost_estimate=SMALL,
    )(*operands, *after)


def turned_terms(rows):
    turned = rows.T
    high = turned.astype(BF16)
    return jnp.concatenate([high, (turned - high.astype(F32)).astype(BF16)], axis=0)


def pool_part(terms, count_rows):
    part = jnp.dot(terms, count_rows, preferred_element_type=F32)
    return part[:E] + part[E:]


def pool_own_kernel(rows, c0, c1, c2, c3, out):
    terms = turned_terms(rows[...])
    for x, c in enumerate((c0, c1, c2, c3)):
        out[x] = pool_part(terms, c[:HALF_ROWS])


def pool_other_kernel(rows, base, c0, c1, c2, c3, out):
    terms = turned_terms(rows[...])
    for x, c in enumerate((c0, c1, c2, c3)):
        total = base[x] + pool_part(terms, c[HALF_ROWS:])
        for y in range(NY):
            out[x * NY + y] = total[:, y * SB : (y + 1) * SB].T


def cross_kernel(parts, u, v, bias, cot, crossed, out):
    x = [sum(parts[t * NY + y] for y in range(1, NY)) + parts[t * NY] for t in range(NX)]
    base_x = jnp.concatenate(x, axis=1)
    low = jnp.dot(base_x.astype(BF16), u[...], preferred_element_type=F32).astype(BF16)
    scale = jnp.dot(low, v[...], preferred_element_type=F32) + bias[...]
    crossed[...] = (base_x * scale + base_x).astype(BF16)
    upstream = cot[...].astype(F32)
    mixed = (upstream * base_x).astype(BF16)
    last = (((1,), (1,)), ((), ()))
    back_low = lax.dot_general(mixed, v[...], last, preferred_element_type=F32).astype(BF16)
    grad_x = upstream * (scale + 1.0) + lax.dot_general(
        back_low, u[...], last, preferred_element_type=F32
    )
    for t in range(NX):
        for y in range(NY):
            out[t * NY + y] = grad_x[:, t * E : (t + 1) * E]


def rows_grads(rows, terms, counts):
    total = None
    for x, c in enumerate(counts):
        part = jnp.dot(c[rows], terms[x], preferred_element_type=F32)
        total = part if total is None else total + part
    return total[:, :E] + total[:, E:]


def other_grads_kernel(g, c0, c1, c2, c3, out, terms):
    for x in range(NX):
        terms[x] = split_terms(g[x * SAMPLES_Y : (x + 1) * SAMPLES_Y])
    out[...] = rows_grads(slice(HALF_ROWS, NC * HALF_ROWS), terms, (c0, c1, c2, c3))


def own_grads_kernel(terms, c0, c1, c2, c3, out):
    out[...] = rows_grads(slice(0, HALF_ROWS), terms, (c0, c1, c2, c3))


def sums_kernel(a, b, keep, one, two, three, four):
    keep[...] = a[:RB] + b[:RB]
    for i, ref in enumerate((one, two, three)):
        s = slice((2 * i + 1) * RB, (2 * i + 3) * RB)
        ref[...] = a[s] + b[s]
    four[...] = a[7 * RB :] + b[7 * RB :]


def last_sums_kernel(keep, one, two, three, four, mine, other):
    mine[...] = (keep[...] + four[...]) + (one[:RB] + two[:RB] + three[:RB])
    other[...] = one[RB:] + two[RB:] + three[RB:]


def update_kernel(a, b, rows, accum, new_rows, new_accum):
    grad = a[...] + b[...]
    mean = jnp.sum(grad * grad, axis=1, keepdims=True) * (1.0 / E)
    mean_row = jnp.broadcast_to(mean, (RB, E)).T[:1]
    total = accum[...] + mean_row
    new_accum[...] = total
    total_column = jnp.broadcast_to(total, (E, RB)).T
    new_rows[...] = rows[...] - learn_rate * grad / jnp.sqrt(total_column)


def per_device(
    table_rows, row_accum, row_ids, sketch_bits, cross_u, cross_v, cross_bias, cotangent
):
    pos = jnp.stack([lax.axis_index(a) for a in ("hst", "z", "y", "core")]).astype(jnp.int32)
    own = table_rows[0]

    def at_own_z(entries):
        by_owner = entries[0].reshape(BAG, -1, SB).transpose(1, 0, 2).reshape(NX, NZ, NY, NC, BAG, SB)
        return lax.dynamic_index_in_dim(by_owner, pos[1], 1, keepdims=False)

    ids, bits = at_own_z(row_ids), at_own_z(sketch_bits)
    other = move(own, "core", 1)
    (pair,) = call_after(
        pair_kernel, [(2 * RB, E)], (own, other), (), pl.ANY, [pltpu.SemaphoreType.DMA]
    )
    four, three = move_ways(own, "z", 4), move_ways(pair, "z", 3)
    two, one = move_ways(pair, "z", 2), move_ways(pair, "z", 1)
    entries = entries_of(pos, ids, bits)
    counts = [counts_of(entries, x) for x in range(NX)]
    (rows,) = call_after(rows_kernel, [(HALF_ROWS, E)], (own, one, two, three, four), counts)
    other_rows = move(rows, "core", 1)
    (bags,) = call(pool_own_kernel, [((NX, E, SAMPLES_Y), F32)], rows, *counts)
    blocks = ((NX * NY, SB, E), F32)
    (bags,) = call(pool_other_kernel, [blocks], other_rows, bags, *counts)

    def exchange(parts):
        return lax.all_to_all(parts, ("hst", "y"), split_axis=0, concat_axis=0, tiled=True)

    crossed, bag_grads = call(
        cross_kernel,
        [(cotangent.shape, BF16), blocks],
        exchange(bags),
        cross_u,
        cross_v,
        cross_bias.reshape(1, -1),
        cotangent,
    )
    bag_grads = exchange(bag_grads).reshape(NX * NY * SB, E)
    block, pair, half = (((n * RB, E), F32) for n in (1, 2, 8))
    terms_shape = ((NX, SAMPLES_Y, 2 * E), BF16)
    other_grads, terms = call(other_grads_kernel, [half, terms_shape], bag_grads, *counts)
    from_core = move(other_grads, "core", 1)
    (own_grads,) = call(own_grads_kernel, [half], terms, *counts)
    keep, *sums = call(sums_kernel, [block, pair, pair, pair, block], own_grads, from_core)
    far = [move_ways(sums[s - 1], "z", -s) for s in (4, 3, 2, 1)]
    mine, others = call(last_sums_kernel, [block] * 2, keep, *far[::-1])
    new_rows, new_accum = call(
        update_kernel, [block, ((1, RB), F32)], mine, move(others, "core", 1), own, row_accum
    )
    return (crossed, new_rows[None], new_accum)


def solution(mesh):
    grid = Mesh(mesh.devices.reshape(NX, NZ, NY, NC), ("hst", "z", "y", "core"))
    local = ("z", "y", "core")
    in_specs = (
        P("hst", local, None),
        P("hst", local),
        P("hst", None, None),
        P("hst", None, None),
        P(),
        P(),
        P(),
        P(("hst",) + local, None),
    )
    out_specs = (P(("hst",) + local, None), P("hst", local, None), P("hst", local))
    return jax.shard_map(
        per_device, mesh=grid, in_specs=in_specs, out_specs=out_specs, check_vma=False
    )
```

time: 336 us -> 94.1 us (0.28)
  the two profiles are of different devices: /device:TPU:1 before, /device:TPU:33 now
where the time goes in v3:
time: 94.1 us; the launch traced here: 93.9 us
  blocking collectives  41.1 us (44%)
  starting transfers between devices  26.6 us (28%)
  Pallas kernels  13.4 us (14%)
  waiting for transfers between devices  9.9 us (11%)
  local copies, waits for them, and re-layouts  1.89 us (2%)
    all_to_all x2, blocking collectives, exchange(): lax.all_to_all(parts, ('hst', 'y'), split_axis=0, concat_axis=0, tiled=True)  41.1 us
    ppermute x8, starting transfers between devices, move_ways(): return lax.ppermute(array, (axis, 'core'), pairs)  17.8 us
    ppermute x4, starting transfers between devices, move(): return lax.ppermute(array, axis, [(i, (i + step) % n) for i in range(n)])  8.79 us
    ppermute x8, waiting for transfers between devices, move_ways(): return lax.ppermute(array, (axis, 'core'), pairs)  8.47 us
    pallas_call x8, Pallas kernels, call(): pl.pallas_call(kernel, in_specs=[vm] * len(operands), out_specs=[vm] * le...  7.43 us
    pallas_call x4, Pallas kernels, counts_of(): pl.pallas_call(lambda s, v, *rest: counts_kernel(s, v, rest[-1]), grid=(1...  5.25 us
  transfers between devices with their start and end apart: 12, of which 5 were waited for; matrix products, arithmetic and copies ran while one was open for 1% of the time, Pallas kernels for 9%

profile of v3, /device:TPU:33, one launch (start us, length us, event | category | flops | bytes accessed | tf_op | source)
XLA Modules:
  0.0 93.9 jit_solution(1006472736670012216)
XLA Ops:
  1.4 6.0 %collective-permute-start.4 = (f32[128,128]{1,0:T(8,128)}, f32[128,128]{1,0:T(8,128)S(1)}, u32[]{:S(2)}, u32[]{:S(2)}) collective-permute-start(f32[128,128]{1,0:T(8,128)} %bitcast.24), channel_id=1, source_target_pairs={{0,32},{1,33},{8,40},{9,41},{16,48},{17,49},{24,56},{25,57},{32,0}... | collective-permute-start | bytes 196616 | tf_op jit(solution)/shard_map/ppermute | solution.py:32
  9.1 1.2 %collective-permute-start.2 = (f32[256,128]{1,0:T(8,128)S(1)}, f32[256,128]{1,0:T(8,128)S(1)}, u32[]{:S(2)}, u32[]{:S(2)}) collective-permute-start(f32[256,128]{1,0:T(8,128)S(1)} %shard_map.103), channel_id=1, source_target_pairs={{0,16},{1,49},{8,24},{9,57},{16,32},{17,1},{24,40},{25,9},{32,48},... | collective-permute-start | bytes 393224 | tf_op jit(solution)/shard_map/ppermute | solution.py:32
  10.2 3.0 %collective-permute-start.1 = (f32[256,128]{1,0:T(8,128)S(1)}, f32[256,128]{1,0:T(8,128)S(1)}, u32[]{:S(2)}, u32[]{:S(2)}) collective-permute-start(f32[256,128]{1,0:T(8,128)S(1)} %shard_map.103), channel_id=1, source_target_pairs={{0,8},{1,57},{8,16},{9,1},{16,24},{17,9},{24,32},{25,17},{32,40},{... | collective-permute-start | bytes 393224 | tf_op jit(solution)/shard_map/ppermute | solution.py:32
  13.2 1.0 %dynamic-slice_bitcast_fusion = (s32[4,4,2,8,128]{4,3,2,1,0:T(8,128)S(1)}, s32[4,4,2,8,128]{4,3,2,1,0:T(8,128)S(1)}) fusion(s32[4,8,4,2,8,128]{5,4,3,2,1,0:T(8,128)} %bitcast.29, s32[]{:T(128)S(6)} %select_n.5, s32[4,8,4,2,8,128]{5,4,3,2,1,0:T(8,128)} %bitcast.30), kind=kLoop, calls=%fused_computation | loop fusion | bytes 524292 | tf_op jit(solution)/shard_map/jit(dynamic_index_in_dim)/squeeze | solution.py:238
  14.9 1.3 %shard_map.108.refs_3_.c3 = bf16[2048,512]{1,0:T(8,128)(2,1)S(1)} custom-call(s32[4,4,8,128]{3,2,1,0:T(8,128)S(1)} %get-tuple-element.18.s, f32[4,4,8,128]{3,2,1,0:T(8,128)S(1)} %get-tuple-element.19.v), custom_call_target="tpu_custom_call" | custom-call | bytes 1024 | tf_op jit(solution)/shard_map/pallas_call | solution.py:106
  16.2 1.3 %shard_map.107.refs_2_.c2 = bf16[2048,512]{1,0:T(8,128)(2,1)S(1)} custom-call(s32[4,4,8,128]{3,2,1,0:T(8,128)S(1)} %get-tuple-element.18.s, f32[4,4,8,128]{3,2,1,0:T(8,128)S(1)} %get-tuple-element.19.v), custom_call_target="tpu_custom_call" | custom-call | bytes 1024 | tf_op jit(solution)/shard_map/pallas_call | solution.py:106
  17.6 1.3 %shard_map.106.refs_1_.c1 = bf16[2048,512]{1,0:T(8,128)(2,1)S(1)} custom-call(s32[4,4,8,128]{3,2,1,0:T(8,128)S(1)} %get-tuple-element.18.s, f32[4,4,8,128]{3,2,1,0:T(8,128)S(1)} %get-tuple-element.19.v), custom_call_target="tpu_custom_call" | custom-call | bytes 1024 | tf_op jit(solution)/shard_map/pallas_call | solution.py:106
  18.9 1.3 %shard_map.105.refs_0_.c0 = bf16[2048,512]{1,0:T(8,128)(2,1)S(1)} custom-call(s32[4,4,8,128]{3,2,1,0:T(8,128)S(1)} %get-tuple-element.18.s, f32[4,4,8,128]{3,2,1,0:T(8,128)S(1)} %get-tuple-element.19.v), custom_call_target="tpu_custom_call" | custom-call | bytes 1024 | tf_op jit(solution)/shard_map/pallas_call | solution.py:106
  20.3 1.7 %collective-permute-start.5 = (f32[1024,128]{1,0:T(8,128)S(1)}, f32[1024,128]{1,0:T(8,128)S(1)}, u32[]{:S(2)}, u32[]{:S(2)}) collective-permute-start(f32[1024,128]{1,0:T(8,128)S(1)} %shard_map.109.rows), channel_id=1, source_target_pairs={{0,1},{1,0},{2,3},{3,2},{4,5},{5,4},{6,7},{7,6},{8,9},{9,8},{10,11... | collective-permute-start | bytes 1572872 | tf_op jit(solution)/shard_map/ppermute | solution.py:24
  22.0 1.3 %shard_map.110.base = f32[4,128,512]{2,1,0:T(8,128)S(1)} custom-call(f32[1024,128]{1,0:T(8,128)S(1)} %shard_map.109.rows, bf16[2048,512]{1,0:T(8,128)(2,1)S(1)} %shard_map.105.refs_0_.c0, bf16[2048,512]{1,0:T(8,128)(2,1)S(1)} %shard_map.106.refs_1_.c1, bf16[2048,512]{1,0:T(8,128)(2,1)S(1)} %shard_map.107.refs_2_.c2, bf16[2048,512]{1,0:T(8,128)(2,1)S(1)} %shard_map.108.refs_3_.c3), custom_call_target="tpu_custom_call" | custom-call | bytes 1024 | tf_op jit(solution)/shard_map/pallas_call | solution.py:37
  23.5 1.4 %shard_map.111 = f32[16,128,128]{2,1,0:T(8,128)S(1)} custom-call(f32[1024,128]{1,0:T(8,128)S(1)} %collective-permute-done.5.rows, f32[4,128,512]{2,1,0:T(8,128)S(1)} %shard_map.110.base, bf16[2048,512]{1,0:T(8,128)(2,1)S(1)} %shard_map.105.refs_0_.c0, bf16[2048,512]{1,0:T(8,128)(2,1)S(1)} %shard_map.106.refs_1_.c1, ...), custom_call_target="tpu_custom_call" | custom-call | bytes 1024 | tf_op jit(solution)/shard_map/pallas_call | solution.py:37
  25.0 22.8 %all_to_all.10.parts = f32[16,128,128]{2,1,0:T(8,128)S(1)} all-to-all(f32[16,128,128]{2,1,0:T(8,128)S(1)} %shard_map.111), channel_id=1, replica_groups=mesh['hst'=4,'z'=8,'y'=4,'core'=2] {'hst','y'}, dimensions={0} | all-to-all | bytes 2097152 | tf_op jit(solution)/shard_map/all_to_all | solution.py:256
  47.8 1.3 %shard_map.112 = (bf16[128,512]{1,0:T(8,128)(2,1)}, f32[16,128,128]{2,1,0:T(8,128)S(1)}) custom-call(f32[16,128,128]{2,1,0:T(8,128)S(1)} %all_to_all.10.parts, bf16[512,512]{1,0:T(8,128)(2,1)S(1)} %copy-done.2, bf16[512,512]{1,0:T(8,128)(2,1)S(1)} %copy-done.3, f32[1,512]{1,0:T(1,128)S(1)} %bitcast.28, bf16[128,512]{1,0:T(8,128)(2,1)S(1)} %copy-done.4), custom_call_target="tpu_custom_call" | custom-call | bytes 1024 | tf_op jit(solution)/shard_map/pallas_call | solution.py:37
  49.0 18.3 %all_to_all.11 = f32[16,128,128]{2,1,0:T(8,128)S(1)} all-to-all(f32[16,128,128]{2,1,0:T(8,128)S(1)} %get-tuple-element.21), channel_id=1, replica_groups=mesh['hst'=4,'z'=8,'y'=4,'core'=2] {'hst','y'}, dimensions={0} | all-to-all | bytes 2097152 | tf_op jit(solution)/shard_map/all_to_all | solution.py:256
  67.4 1.3 %shard_map.113 = (f32[1024,128]{1,0:T(8,128)S(1)}, bf16[4,512,256]{2,1,0:T(8,128)(2,1)S(1)}) custom-call(f32[2048,128]{1,0:T(8,128)S(1)} %bitcast.22, bf16[2048,512]{1,0:T(8,128)(2,1)S(1)} %shard_map.105.refs_0_.c0, bf16[2048,512]{1,0:T(8,128)(2,1)S(1)} %shard_map.106.refs_1_.c1, bf16[2048,512]{1,0:T(8,128)(2,1)S(1)} %shard_map.107.refs_2_.c2, ...), custom_call_target="tpu_custom_call" | custom-call | bytes 1024 | tf_op jit(solution)/shard_map/pallas_call | solution.py:37
  68.6 3.3 %collective-permute-start.6 = (f32[1024,128]{1,0:T(8,128)S(1)}, f32[1024,128]{1,0:T(8,128)S(1)}, u32[]{:S(2)}, u32[]{:S(2)}) collective-permute-start(f32[1024,128]{1,0:T(8,128)S(1)} %get-tuple-element.23), channel_id=1, source_target_pairs={{0,1},{1,0},{2,3},{3,2},{4,5},{5,4},{6,7},{7,6},{8,9},{9,8},{10,11... | collective-permute-start | bytes 1572872 | tf_op jit(solution)/shard_map/ppermute | solution.py:24
  72.0 1.2 %shard_map.114.a = f32[1024,128]{1,0:T(8,128)S(1)} custom-call(bf16[4,512,256]{2,1,0:T(8,128)(2,1)S(1)} %get-tuple-element.22.terms, bf16[2048,512]{1,0:T(8,128)(2,1)S(1)} %shard_map.105.refs_0_.c0, bf16[2048,512]{1,0:T(8,128)(2,1)S(1)} %shard_map.106.refs_1_.c1, bf16[2048,512]{1,0:T(8,128)(2,1)S(1)} %shard_map.107.refs_2_.c2, ...), custom_call_target="tpu_custom_call" | custom-call | bytes 1024 | tf_op jit(solution)/shard_map/pallas_call | solution.py:37
  73.9 2.6 %collective-permute-start.8 = (f32[256,128]{1,0:T(8,128)S(1)}, f32[256,128]{1,0:T(8,128)S(1)}, u32[]{:S(2)}, u32[]{:S(2)}) collective-permute-start(f32[256,128]{1,0:T(8,128)S(1)} %get-tuple-element.26), channel_id=1, source_target_pairs={{0,48},{1,17},{8,56},{9,25},{16,0},{17,33},{24,8},{25,41},{32,16},... | collective-permute-start | bytes 393224 | tf_op jit(solution)/shard_map/ppermute | solution.py:32
  76.5 1.6 %collective-permute-start.9 = (f32[256,128]{1,0:T(8,128)S(1)}, f32[256,128]{1,0:T(8,128)S(1)}, u32[]{:S(2)}, u32[]{:S(2)}) collective-permute-start(f32[256,128]{1,0:T(8,128)S(1)} %get-tuple-element.27), channel_id=1, source_target_pairs={{0,40},{1,25},{8,48},{9,33},{16,56},{17,41},{24,0},{25,49},{32,8},... | collective-permute-start | bytes 393224 | tf_op jit(solution)/shard_map/ppermute | solution.py:32
  78.1 2.4 %collective-permute-start.10 = (f32[128,128]{1,0:T(8,128)S(1)}, f32[128,128]{1,0:T(8,128)S(1)}, u32[]{:S(2)}, u32[]{:S(2)}) collective-permute-start(f32[128,128]{1,0:T(8,128)S(1)} %get-tuple-element.28), channel_id=1, source_target_pairs={{0,32},{1,33},{8,40},{9,41},{16,48},{17,49},{24,56},{25,57},{32,0}... | collective-permute-start | bytes 196616 | tf_op jit(solution)/shard_map/ppermute | solution.py:32
  80.5 7.5 %collective-permute-done.10.four = f32[128,128]{1,0:T(8,128)S(1)} collective-permute-done((f32[128,128]{1,0:T(8,128)S(1)}, f32[128,128]{1,0:T(8,128)S(1)}, u32[]{:S(2)}, u32[]{:S(2)}) %collective-permute-start.10) | collective-permute-done | bytes 65568 | tf_op jit(solution)/shard_map/ppermute | solution.py:32
  88.0 1.0 %collective-permute-done.9.three = f32[256,128]{1,0:T(8,128)S(1)} collective-permute-done((f32[256,128]{1,0:T(8,128)S(1)}, f32[256,128]{1,0:T(8,128)S(1)}, u32[]{:S(2)}, u32[]{:S(2)}) %collective-permute-start.9) | collective-permute-done | bytes 131104 | tf_op jit(solution)/shard_map/ppermute | solution.py:32
  89.0 3.0 %collective-permute-start.11 = (f32[128,128]{1,0:T(8,128)S(1)}, f32[128,128]{1,0:T(8,128)S(1)}, u32[]{:S(2)}, u32[]{:S(2)}) collective-permute-start(f32[128,128]{1,0:T(8,128)S(1)} %get-tuple-element.30), channel_id=1, source_target_pairs={{0,1},{1,0},{2,3},{3,2},{4,5},{5,4},{6,7},{7,6},{8,9},{9,8},{10,11... | collective-permute-start | bytes 196616 | tf_op jit(solution)/shard_map/ppermute | solution.py:24
  92.1 0.9 collective-permute-done.11.b
  (33 shorter events, 5.0 us)
Async XLA Ops:
  0.6 6.8 %collective-permute-start = (f32[128,128]{1,0:T(8,128)}, f32[128,128]{1,0:T(8,128)S(1)}, u32[]{:S(2)}, u32[]{:S(2)}) collective-permute-start(f32[128,128]{1,0:T(8,128)} %bitcast.23), channel_id=1, source_target_pairs={{0,1},{1,0},{2,3},{3,2},{4,5},{5,4},{6,7},{7,6},{8,9},{9,8},{10,11... | collective-permute-start | bytes 196616 | tf_op jit(solution)/shard_map/ppermute | solution.py:24
  1.4 18.8 %collective-permute-start.4 = (f32[128,128]{1,0:T(8,128)}, f32[128,128]{1,0:T(8,128)S(1)}, u32[]{:S(2)}, u32[]{:S(2)}) collective-permute-start(f32[128,128]{1,0:T(8,128)} %bitcast.24), channel_id=1, source_target_pairs={{0,32},{1,33},{8,40},{9,41},{16,48},{17,49},{24,56},{25,57},{32,0}... | collective-permute-start | bytes 196616 | tf_op jit(solution)/shard_map/ppermute | solution.py:32
  7.4 0.9 copy-start
  8.4 11.9 %collective-permute-start.3 = (f32[256,128]{1,0:T(8,128)S(1)}, f32[256,128]{1,0:T(8,128)S(1)}, u32[]{:S(2)}, u32[]{:S(2)}) collective-permute-start(f32[256,128]{1,0:T(8,128)S(1)} %shard_map.103), channel_id=1, source_target_pairs={{0,24},{1,41},{8,32},{9,49},{16,40},{17,57},{24,48},{25,1},{32,56}... | collective-permute-start | bytes 393224 | tf_op jit(solution)/shard_map/ppermute | solution.py:32
  9.1 11.2 %collective-permute-start.2 = (f32[256,128]{1,0:T(8,128)S(1)}, f32[256,128]{1,0:T(8,128)S(1)}, u32[]{:S(2)}, u32[]{:S(2)}) collective-permute-start(f32[256,128]{1,0:T(8,128)S(1)} %shard_map.103), channel_id=1, source_target_pairs={{0,16},{1,49},{8,24},{9,57},{16,32},{17,1},{24,40},{25,9},{32,48},... | collective-permute-start | bytes 393224 | tf_op jit(solution)/shard_map/ppermute | solution.py:32
  10.2 10.0 %collective-permute-start.1 = (f32[256,128]{1,0:T(8,128)S(1)}, f32[256,128]{1,0:T(8,128)S(1)}, u32[]{:S(2)}, u32[]{:S(2)}) collective-permute-start(f32[256,128]{1,0:T(8,128)S(1)} %shard_map.103), channel_id=1, source_target_pairs={{0,8},{1,57},{8,16},{9,1},{16,24},{17,9},{24,32},{25,17},{32,40},{... | collective-permute-start | bytes 393224 | tf_op jit(solution)/shard_map/ppermute | solution.py:32
  17.6 2.7 %copy-start.1 = (f32[1,128,128]{2,1,0:T(8,128)S(1)}, f32[1,128,128]{2,1,0:T(8,128)}, u32[]{:S(2)}) copy-start(f32[1,128,128]{2,1,0:T(8,128)} %param.8) | copy-start | bytes 196612
  20.3 3.2 %collective-permute-start.5 = (f32[1024,128]{1,0:T(8,128)S(1)}, f32[1024,128]{1,0:T(8,128)S(1)}, u32[]{:S(2)}, u32[]{:S(2)}) collective-permute-start(f32[1024,128]{1,0:T(8,128)S(1)} %shard_map.109.rows), channel_id=1, source_target_pairs={{0,1},{1,0},{2,3},{3,2},{4,5},{5,4},{6,7},{7,6},{8,9},{9,8},{10,11... | collective-permute-start | bytes 1572872 | tf_op jit(solution)/shard_map/ppermute | solution.py:24
  24.9 22.8 %copy-start.2 = (bf16[512,512]{1,0:T(8,128)(2,1)S(1)}, bf16[512,512]{1,0:T(8,128)(2,1)}, u32[]{:S(2)}) copy-start(bf16[512,512]{1,0:T(8,128)(2,1)} %u.1) | copy-start | bytes 1572868
  24.9 22.8 %copy-start.3 = (bf16[512,512]{1,0:T(8,128)(2,1)S(1)}, bf16[512,512]{1,0:T(8,128)(2,1)}, u32[]{:S(2)}) copy-start(bf16[512,512]{1,0:T(8,128)(2,1)} %v.1) | copy-start | bytes 1572868
  24.9 22.8 %copy-start.4 = (bf16[128,512]{1,0:T(8,128)(2,1)S(1)}, bf16[128,512]{1,0:T(8,128)(2,1)}, u32[]{:S(2)}) copy-start(bf16[128,512]{1,0:T(8,128)(2,1)} %cot.1) | copy-start | bytes 393220
  24.9 22.8 %copy-start.5 = (f32[512]{0:T(512)S(1)}, f32[512]{0:T(512)}, u32[]{:S(2)}) copy-start(f32[512]{0:T(512)} %param.14) | copy-start | bytes 6148
  68.6 4.9 %collective-permute-start.6 = (f32[1024,128]{1,0:T(8,128)S(1)}, f32[1024,128]{1,0:T(8,128)S(1)}, u32[]{:S(2)}, u32[]{:S(2)}) collective-permute-start(f32[1024,128]{1,0:T(8,128)S(1)} %get-tuple-element.23), channel_id=1, source_target_pairs={{0,1},{1,0},{2,3},{3,2},{4,5},{5,4},{6,7},{7,6},{8,9},{9,8},{10,11... | collective-permute-start | bytes 1572872 | tf_op jit(solution)/shard_map/ppermute | solution.py:24
  72.0 21.0 %copy-start.6 = (f32[1,128]{1,0:T(1,128)S(1)}, f32[1,128]{1,0:T(1,128)}, u32[]{:S(2)}) copy-start(f32[1,128]{1,0:T(1,128)} %accum.1) | copy-start | bytes 1540
  73.6 14.4 %collective-permute-start.7 = (f32[256,128]{1,0:T(8,128)S(1)}, f32[256,128]{1,0:T(8,128)S(1)}, u32[]{:S(2)}, u32[]{:S(2)}) collective-permute-start(f32[256,128]{1,0:T(8,128)S(1)} %get-tuple-element.25), channel_id=1, source_target_pairs={{0,56},{1,9},{8,0},{9,17},{16,8},{17,25},{24,16},{25,33},{32,24},{... | collective-permute-start | bytes 393224 | tf_op jit(solution)/shard_map/ppermute | solution.py:32
  73.9 14.2 %collective-permute-start.8 = (f32[256,128]{1,0:T(8,128)S(1)}, f32[256,128]{1,0:T(8,128)S(1)}, u32[]{:S(2)}, u32[]{:S(2)}) collective-permute-start(f32[256,128]{1,0:T(8,128)S(1)} %get-tuple-element.26), channel_id=1, source_target_pairs={{0,48},{1,17},{8,56},{9,25},{16,0},{17,33},{24,8},{25,41},{32,16},... | collective-permute-start | bytes 393224 | tf_op jit(solution)/shard_map/ppermute | solution.py:32
  76.5 12.5 %collective-permute-start.9 = (f32[256,128]{1,0:T(8,128)S(1)}, f32[256,128]{1,0:T(8,128)S(1)}, u32[]{:S(2)}, u32[]{:S(2)}) collective-permute-start(f32[256,128]{1,0:T(8,128)S(1)} %get-tuple-element.27), channel_id=1, source_target_pairs={{0,40},{1,25},{8,48},{9,33},{16,56},{17,41},{24,0},{25,49},{32,8},... | collective-permute-start | bytes 393224 | tf_op jit(solution)/shard_map/ppermute | solution.py:32
  78.1 9.9 %collective-permute-start.10 = (f32[128,128]{1,0:T(8,128)S(1)}, f32[128,128]{1,0:T(8,128)S(1)}, u32[]{:S(2)}, u32[]{:S(2)}) collective-permute-start(f32[128,128]{1,0:T(8,128)S(1)} %get-tuple-element.28), channel_id=1, source_target_pairs={{0,32},{1,33},{8,40},{9,41},{16,48},{17,49},{24,56},{25,57},{32,0}... | collective-permute-start | bytes 196616 | tf_op jit(solution)/shard_map/ppermute | solution.py:32
  89.0 3.9 %collective-permute-start.11 = (f32[128,128]{1,0:T(8,128)S(1)}, f32[128,128]{1,0:T(8,128)S(1)}, u32[]{:S(2)}, u32[]{:S(2)}) collective-permute-start(f32[128,128]{1,0:T(8,128)S(1)} %get-tuple-element.30), channel_id=1, source_target_pairs={{0,1},{1,0},{2,3},{3,2},{4,5},{5,4},{6,7},{7,6},{8,9},{9,8},{10,11... | collective-permute-start | bytes 196616 | tf_op jit(solution)/shard_map/ppermute | solution.py:24

commit v4 on v3

--- a/solution.py
+++ b/solution.py
@@ -49,34 +49,25 @@
     return jnp.concatenate([high, (value - high.astype(F32)).astype(BF16)], axis=1)
 
 
-def entries_kernel(pos, ids, bits, spot_ref, value_ref):
-    z, y, c = pos[1], pos[2], pos[3]
-    for x in range(NX):
-        for at_y in range(NY):
-            row = ids[x, at_y, c]
-            steps = ((z - (row >> 10)) * (1 - 2 * c)) & (NZ - 1)
-            crossed = ((row >> 7) & 1) ^ c
-            beyond = steps > NZ // 2
-            ends = (steps & (NZ // 2 - 1)) == 0
-            other = jnp.where(ends, crossed, jnp.where(beyond, 1, 0))
-            near_core = jnp.where(ends, 0, crossed ^ other)
-            k = jnp.where(beyond, NZ - steps, steps)
-            spot = jnp.where(k == 0, 0, (2 * k - 1 + near_core) * RB) + (row & (RB - 1))
-            spot_ref[x, at_y] = jnp.where(((row >> 8) & (NY - 1)) == y, spot, -1)
-            value_ref[x, at_y] = (2 * bits[x, at_y, c] - 1).astype(F32) * (1 + (RADIX - 1) * other).astype(F32)
-
-
-def entries_of(pos, ids, bits):
-    shape = (4, NX, BAG, SB)
-    vm = pl.BlockSpec(memory_space=pltpu.VMEM)
-    return pl.pallas_call(
-        entries_kernel,
-        in_specs=[pl.BlockSpec(memory_space=pltpu.SMEM), vm, vm],
-        out_specs=[vm] * 2,
-        out_shape=[jax.ShapeDtypeStruct(shape, jnp.int32), jax.ShapeDtypeStruct(shape, F32)],
-        compiler_params=VMEM,
-        cost_estimate=SMALL,
-    )(pos, ids, bits)
+def entries_of(row_ids, sketch_bits):
+    z, y, c = (lax.axis_index(a).astype(jnp.int32) for a in ("z", "y", "core"))
+
+    def at_own(entries):
+        by_owner = entries[0].reshape(BAG, -1, SB).transpose(1, 0, 2).reshape(NX, NZ, NY, NC, BAG, SB)
+        part = lax.dynamic_slice(by_owner, (0, z, 0, c, 0, 0), (NX, 1, NY, 1, BAG, SB))
+        return part.reshape(NX, NY, BAG, SB)
+
+    row, bits = at_own(row_ids), at_own(sketch_bits)
+    steps = ((z - (row >> 10)) * (1 - 2 * c)) & (NZ - 1)
+    crossed = ((row >> 7) & 1) ^ c
+    beyond = steps > NZ // 2
+    ends = (steps & (NZ // 2 - 1)) == 0
+    other = jnp.where(ends, crossed, beyond.astype(jnp.int32))
+    near_core = jnp.where(ends, 0, crossed ^ other)
+    k = jnp.where(beyond, NZ - steps, steps)
+    spot = jnp.where(k == 0, 0, (2 * k - 1 + near_core) * RB) + (row & (RB - 1))
+    spot = jnp.where(((row >> 8) & (NY - 1)) == y, spot, -1)
+    return spot, ((2 * bits - 1) * (1 + (RADIX - 1) * other)).astype(F32)
 
 
 def counts_kernel(spot_ref, value_ref, out_ref):
@@ -114,30 +105,34 @@
     )(*entries, *after)
 
 
-def pair_kernel(own, other, *refs):
-    out, sem = refs[-2:]
-    copy = pltpu.make_async_copy(own, out.at[:RB], sem)
-    copy.start()
+def copy_kernel(a, *refs):
+    refs[-1][...] = a[...]
+
+
+def pair_kernel(own, other, out):
+    out[:RB] = own[...]
     out[RB:] = other[...]
-    copy.wait()
-
-
-def rows_kernel(own, one, two, three, four, *refs):
+
+
+def onward_kernel(three, *refs):
+    refs[-1][...] = three[:RB]
+
+
+def rows_kernel(pair, one, two, three, four, *refs):
     out = refs[-1]
-    out[:RB] = own[...]
+    out[:RB] = pair[:RB]
     for i, ref in enumerate((one, two, three)):
         out[(2 * i + 1) * RB : (2 * i + 3) * RB] = ref[...]
     out[7 * RB :] = four[...]
 
 
-def call_after(kernel, out_shapes, operands, after, first=pltpu.VMEM, scratch=()):
+def call_after(kernel, out_shapes, operands, after):
     vm, anywhere = pl.BlockSpec(memory_space=pltpu.VMEM), pl.BlockSpec(memory_space=pl.ANY)
     return pl.pallas_call(
         kernel,
-        in_specs=[pl.BlockSpec(memory_space=first)] + [vm] * (len(operands) - 1) + [anywhere] * len(after),
+        in_specs=[vm] * len(operands) + [anywhere] * len(after),
         out_specs=[vm] * len(out_shapes),
         out_shape=[jax.ShapeDtypeStruct(s, F32) for s in out_shapes],
-        scratch_shapes=scratch,
         compiler_params=VMEM,
         cost_estimate=SMALL,
     )(*operands, *after)
@@ -204,7 +199,7 @@
     out[...] = rows_grads(slice(0, HALF_ROWS), terms, (c0, c1, c2, c3))
 
 
-def sums_kernel(a, b, keep, one, two, three, four):
+def sums_kernel(a, b, four, two, one, three, keep):
     keep[...] = a[:RB] + b[:RB]
     for i, ref in enumerate((one, two, three)):
         s = slice((2 * i + 1) * RB, (2 * i + 3) * RB)
@@ -212,8 +207,13 @@
     four[...] = a[7 * RB :] + b[7 * RB :]
 
 
-def last_sums_kernel(keep, one, two, three, four, mine, other):
-    mine[...] = (keep[...] + four[...]) + (one[:RB] + two[:RB] + three[:RB])
+def relay_kernel(three, four, out):
+    out[:RB] = three[:RB] + four[...]
+    out[RB:] = three[RB:]
+
+
+def last_sums_kernel(three, two, one, keep, mine, other):
+    mine[...] = keep[...] + (one[:RB] + two[:RB] + three[:RB])
     other[...] = one[RB:] + two[RB:] + three[RB:]
 
 
@@ -224,29 +224,24 @@
     total = accum[...] + mean_row
     new_accum[...] = total
     total_column = jnp.broadcast_to(total, (E, RB)).T
-    new_rows[...] = rows[...] - learn_rate * grad / jnp.sqrt(total_column)
+    new_rows[...] = rows[:RB] - learn_rate * grad / jnp.sqrt(total_column)
 
 
 def per_device(
     table_rows, row_accum, row_ids, sketch_bits, cross_u, cross_v, cross_bias, cotangent
 ):
-    pos = jnp.stack([lax.axis_index(a) for a in ("hst", "z", "y", "core")]).astype(jnp.int32)
     own = table_rows[0]
 
-    def at_own_z(entries):
-        by_owner = entries[0].reshape(BAG, -1, SB).transpose(1, 0, 2).reshape(NX, NZ, NY, NC, BAG, SB)
-        return lax.dynamic_index_in_dim(by_owner, pos[1], 1, keepdims=False)
-
-    ids, bits = at_own_z(row_ids), at_own_z(sketch_bits)
     other = move(own, "core", 1)
-    (pair,) = call_after(
-        pair_kernel, [(2 * RB, E)], (own, other), (), pl.ANY, [pltpu.SemaphoreType.DMA]
-    )
-    four, three = move_ways(own, "z", 4), move_ways(pair, "z", 3)
-    two, one = move_ways(pair, "z", 2), move_ways(pair, "z", 1)
-    entries = entries_of(pos, ids, bits)
-    counts = [counts_of(entries, x) for x in range(NX)]
-    (rows,) = call_after(rows_kernel, [(HALF_ROWS, E)], (own, one, two, three, four), counts)
+    (held,) = call(copy_kernel, [((RB, E), F32)], own)
+    (pair,) = call(pair_kernel, [((2 * RB, E), F32)], held, other)
+    three, two, one = (move_ways(pair, "z", s) for s in (3, 2, 1))
+    entries = entries_of(row_ids, sketch_bits)
+    counts = [counts_of(entries, x) for x in range(2)]
+    (onward,) = call_after(onward_kernel, [(RB, E)], (three,), counts)
+    four = move_ways(onward, "z", 1)
+    counts = counts + [counts_of(entries, x, onward) for x in range(2, NX)]
+    (rows,) = call_after(rows_kernel, [(HALF_ROWS, E)], (pair, one, two, three, four), counts)
     other_rows = move(rows, "core", 1)
     (bags,) = call(pool_own_kernel, [((NX, E, SAMPLES_Y), F32)], rows, *counts)
     blocks = ((NX * NY, SB, E), F32)
@@ -265,16 +260,20 @@
         cotangent,
     )
     bag_grads = exchange(bag_grads).reshape(NX * NY * SB, E)
-    block, pair, half = (((n * RB, E), F32) for n in (1, 2, 8))
+    block, pair_shape, half = (((n * RB, E), F32) for n in (1, 2, 8))
     terms_shape = ((NX, SAMPLES_Y, 2 * E), BF16)
     other_grads, terms = call(other_grads_kernel, [half, terms_shape], bag_grads, *counts)
     from_core = move(other_grads, "core", 1)
     (own_grads,) = call(own_grads_kernel, [half], terms, *counts)
-    keep, *sums = call(sums_kernel, [block, pair, pair, pair, block], own_grads, from_core)
-    far = [move_ways(sums[s - 1], "z", -s) for s in (4, 3, 2, 1)]
-    mine, others = call(last_sums_kernel, [block] * 2, keep, *far[::-1])
+    four, two, one, three, keep = call(
+        sums_kernel, [block, pair_shape, pair_shape, pair_shape, block], own_grads, from_core
+    )
+    four_in, two_in, one_in = (move_ways(v, "z", -s) for v, s in ((four, 1), (two, 2), (one, 1)))
+    (three,) = call(relay_kernel, [pair_shape], three, four_in)
+    three_in = move_ways(three, "z", -3)
+    mine, others = call(last_sums_kernel, [block] * 2, three_in, two_in, one_in, keep)
     new_rows, new_accum = call(
-        update_kernel, [block, ((1, RB), F32)], mine, move(others, "core", 1), own, row_accum
+        update_kernel, [block, ((1, RB), F32)], mine, move(others, "core", 1), pair, row_accum
     )
     return (crossed, new_rows[None], new_accum)
 

time: 94.1 us -> 91.6 us (0.973)
  the two profiles are of different devices: /device:TPU:33 before, /device:TPU:1 now
where the time goes in v4:
time: 91.6 us; the launch traced here: 91.4 us
  blocking collectives  41 us (45%)
  starting transfers between devices  22.1 us (24%)
  waiting for transfers between devices  13 us (14%)
  Pallas kernels  12.7 us (14%)
  other arithmetic  0.95 us (1%)
    all_to_all x2, blocking collectives, exchange(): lax.all_to_all(parts, ('hst', 'y'), split_axis=0, concat_axis=0, tiled=True)  41 us
    ppermute x8, starting transfers between devices, move_ways(): return lax.ppermute(array, (axis, 'core'), pairs)  12.6 us
    ppermute x8, waiting for transfers between devices, move_ways(): return lax.ppermute(array, (axis, 'core'), pairs)  11.1 us
    ppermute x4, starting transfers between devices, move(): return lax.ppermute(array, axis, [(i, (i + step) % n) for i in range(n)])  9.54 us
    pallas_call x11, Pallas kernels, call(): pl.pallas_call(kernel, in_specs=[vm] * len(operands), out_specs=[vm] * le...  7.45 us
    pallas_call x4, Pallas kernels, counts_of(): pl.pallas_call(lambda s, v, *rest: counts_kernel(s, v, rest[-1]), grid=(1...  5.24 us
    ppermute x4, waiting for transfers between devices, move(): return lax.ppermute(array, axis, [(i, (i + step) % n) for i in range(n)])  1.88 us
  transfers between devices with their start and end apart: 12, of which 10 were waited for; matrix products, arithmetic and copies ran while one was open for 1% of the time, Pallas kernels for 9%

profile of v4, /device:TPU:1, one launch (start us, length us, event | category | flops | bytes accessed | tf_op | source)
XLA Modules:
  0.0 91.4 jit_solution(16063187306469804753)
XLA Ops:
  0.6 3.3 %collective-permute-start = (f32[128,128]{1,0:T(8,128)}, f32[128,128]{1,0:T(8,128)S(1)}, u32[]{:S(2)}, u32[]{:S(2)}) collective-permute-start(f32[128,128]{1,0:T(8,128)} %bitcast.102), channel_id=1, source_target_pairs={{0,1},{1,0},{2,3},{3,2},{4,5},{5,4},{6,7},{7,6},{8,9},{9,8},{10,11... | collective-permute-start | bytes 196616 | tf_op jit(solution)/shard_map/ppermute | solution.py:24
  5.1 4.8 %collective-permute-start.3 = (f32[256,128]{1,0:T(8,128)S(1)}, f32[256,128]{1,0:T(8,128)S(1)}, u32[]{:S(2)}, u32[]{:S(2)}) collective-permute-start(f32[256,128]{1,0:T(8,128)S(1)} %shard_map.104.pair.rows), channel_id=1, source_target_pairs={{0,24},{1,41},{8,32},{9,49},{16,40},{17,57},{24,48},{25,1},{32,56}... | collective-permute-start | bytes 393224 | tf_op jit(solution)/shard_map/ppermute | solution.py:32
  10.6 1.0 %fusion.4 = (f32[4,4,8,128]{3,2,1,0:T(8,128)S(1)}, s32[4,4,8,128]{3,2,1,0:T(8,128)S(1)}) fusion(s32[4,8,4,2,8,128]{5,4,3,2,1,0:T(8,128)} %bitcast.105, s32[]{:T(128)S(6)} %select_n.26, s32[]{:T(128)S(6)} %select_n.27, s32[4,8,4,2,8,128]{5,4,3,2,1,0:T(8,128)} %bitcast.106, s32[]{:T(128)S(6)} %axis_index.35, s32[]{:T(128)S(6)} %sub.23, s32[]{:T(128)S(6)} %axis_index.33, ...), kind=kLoop, calls=%fused_computation.7 | loop fusion | flops 557056 | bytes 262168 | tf_op jit(solution)/shard_map/convert_element_type | solution.py:70
  11.6 1.3 %shard_map.106.refs_1_.c1 = bf16[2048,512]{1,0:T(8,128)(2,1)S(1)} custom-call(s32[4,4,8,128]{3,2,1,0:T(8,128)S(1)} %get-tuple-element.30.s, f32[4,4,8,128]{3,2,1,0:T(8,128)S(1)} %get-tuple-element.29.v), custom_call_target="tpu_custom_call" | custom-call | bytes 1024 | tf_op jit(solution)/shard_map/pallas_call | solution.py:97
  12.9 1.3 %shard_map.105.refs_0_.c0 = bf16[2048,512]{1,0:T(8,128)(2,1)S(1)} custom-call(s32[4,4,8,128]{3,2,1,0:T(8,128)S(1)} %get-tuple-element.30.s, f32[4,4,8,128]{3,2,1,0:T(8,128)S(1)} %get-tuple-element.29.v), custom_call_target="tpu_custom_call" | custom-call | bytes 1024 | tf_op jit(solution)/shard_map/pallas_call | solution.py:97
  14.2 1.4 %collective-permute-done.3.three = f32[256,128]{1,0:T(8,128)S(1)} collective-permute-done((f32[256,128]{1,0:T(8,128)S(1)}, f32[256,128]{1,0:T(8,128)S(1)}, u32[]{:S(2)}, u32[]{:S(2)}) %collective-permute-start.3) | collective-permute-done | bytes 131104 | tf_op jit(solution)/shard_map/ppermute | solution.py:32
  16.0 1.3 %shard_map.109.refs_3_.c3 = bf16[2048,512]{1,0:T(8,128)(2,1)S(1)} custom-call(s32[4,4,8,128]{3,2,1,0:T(8,128)S(1)} %get-tuple-element.30.s, f32[4,4,8,128]{3,2,1,0:T(8,128)S(1)} %get-tuple-element.29.v, f32[128,128]{1,0:T(8,128)S(1)} %shard_map.107.rest_0_), custom_call_target="tpu_custom_call" | custom-call | bytes 1024 | tf_op jit(solution)/shard_map/pallas_call | solution.py:97
  17.3 1.3 %shard_map.108.refs_2_.c2 = bf16[2048,512]{1,0:T(8,128)(2,1)S(1)} custom-call(s32[4,4,8,128]{3,2,1,0:T(8,128)S(1)} %get-tuple-element.30.s, f32[4,4,8,128]{3,2,1,0:T(8,128)S(1)} %get-tuple-element.29.v, f32[128,128]{1,0:T(8,128)S(1)} %shard_map.107.rest_0_), custom_call_target="tpu_custom_call" | custom-call | bytes 1024 | tf_op jit(solution)/shard_map/pallas_call | solution.py:97
  19.7 2.6 %collective-permute-start.5 = (f32[1024,128]{1,0:T(8,128)S(1)}, f32[1024,128]{1,0:T(8,128)S(1)}, u32[]{:S(2)}, u32[]{:S(2)}) collective-permute-start(f32[1024,128]{1,0:T(8,128)S(1)} %shard_map.110.rows), channel_id=1, source_target_pairs={{0,1},{1,0},{2,3},{3,2},{4,5},{5,4},{6,7},{7,6},{8,9},{9,8},{10,11... | collective-permute-start | bytes 1572872 | tf_op jit(solution)/shard_map/ppermute | solution.py:24
  22.3 1.3 %shard_map.111.base = f32[4,128,512]{2,1,0:T(8,128)S(1)} custom-call(f32[1024,128]{1,0:T(8,128)S(1)} %shard_map.110.rows, bf16[2048,512]{1,0:T(8,128)(2,1)S(1)} %shard_map.105.refs_0_.c0, bf16[2048,512]{1,0:T(8,128)(2,1)S(1)} %shard_map.106.refs_1_.c1, bf16[2048,512]{1,0:T(8,128)(2,1)S(1)} %shard_map.108.refs_2_.c2, bf16[2048,512]{1,0:T(8,128)(2,1)S(1)} %shard_map.109.refs_3_.c3), custom_call_target="tpu_custom_call" | custom-call | bytes 1024 | tf_op jit(solution)/shard_map/pallas_call | solution.py:37
  23.8 1.4 %shard_map.112 = f32[16,128,128]{2,1,0:T(8,128)S(1)} custom-call(f32[1024,128]{1,0:T(8,128)S(1)} %collective-permute-done.5.rows, f32[4,128,512]{2,1,0:T(8,128)S(1)} %shard_map.111.base, bf16[2048,512]{1,0:T(8,128)(2,1)S(1)} %shard_map.105.refs_0_.c0, bf16[2048,512]{1,0:T(8,128)(2,1)S(1)} %shard_map.106.refs_1_.c1, ...), custom_call_target="tpu_custom_call" | custom-call | bytes 1024 | tf_op jit(solution)/shard_map/pallas_call | solution.py:37
  25.3 22.7 %all_to_all.10.parts = f32[16,128,128]{2,1,0:T(8,128)S(1)} all-to-all(f32[16,128,128]{2,1,0:T(8,128)S(1)} %shard_map.112), channel_id=1, replica_groups=mesh['hst'=4,'z'=8,'y'=4,'core'=2] {'hst','y'}, dimensions={0} | all-to-all | bytes 2097152 | tf_op jit(solution)/shard_map/all_to_all | solution.py:251
  48.0 1.3 %shard_map.113 = (bf16[128,512]{1,0:T(8,128)(2,1)}, f32[16,128,128]{2,1,0:T(8,128)S(1)}) custom-call(f32[16,128,128]{2,1,0:T(8,128)S(1)} %all_to_all.10.parts, bf16[512,512]{1,0:T(8,128)(2,1)S(1)} %copy-done, bf16[512,512]{1,0:T(8,128)(2,1)S(1)} %copy-done.1, f32[1,512]{1,0:T(1,128)S(1)} %bitcast.104, bf16[128,512]{1,0:T(8,128)(2,1)S(1)} %copy-done.2), custom_call_target="tpu_custom_call" | custom-call | bytes 1024 | tf_op jit(solution)/shard_map/pallas_call | solution.py:37
  49.2 18.3 %all_to_all.11 = f32[16,128,128]{2,1,0:T(8,128)S(1)} all-to-all(f32[16,128,128]{2,1,0:T(8,128)S(1)} %get-tuple-element.17), channel_id=1, replica_groups=mesh['hst'=4,'z'=8,'y'=4,'core'=2] {'hst','y'}, dimensions={0} | all-to-all | bytes 2097152 | tf_op jit(solution)/shard_map/all_to_all | solution.py:251
  67.6 1.3 %shard_map.114 = (f32[1024,128]{1,0:T(8,128)S(1)}, bf16[4,512,256]{2,1,0:T(8,128)(2,1)S(1)}) custom-call(f32[2048,128]{1,0:T(8,128)S(1)} %bitcast.101, bf16[2048,512]{1,0:T(8,128)(2,1)S(1)} %shard_map.105.refs_0_.c0, bf16[2048,512]{1,0:T(8,128)(2,1)S(1)} %shard_map.106.refs_1_.c1, bf16[2048,512]{1,0:T(8,128)(2,1)S(1)} %shard_map.108.refs_2_.c2, ...), custom_call_target="tpu_custom_call" | custom-call | bytes 1024 | tf_op jit(solution)/shard_map/pallas_call | solution.py:37
  68.8 3.3 %collective-permute-start.6 = (f32[1024,128]{1,0:T(8,128)S(1)}, f32[1024,128]{1,0:T(8,128)S(1)}, u32[]{:S(2)}, u32[]{:S(2)}) collective-permute-start(f32[1024,128]{1,0:T(8,128)S(1)} %get-tuple-element.19), channel_id=1, source_target_pairs={{0,1},{1,0},{2,3},{3,2},{4,5},{5,4},{6,7},{7,6},{8,9},{9,8},{10,11... | collective-permute-start | bytes 1572872 | tf_op jit(solution)/shard_map/ppermute | solution.py:24
  72.2 1.2 %shard_map.115.a = f32[1024,128]{1,0:T(8,128)S(1)} custom-call(bf16[4,512,256]{2,1,0:T(8,128)(2,1)S(1)} %get-tuple-element.18.terms, bf16[2048,512]{1,0:T(8,128)(2,1)S(1)} %shard_map.105.refs_0_.c0, bf16[2048,512]{1,0:T(8,128)(2,1)S(1)} %shard_map.106.refs_1_.c1, bf16[2048,512]{1,0:T(8,128)(2,1)S(1)} %shard_map.108.refs_2_.c2, ...), custom_call_target="tpu_custom_call" | custom-call | bytes 1024 | tf_op jit(solution)/shard_map/pallas_call | solution.py:37
  74.1 2.5 %collective-permute-start.9 = (f32[256,128]{1,0:T(8,128)S(1)}, f32[256,128]{1,0:T(8,128)S(1)}, u32[]{:S(2)}, u32[]{:S(2)}) collective-permute-start(f32[256,128]{1,0:T(8,128)S(1)} %get-tuple-element.22), channel_id=1, source_target_pairs={{0,48},{1,17},{8,56},{9,25},{16,0},{17,33},{24,8},{25,41},{32,16},... | collective-permute-start | bytes 393224 | tf_op jit(solution)/shard_map/ppermute | solution.py:32
  76.6 2.5 %collective-permute-start.10 = (f32[256,128]{1,0:T(8,128)S(1)}, f32[256,128]{1,0:T(8,128)S(1)}, u32[]{:S(2)}, u32[]{:S(2)}) collective-permute-start(f32[256,128]{1,0:T(8,128)S(1)} %get-tuple-element.23), channel_id=1, source_target_pairs={{0,56},{1,9},{8,0},{9,17},{16,8},{17,25},{24,16},{25,33},{32,24},{... | collective-permute-start | bytes 393224 | tf_op jit(solution)/shard_map/ppermute | solution.py:32
  79.2 1.2 %collective-permute-start.8 = (f32[256,128]{1,0:T(8,128)S(1)}, f32[256,128]{1,0:T(8,128)S(1)}, u32[]{:S(2)}, u32[]{:S(2)}) collective-permute-start(f32[256,128]{1,0:T(8,128)S(1)} %shard_map.117), channel_id=1, source_target_pairs={{0,40},{1,25},{8,48},{9,33},{16,56},{17,41},{24,0},{25,49},{32,8},... | collective-permute-start | bytes 393224 | tf_op jit(solution)/shard_map/ppermute | solution.py:32
  80.4 1.0 %collective-permute-done.9.two = f32[256,128]{1,0:T(8,128)S(1)} collective-permute-done((f32[256,128]{1,0:T(8,128)S(1)}, f32[256,128]{1,0:T(8,128)S(1)}, u32[]{:S(2)}, u32[]{:S(2)}) %collective-permute-start.9) | collective-permute-done | bytes 131104 | tf_op jit(solution)/shard_map/ppermute | solution.py:32
  81.3 1.2 %collective-permute-done.10.one = f32[256,128]{1,0:T(8,128)S(1)} collective-permute-done((f32[256,128]{1,0:T(8,128)S(1)}, f32[256,128]{1,0:T(8,128)S(1)}, u32[]{:S(2)}, u32[]{:S(2)}) %collective-permute-start.10) | collective-permute-done | bytes 131104 | tf_op jit(solution)/shard_map/ppermute | solution.py:32
  82.5 6.6 %collective-permute-done.8.three = f32[256,128]{1,0:T(8,128)S(1)} collective-permute-done((f32[256,128]{1,0:T(8,128)S(1)}, f32[256,128]{1,0:T(8,128)S(1)}, u32[]{:S(2)}, u32[]{:S(2)}) %collective-permute-start.8) | collective-permute-done | bytes 131104 | tf_op jit(solution)/shard_map/ppermute | solution.py:32
  89.4 1.1 %collective-permute-done.11.b = f32[128,128]{1,0:T(8,128)S(1)} collective-permute-done((f32[128,128]{1,0:T(8,128)S(1)}, f32[128,128]{1,0:T(8,128)S(1)}, u32[]{:S(2)}, u32[]{:S(2)}) %collective-permute-start.11) | collective-permute-done | bytes 65568 | tf_op jit(solution)/shard_map/ppermute | solution.py:24
  (32 shorter events, 5.4 us)
Async XLA Ops:
  0.6 4.4 %collective-permute-start = (f32[128,128]{1,0:T(8,128)}, f32[128,128]{1,0:T(8,128)S(1)}, u32[]{:S(2)}, u32[]{:S(2)}) collective-permute-start(f32[128,128]{1,0:T(8,128)} %bitcast.102), channel_id=1, source_target_pairs={{0,1},{1,0},{2,3},{3,2},{4,5},{5,4},{6,7},{7,6},{8,9},{9,8},{10,11... | collective-permute-start | bytes 196616 | tf_op jit(solution)/shard_map/ppermute | solution.py:24
  4.0 0.8 copy-start.3
  5.1 10.5 %collective-permute-start.3 = (f32[256,128]{1,0:T(8,128)S(1)}, f32[256,128]{1,0:T(8,128)S(1)}, u32[]{:S(2)}, u32[]{:S(2)}) collective-permute-start(f32[256,128]{1,0:T(8,128)S(1)} %shard_map.104.pair.rows), channel_id=1, source_target_pairs={{0,24},{1,41},{8,32},{9,49},{16,40},{17,57},{24,48},{25,1},{32,56}... | collective-permute-start | bytes 393224 | tf_op jit(solution)/shard_map/ppermute | solution.py:32
  9.9 8.8 %collective-permute-start.2 = (f32[256,128]{1,0:T(8,128)S(1)}, f32[256,128]{1,0:T(8,128)S(1)}, u32[]{:S(2)}, u32[]{:S(2)}) collective-permute-start(f32[256,128]{1,0:T(8,128)S(1)} %shard_map.104.pair.rows), channel_id=1, source_target_pairs={{0,16},{1,49},{8,24},{9,57},{16,32},{17,1},{24,40},{25,9},{32,48},... | collective-permute-start | bytes 393224 | tf_op jit(solution)/shard_map/ppermute | solution.py:32
  10.2 8.7 %collective-permute-start.1 = (f32[256,128]{1,0:T(8,128)S(1)}, f32[256,128]{1,0:T(8,128)S(1)}, u32[]{:S(2)}, u32[]{:S(2)}) collective-permute-start(f32[256,128]{1,0:T(8,128)S(1)} %shard_map.104.pair.rows), channel_id=1, source_target_pairs={{0,8},{1,57},{8,16},{9,1},{16,24},{17,9},{24,32},{25,17},{32,40},{... | collective-permute-start | bytes 393224 | tf_op jit(solution)/shard_map/ppermute | solution.py:32
  15.6 4.1 %collective-permute-start.4 = (f32[128,128]{1,0:T(8,128)S(1)}, f32[128,128]{1,0:T(8,128)S(1)}, u32[]{:S(2)}, u32[]{:S(2)}) collective-permute-start(f32[128,128]{1,0:T(8,128)S(1)} %shard_map.107.rest_0_), channel_id=1, source_target_pairs={{0,8},{1,57},{8,16},{9,1},{16,24},{17,9},{24,32},{25,17},{32,40},{... | collective-permute-start | bytes 196616 | tf_op jit(solution)/shard_map/ppermute | solution.py:32
  19.7 4.2 %collective-permute-start.5 = (f32[1024,128]{1,0:T(8,128)S(1)}, f32[1024,128]{1,0:T(8,128)S(1)}, u32[]{:S(2)}, u32[]{:S(2)}) collective-permute-start(f32[1024,128]{1,0:T(8,128)S(1)} %shard_map.110.rows), channel_id=1, source_target_pairs={{0,1},{1,0},{2,3},{3,2},{4,5},{5,4},{6,7},{7,6},{8,9},{9,8},{10,11... | collective-permute-start | bytes 1572872 | tf_op jit(solution)/shard_map/ppermute | solution.py:24
  25.2 22.7 %copy-start = (bf16[512,512]{1,0:T(8,128)(2,1)S(1)}, bf16[512,512]{1,0:T(8,128)(2,1)}, u32[]{:S(2)}) copy-start(bf16[512,512]{1,0:T(8,128)(2,1)} %u.1) | copy-start | bytes 1572868
  25.3 22.7 %copy-start.1 = (bf16[512,512]{1,0:T(8,128)(2,1)S(1)}, bf16[512,512]{1,0:T(8,128)(2,1)}, u32[]{:S(2)}) copy-start(bf16[512,512]{1,0:T(8,128)(2,1)} %v.1) | copy-start | bytes 1572868
  25.3 22.7 %copy-start.2 = (bf16[128,512]{1,0:T(8,128)(2,1)S(1)}, bf16[128,512]{1,0:T(8,128)(2,1)}, u32[]{:S(2)}) copy-start(bf16[128,512]{1,0:T(8,128)(2,1)} %cot.1) | copy-start | bytes 393220
  25.3 22.7 %copy-start.4 = (f32[512]{0:T(512)S(1)}, f32[512]{0:T(512)}, u32[]{:S(2)}) copy-start(f32[512]{0:T(512)} %param.14) | copy-start | bytes 6148
  68.8 4.9 %collective-permute-start.6 = (f32[1024,128]{1,0:T(8,128)S(1)}, f32[1024,128]{1,0:T(8,128)S(1)}, u32[]{:S(2)}, u32[]{:S(2)}) collective-permute-start(f32[1024,128]{1,0:T(8,128)S(1)} %get-tuple-element.19), channel_id=1, source_target_pairs={{0,1},{1,0},{2,3},{3,2},{4,5},{5,4},{6,7},{7,6},{8,9},{9,8},{10,11... | collective-permute-start | bytes 1572872 | tf_op jit(solution)/shard_map/ppermute | solution.py:24
  72.2 18.3 %copy-start.5 = (f32[1,128]{1,0:T(1,128)S(1)}, f32[1,128]{1,0:T(1,128)}, u32[]{:S(2)}) copy-start(f32[1,128]{1,0:T(1,128)} %accum.1) | copy-start | bytes 1540
  73.8 5.4 %collective-permute-start.7 = (f32[128,128]{1,0:T(8,128)S(1)}, f32[128,128]{1,0:T(8,128)S(1)}, u32[]{:S(2)}, u32[]{:S(2)}) collective-permute-start(f32[128,128]{1,0:T(8,128)S(1)} %get-tuple-element.21), channel_id=1, source_target_pairs={{0,56},{1,9},{8,0},{9,17},{16,8},{17,25},{24,16},{25,33},{32,24},{... | collective-permute-start | bytes 196616 | tf_op jit(solution)/shard_map/ppermute | solution.py:32
  74.1 7.2 %collective-permute-start.9 = (f32[256,128]{1,0:T(8,128)S(1)}, f32[256,128]{1,0:T(8,128)S(1)}, u32[]{:S(2)}, u32[]{:S(2)}) collective-permute-start(f32[256,128]{1,0:T(8,128)S(1)} %get-tuple-element.22), channel_id=1, source_target_pairs={{0,48},{1,17},{8,56},{9,25},{16,0},{17,33},{24,8},{25,41},{32,16},... | collective-permute-start | bytes 393224 | tf_op jit(solution)/shard_map/ppermute | solution.py:32
  76.6 5.9 %collective-permute-start.10 = (f32[256,128]{1,0:T(8,128)S(1)}, f32[256,128]{1,0:T(8,128)S(1)}, u32[]{:S(2)}, u32[]{:S(2)}) collective-permute-start(f32[256,128]{1,0:T(8,128)S(1)} %get-tuple-element.23), channel_id=1, source_target_pairs={{0,56},{1,9},{8,0},{9,17},{16,8},{17,25},{24,16},{25,33},{32,24},{... | collective-permute-start | bytes 393224 | tf_op jit(solution)/shard_map/ppermute | solution.py:32
  79.2 9.9 %collective-permute-start.8 = (f32[256,128]{1,0:T(8,128)S(1)}, f32[256,128]{1,0:T(8,128)S(1)}, u32[]{:S(2)}, u32[]{:S(2)}) collective-permute-start(f32[256,128]{1,0:T(8,128)S(1)} %shard_map.117), channel_id=1, source_target_pairs={{0,40},{1,25},{8,48},{9,33},{16,56},{17,41},{24,0},{25,49},{32,8},... | collective-permute-start | bytes 393224 | tf_op jit(solution)/shard_map/ppermute | solution.py:32
  89.1 1.3 %collective-permute-start.11 = (f32[128,128]{1,0:T(8,128)S(1)}, f32[128,128]{1,0:T(8,128)S(1)}, u32[]{:S(2)}, u32[]{:S(2)}) collective-permute-start(f32[128,128]{1,0:T(8,128)S(1)} %get-tuple-element.26), channel_id=1, source_target_pairs={{0,1},{1,0},{2,3},{3,2},{4,5},{5,4},{6,7},{7,6},{8,9},{9,8},{10,11... | collective-permute-start | bytes 196616 | tf_op jit(solution)/shard_map/ppermute | solution.py:24

commit v5 on v4

--- a/solution.py
+++ b/solution.py
@@ -13,6 +13,7 @@
 SIZES = {"hst": NX, "z": NZ, "y": NY, "core": NC}
 HALF_ROWS = NZ * RB
 RADIX = 17
+FLIP = 10
 SAMPLES_Y = NX * SB
 F32, BF16 = jnp.float32, jnp.bfloat16
 VMEM = pltpu.CompilerParams(vmem_limit_bytes=40 << 20)
@@ -42,6 +43,21 @@
         compiler_params=VMEM,
         cost_estimate=SMALL,
     )(*operands)
+
+
+def own_flip():
+    return lax.axis_index("core").astype(jnp.int32) * FLIP
+
+
+def exchange(parts):
+    groups = []
+    for z in range(NZ):
+        for c in range(NC):
+            places = [place ^ (FLIP * c) for place in range(NX * NY)]
+            groups.append([((p // NY * NZ + z) * NY + p % NY) * NC + c for p in places])
+    return lax.all_to_all(
+        parts, ("hst", "z", "y", "core"), split_axis=0, concat_axis=0, tiled=True, axis_index_groups=groups
+    )
 
 
 def split_terms(value):
@@ -156,15 +172,17 @@
 
 
 def pool_other_kernel(rows, base, c0, c1, c2, c3, out):
+    flip = own_flip()
     terms = turned_terms(rows[...])
     for x, c in enumerate((c0, c1, c2, c3)):
         total = base[x] + pool_part(terms, c[HALF_ROWS:])
         for y in range(NY):
-            out[x * NY + y] = total[:, y * SB : (y + 1) * SB].T
+            out[(x * NY + y) ^ flip] = total[:, y * SB : (y + 1) * SB].T
 
 
 def cross_kernel(parts, u, v, bias, cot, crossed, out):
-    x = [sum(parts[t * NY + y] for y in range(1, NY)) + parts[t * NY] for t in range(NX)]
+    flip = own_flip()
+    x = [sum(parts[(t * NY + y) ^ flip] for y in range(1, NY)) + parts[(t * NY) ^ flip] for t in range(NX)]
     base_x = jnp.concatenate(x, axis=1)
     low = jnp.dot(base_x.astype(BF16), u[...], preferred_element_type=F32).astype(BF16)
     scale = jnp.dot(low, v[...], preferred_element_type=F32) + bias[...]
@@ -178,7 +196,7 @@
     )
     for t in range(NX):
         for y in range(NY):
-            out[t * NY + y] = grad_x[:, t * E : (t + 1) * E]
+            out[(t * NY + y) ^ flip] = grad_x[:, t * E : (t + 1) * E]
 
 
 def rows_grads(rows, terms, counts):
@@ -190,8 +208,10 @@
 
 
 def other_grads_kernel(g, c0, c1, c2, c3, out, terms):
+    flip = own_flip()
     for x in range(NX):
-        terms[x] = split_terms(g[x * SAMPLES_Y : (x + 1) * SAMPLES_Y])
+        for y in range(NY):
+            terms[x, y * SB : (y + 1) * SB] = split_terms(g[(x * NY + y) ^ flip])
     out[...] = rows_grads(slice(HALF_ROWS, NC * HALF_ROWS), terms, (c0, c1, c2, c3))
 
 
@@ -247,9 +267,6 @@
     blocks = ((NX * NY, SB, E), F32)
     (bags,) = call(pool_other_kernel, [blocks], other_rows, bags, *counts)
 
-    def exchange(parts):
-        return lax.all_to_all(parts, ("hst", "y"), split_axis=0, concat_axis=0, tiled=True)
-
     crossed, bag_grads = call(
         cross_kernel,
         [(cotangent.shape, BF16), blocks],
@@ -259,10 +276,12 @@
         cross_bias.reshape(1, -1),
         cotangent,
     )
-    bag_grads = exchange(bag_grads).reshape(NX * NY * SB, E)
+    bag_grads = exchange(bag_grads)
     block, pair_shape, half = (((n * RB, E), F32) for n in (1, 2, 8))
     terms_shape = ((NX, SAMPLES_Y, 2 * E), BF16)
-    other_grads, terms = call(other_grads_kernel, [half, terms_shape], bag_grads, *counts)
+    other_grads, terms = call(
+        other_grads_kernel, [half, terms_shape], bag_grads, *counts
+    )
     from_core = move(other_grads, "core", 1)
     (own_grads,) = call(own_grads_kernel, [half], terms, *counts)
     four, two, one, three, keep = call(

time: 91.6 us -> 88.3 us (0.964)
  blocking collectives: 41 us -> 39.1 us
  starting transfers between devices: 22.1 us -> 20.6 us
    all_to_all x2, blocking collectives: 41 us -> 39.1 us  [exchange(): lax.all_to_all(parts, ('hst', 'z', 'y', 'core'), split_axis=0, concat_axi...]
    ppermute x4, starting transfers between devices: 9.54 us -> 8.05 us  [move(): return lax.ppermute(array, axis, [(i, (i + step) % n) for i in range(n)])]
where the time goes in v5:
time: 88.3 us; the launch traced here: 88 us
  blocking collectives  39.1 us (44%)
  starting transfers between devices  20.6 us (23%)
  waiting for transfers between devices  12.9 us (15%)
  Pallas kernels  12.7 us (14%)
  other arithmetic  0.95 us (1%)
    all_to_all x2, blocking collectives, exchange(): lax.all_to_all(parts, ('hst', 'z', 'y', 'core'), split_axis=0, concat_axi...  39.1 us
    ppermute x8, starting transfers between devices, move_ways(): return lax.ppermute(array, (axis, 'core'), pairs)  12.6 us
    ppermute x8, waiting for transfers between devices, move_ways(): return lax.ppermute(array, (axis, 'core'), pairs)  11.1 us
    ppermute x4, starting transfers between devices, move(): return lax.ppermute(array, axis, [(i, (i + step) % n) for i in range(n)])  8.05 us
    pallas_call x11, Pallas kernels, call(): pl.pallas_call(kernel, in_specs=[vm] * len(operands), out_specs=[vm] * le...  7.46 us
    pallas_call x4, Pallas kernels, counts_of(): pl.pallas_call(lambda s, v, *rest: counts_kernel(s, v, rest[-1]), grid=(1...  5.24 us
    ppermute x4, waiting for transfers between devices, move(): return lax.ppermute(array, axis, [(i, (i + step) % n) for i in range(n)])  1.87 us
  transfers between devices with their start and end apart: 12, of which 10 were waited for; matrix products, arithmetic and copies ran while one was open for 1% of the time, Pallas kernels for 9%

profile of v5, /device:TPU:1, one launch (start us, length us, event | category | flops | bytes accessed | tf_op | source)
XLA Modules:
  0.0 88.0 jit_solution(3383686455878226938)
XLA Ops:
  0.6 3.3 %collective-permute-start = (f32[128,128]{1,0:T(8,128)}, f32[128,128]{1,0:T(8,128)S(1)}, u32[]{:S(2)}, u32[]{:S(2)}) collective-permute-start(f32[128,128]{1,0:T(8,128)} %bitcast.100), channel_id=1, source_target_pairs={{0,1},{1,0},{2,3},{3,2},{4,5},{5,4},{6,7},{7,6},{8,9},{9,8},{10,11... | collective-permute-start | bytes 196616 | tf_op jit(solution)/shard_map/ppermute | solution.py:25
  5.1 4.8 %collective-permute-start.3 = (f32[256,128]{1,0:T(8,128)S(1)}, f32[256,128]{1,0:T(8,128)S(1)}, u32[]{:S(2)}, u32[]{:S(2)}) collective-permute-start(f32[256,128]{1,0:T(8,128)S(1)} %shard_map.104.pair.rows), channel_id=1, source_target_pairs={{0,24},{1,41},{8,32},{9,49},{16,40},{17,57},{24,48},{25,1},{32,56}... | collective-permute-start | bytes 393224 | tf_op jit(solution)/shard_map/ppermute | solution.py:33
  10.6 1.0 %fusion.4 = (f32[4,4,8,128]{3,2,1,0:T(8,128)S(1)}, s32[4,4,8,128]{3,2,1,0:T(8,128)S(1)}) fusion(s32[4,8,4,2,8,128]{5,4,3,2,1,0:T(8,128)} %bitcast.103, s32[]{:T(128)S(6)} %select_n.26, s32[]{:T(128)S(6)} %select_n.27, s32[4,8,4,2,8,128]{5,4,3,2,1,0:T(8,128)} %bitcast.104, s32[]{:T(128)S(6)} %axis_index.35, s32[]{:T(128)S(6)} %sub.23, s32[]{:T(128)S(6)} %axis_index.33, ...), kind=kLoop, calls=%fused_computation.7 | loop fusion | flops 557056 | bytes 262168 | tf_op jit(solution)/shard_map/convert_element_type | solution.py:86
  11.6 1.3 %shard_map.106.refs_1_.c1 = bf16[2048,512]{1,0:T(8,128)(2,1)S(1)} custom-call(s32[4,4,8,128]{3,2,1,0:T(8,128)S(1)} %get-tuple-element.30.s, f32[4,4,8,128]{3,2,1,0:T(8,128)S(1)} %get-tuple-element.29.v), custom_call_target="tpu_custom_call" | custom-call | bytes 1024 | tf_op jit(solution)/shard_map/pallas_call | solution.py:113
  12.9 1.3 %shard_map.105.refs_0_.c0 = bf16[2048,512]{1,0:T(8,128)(2,1)S(1)} custom-call(s32[4,4,8,128]{3,2,1,0:T(8,128)S(1)} %get-tuple-element.30.s, f32[4,4,8,128]{3,2,1,0:T(8,128)S(1)} %get-tuple-element.29.v), custom_call_target="tpu_custom_call" | custom-call | bytes 1024 | tf_op jit(solution)/shard_map/pallas_call | solution.py:113
  14.2 1.4 %collective-permute-done.3.three = f32[256,128]{1,0:T(8,128)S(1)} collective-permute-done((f32[256,128]{1,0:T(8,128)S(1)}, f32[256,128]{1,0:T(8,128)S(1)}, u32[]{:S(2)}, u32[]{:S(2)}) %collective-permute-start.3) | collective-permute-done | bytes 131104 | tf_op jit(solution)/shard_map/ppermute | solution.py:33
  16.0 1.3 %shard_map.109.refs_3_.c3 = bf16[2048,512]{1,0:T(8,128)(2,1)S(1)} custom-call(s32[4,4,8,128]{3,2,1,0:T(8,128)S(1)} %get-tuple-element.30.s, f32[4,4,8,128]{3,2,1,0:T(8,128)S(1)} %get-tuple-element.29.v, f32[128,128]{1,0:T(8,128)S(1)} %shard_map.107.rest_0_), custom_call_target="tpu_custom_call" | custom-call | bytes 1024 | tf_op jit(solution)/shard_map/pallas_call | solution.py:113
  17.3 1.3 %shard_map.108.refs_2_.c2 = bf16[2048,512]{1,0:T(8,128)(2,1)S(1)} custom-call(s32[4,4,8,128]{3,2,1,0:T(8,128)S(1)} %get-tuple-element.30.s, f32[4,4,8,128]{3,2,1,0:T(8,128)S(1)} %get-tuple-element.29.v, f32[128,128]{1,0:T(8,128)S(1)} %shard_map.107.rest_0_), custom_call_target="tpu_custom_call" | custom-call | bytes 1024 | tf_op jit(solution)/shard_map/pallas_call | solution.py:113
  19.7 2.6 %collective-permute-start.5 = (f32[1024,128]{1,0:T(8,128)S(1)}, f32[1024,128]{1,0:T(8,128)S(1)}, u32[]{:S(2)}, u32[]{:S(2)}) collective-permute-start(f32[1024,128]{1,0:T(8,128)S(1)} %shard_map.110.rows), channel_id=1, source_target_pairs={{0,1},{1,0},{2,3},{3,2},{4,5},{5,4},{6,7},{7,6},{8,9},{9,8},{10,11... | collective-permute-start | bytes 1572872 | tf_op jit(solution)/shard_map/ppermute | solution.py:25
  22.3 1.3 %shard_map.111.base = f32[4,128,512]{2,1,0:T(8,128)S(1)} custom-call(f32[1024,128]{1,0:T(8,128)S(1)} %shard_map.110.rows, bf16[2048,512]{1,0:T(8,128)(2,1)S(1)} %shard_map.105.refs_0_.c0, bf16[2048,512]{1,0:T(8,128)(2,1)S(1)} %shard_map.106.refs_1_.c1, bf16[2048,512]{1,0:T(8,128)(2,1)S(1)} %shard_map.108.refs_2_.c2, bf16[2048,512]{1,0:T(8,128)(2,1)S(1)} %shard_map.109.refs_3_.c3), custom_call_target="tpu_custom_call" | custom-call | bytes 1024 | tf_op jit(solution)/shard_map/pallas_call | solution.py:38
  23.8 1.4 %shard_map.112 = f32[16,128,128]{2,1,0:T(8,128)S(1)} custom-call(f32[1024,128]{1,0:T(8,128)S(1)} %collective-permute-done.5.rows, f32[4,128,512]{2,1,0:T(8,128)S(1)} %shard_map.111.base, bf16[2048,512]{1,0:T(8,128)(2,1)S(1)} %shard_map.105.refs_0_.c0, bf16[2048,512]{1,0:T(8,128)(2,1)S(1)} %shard_map.106.refs_1_.c1, ...), custom_call_target="tpu_custom_call" | custom-call | bytes 1024 | tf_op jit(solution)/shard_map/pallas_call | solution.py:38
  25.3 19.4 %all_to_all.10.parts = f32[16,128,128]{2,1,0:T(8,128)S(1)} all-to-all(f32[16,128,128]{2,1,0:T(8,128)S(1)} %shard_map.112), channel_id=1, replica_groups={{0,2,4,6,64,66,68,70,128,130,132,134,192,194,196,198},{133,135,129,131,..., dimensions={0} | all-to-all | bytes 2097152 | tf_op jit(solution)/shard_map/all_to_all | solution.py:58
  44.7 1.3 %shard_map.113 = (bf16[128,512]{1,0:T(8,128)(2,1)}, f32[16,128,128]{2,1,0:T(8,128)S(1)}) custom-call(f32[16,128,128]{2,1,0:T(8,128)S(1)} %all_to_all.10.parts, bf16[512,512]{1,0:T(8,128)(2,1)S(1)} %copy-done, bf16[512,512]{1,0:T(8,128)(2,1)S(1)} %copy-done.1, f32[1,512]{1,0:T(1,128)S(1)} %bitcast.102, bf16[128,512]{1,0:T(8,128)(2,1)S(1)} %copy-done.2), custom_call_target="tpu_custom_call" | custom-call | bytes 1024 | tf_op jit(solution)/shard_map/pallas_call | solution.py:38
  46.0 19.7 %all_to_all.11.g = f32[16,128,128]{2,1,0:T(8,128)S(1)} all-to-all(f32[16,128,128]{2,1,0:T(8,128)S(1)} %get-tuple-element.17), channel_id=1, replica_groups={{0,2,4,6,64,66,68,70,128,130,132,134,192,194,196,198},{133,135,129,131,..., dimensions={0} | all-to-all | bytes 2097152 | tf_op jit(solution)/shard_map/all_to_all | solution.py:58
  65.7 1.3 %shard_map.114 = (f32[1024,128]{1,0:T(8,128)S(1)}, bf16[4,512,256]{2,1,0:T(8,128)(2,1)S(1)}) custom-call(f32[16,128,128]{2,1,0:T(8,128)S(1)} %all_to_all.11.g, bf16[2048,512]{1,0:T(8,128)(2,1)S(1)} %shard_map.105.refs_0_.c0, bf16[2048,512]{1,0:T(8,128)(2,1)S(1)} %shard_map.106.refs_1_.c1, bf16[2048,512]{1,0:T(8,128)(2,1)S(1)} %shard_map.108.refs_2_.c2, ...), custom_call_target="tpu_custom_call" | custom-call | bytes 1024 | tf_op jit(solution)/shard_map/pallas_call | solution.py:38
  67.0 1.8 %collective-permute-start.6 = (f32[1024,128]{1,0:T(8,128)S(1)}, f32[1024,128]{1,0:T(8,128)S(1)}, u32[]{:S(2)}, u32[]{:S(2)}) collective-permute-start(f32[1024,128]{1,0:T(8,128)S(1)} %get-tuple-element.19), channel_id=1, source_target_pairs={{0,1},{1,0},{2,3},{3,2},{4,5},{5,4},{6,7},{7,6},{8,9},{9,8},{10,11... | collective-permute-start | bytes 1572872 | tf_op jit(solution)/shard_map/ppermute | solution.py:25
  68.8 1.2 %shard_map.115.a = f32[1024,128]{1,0:T(8,128)S(1)} custom-call(bf16[4,512,256]{2,1,0:T(8,128)(2,1)S(1)} %get-tuple-element.18.terms, bf16[2048,512]{1,0:T(8,128)(2,1)S(1)} %shard_map.105.refs_0_.c0, bf16[2048,512]{1,0:T(8,128)(2,1)S(1)} %shard_map.106.refs_1_.c1, bf16[2048,512]{1,0:T(8,128)(2,1)S(1)} %shard_map.108.refs_2_.c2, ...), custom_call_target="tpu_custom_call" | custom-call | bytes 1024 | tf_op jit(solution)/shard_map/pallas_call | solution.py:38
  70.8 2.5 %collective-permute-start.9 = (f32[256,128]{1,0:T(8,128)S(1)}, f32[256,128]{1,0:T(8,128)S(1)}, u32[]{:S(2)}, u32[]{:S(2)}) collective-permute-start(f32[256,128]{1,0:T(8,128)S(1)} %get-tuple-element.22), channel_id=1, source_target_pairs={{0,48},{1,17},{8,56},{9,25},{16,0},{17,33},{24,8},{25,41},{32,16},... | collective-permute-start | bytes 393224 | tf_op jit(solution)/shard_map/ppermute | solution.py:33
  73.3 2.5 %collective-permute-start.10 = (f32[256,128]{1,0:T(8,128)S(1)}, f32[256,128]{1,0:T(8,128)S(1)}, u32[]{:S(2)}, u32[]{:S(2)}) collective-permute-start(f32[256,128]{1,0:T(8,128)S(1)} %get-tuple-element.23), channel_id=1, source_target_pairs={{0,56},{1,9},{8,0},{9,17},{16,8},{17,25},{24,16},{25,33},{32,24},{... | collective-permute-start | bytes 393224 | tf_op jit(solution)/shard_map/ppermute | solution.py:33
  75.8 1.2 %collective-permute-start.8 = (f32[256,128]{1,0:T(8,128)S(1)}, f32[256,128]{1,0:T(8,128)S(1)}, u32[]{:S(2)}, u32[]{:S(2)}) collective-permute-start(f32[256,128]{1,0:T(8,128)S(1)} %shard_map.117), channel_id=1, source_target_pairs={{0,40},{1,25},{8,48},{9,33},{16,56},{17,41},{24,0},{25,49},{32,8},... | collective-permute-start | bytes 393224 | tf_op jit(solution)/shard_map/ppermute | solution.py:33
  77.0 1.0 %collective-permute-done.9.two = f32[256,128]{1,0:T(8,128)S(1)} collective-permute-done((f32[256,128]{1,0:T(8,128)S(1)}, f32[256,128]{1,0:T(8,128)S(1)}, u32[]{:S(2)}, u32[]{:S(2)}) %collective-permute-start.9) | collective-permute-done | bytes 131104 | tf_op jit(solution)/shard_map/ppermute | solution.py:33
  78.0 1.2 %collective-permute-done.10.one = f32[256,128]{1,0:T(8,128)S(1)} collective-permute-done((f32[256,128]{1,0:T(8,128)S(1)}, f32[256,128]{1,0:T(8,128)S(1)}, u32[]{:S(2)}, u32[]{:S(2)}) %collective-permute-start.10) | collective-permute-done | bytes 131104 | tf_op jit(solution)/shard_map/ppermute | solution.py:33
  79.2 6.6 %collective-permute-done.8.three = f32[256,128]{1,0:T(8,128)S(1)} collective-permute-done((f32[256,128]{1,0:T(8,128)S(1)}, f32[256,128]{1,0:T(8,128)S(1)}, u32[]{:S(2)}, u32[]{:S(2)}) %collective-permute-start.8) | collective-permute-done | bytes 131104 | tf_op jit(solution)/shard_map/ppermute | solution.py:33
  86.0 1.1 %collective-permute-done.11.b = f32[128,128]{1,0:T(8,128)S(1)} collective-permute-done((f32[128,128]{1,0:T(8,128)S(1)}, f32[128,128]{1,0:T(8,128)S(1)}, u32[]{:S(2)}, u32[]{:S(2)}) %collective-permute-start.11) | collective-permute-done | bytes 65568 | tf_op jit(solution)/shard_map/ppermute | solution.py:25
  (32 shorter events, 5.5 us)
Async XLA Ops:
  0.6 4.4 %collective-permute-start = (f32[128,128]{1,0:T(8,128)}, f32[128,128]{1,0:T(8,128)S(1)}, u32[]{:S(2)}, u32[]{:S(2)}) collective-permute-start(f32[128,128]{1,0:T(8,128)} %bitcast.100), channel_id=1, source_target_pairs={{0,1},{1,0},{2,3},{3,2},{4,5},{5,4},{6,7},{7,6},{8,9},{9,8},{10,11... | collective-permute-start | bytes 196616 | tf_op jit(solution)/shard_map/ppermute | solution.py:25
  4.0 0.8 copy-start.3
  5.1 10.5 %collective-permute-start.3 = (f32[256,128]{1,0:T(8,128)S(1)}, f32[256,128]{1,0:T(8,128)S(1)}, u32[]{:S(2)}, u32[]{:S(2)}) collective-permute-start(f32[256,128]{1,0:T(8,128)S(1)} %shard_map.104.pair.rows), channel_id=1, source_target_pairs={{0,24},{1,41},{8,32},{9,49},{16,40},{17,57},{24,48},{25,1},{32,56}... | collective-permute-start | bytes 393224 | tf_op jit(solution)/shard_map/ppermute | solution.py:33
  9.9 8.8 %collective-permute-start.2 = (f32[256,128]{1,0:T(8,128)S(1)}, f32[256,128]{1,0:T(8,128)S(1)}, u32[]{:S(2)}, u32[]{:S(2)}) collective-permute-start(f32[256,128]{1,0:T(8,128)S(1)} %shard_map.104.pair.rows), channel_id=1, source_target_pairs={{0,16},{1,49},{8,24},{9,57},{16,32},{17,1},{24,40},{25,9},{32,48},... | collective-permute-start | bytes 393224 | tf_op jit(solution)/shard_map/ppermute | solution.py:33
  10.2 8.7 %collective-permute-start.1 = (f32[256,128]{1,0:T(8,128)S(1)}, f32[256,128]{1,0:T(8,128)S(1)}, u32[]{:S(2)}, u32[]{:S(2)}) collective-permute-start(f32[256,128]{1,0:T(8,128)S(1)} %shard_map.104.pair.rows), channel_id=1, source_target_pairs={{0,8},{1,57},{8,16},{9,1},{16,24},{17,9},{24,32},{25,17},{32,40},{... | collective-permute-start | bytes 393224 | tf_op jit(solution)/shard_map/ppermute | solution.py:33
  15.6 4.1 %collective-permute-start.4 = (f32[128,128]{1,0:T(8,128)S(1)}, f32[128,128]{1,0:T(8,128)S(1)}, u32[]{:S(2)}, u32[]{:S(2)}) collective-permute-start(f32[128,128]{1,0:T(8,128)S(1)} %shard_map.107.rest_0_), channel_id=1, source_target_pairs={{0,8},{1,57},{8,16},{9,1},{16,24},{17,9},{24,32},{25,17},{32,40},{... | collective-permute-start | bytes 196616 | tf_op jit(solution)/shard_map/ppermute | solution.py:33
  19.7 4.2 %collective-permute-start.5 = (f32[1024,128]{1,0:T(8,128)S(1)}, f32[1024,128]{1,0:T(8,128)S(1)}, u32[]{:S(2)}, u32[]{:S(2)}) collective-permute-start(f32[1024,128]{1,0:T(8,128)S(1)} %shard_map.110.rows), channel_id=1, source_target_pairs={{0,1},{1,0},{2,3},{3,2},{4,5},{5,4},{6,7},{7,6},{8,9},{9,8},{10,11... | collective-permute-start | bytes 1572872 | tf_op jit(solution)/shard_map/ppermute | solution.py:25
  25.3 19.4 %copy-start = (bf16[512,512]{1,0:T(8,128)(2,1)S(1)}, bf16[512,512]{1,0:T(8,128)(2,1)}, u32[]{:S(2)}) copy-start(bf16[512,512]{1,0:T(8,128)(2,1)} %u.1) | copy-start | bytes 1572868
  25.3 19.4 %copy-start.1 = (bf16[512,512]{1,0:T(8,128)(2,1)S(1)}, bf16[512,512]{1,0:T(8,128)(2,1)}, u32[]{:S(2)}) copy-start(bf16[512,512]{1,0:T(8,128)(2,1)} %v.1) | copy-start | bytes 1572868
  25.3 19.4 %copy-start.2 = (bf16[128,512]{1,0:T(8,128)(2,1)S(1)}, bf16[128,512]{1,0:T(8,128)(2,1)}, u32[]{:S(2)}) copy-start(bf16[128,512]{1,0:T(8,128)(2,1)} %cot.1) | copy-start | bytes 393220
  25.3 19.4 %copy-start.4 = (f32[512]{0:T(512)S(1)}, f32[512]{0:T(512)}, u32[]{:S(2)}) copy-start(f32[512]{0:T(512)} %param.14) | copy-start | bytes 6148
  67.0 3.4 %collective-permute-start.6 = (f32[1024,128]{1,0:T(8,128)S(1)}, f32[1024,128]{1,0:T(8,128)S(1)}, u32[]{:S(2)}, u32[]{:S(2)}) collective-permute-start(f32[1024,128]{1,0:T(8,128)S(1)} %get-tuple-element.19), channel_id=1, source_target_pairs={{0,1},{1,0},{2,3},{3,2},{4,5},{5,4},{6,7},{7,6},{8,9},{9,8},{10,11... | collective-permute-start | bytes 1572872 | tf_op jit(solution)/shard_map/ppermute | solution.py:25
  68.8 18.3 %copy-start.5 = (f32[1,128]{1,0:T(1,128)S(1)}, f32[1,128]{1,0:T(1,128)}, u32[]{:S(2)}) copy-start(f32[1,128]{1,0:T(1,128)} %accum.1) | copy-start | bytes 1540
  70.4 5.4 %collective-permute-start.7 = (f32[128,128]{1,0:T(8,128)S(1)}, f32[128,128]{1,0:T(8,128)S(1)}, u32[]{:S(2)}, u32[]{:S(2)}) collective-permute-start(f32[128,128]{1,0:T(8,128)S(1)} %get-tuple-element.21), channel_id=1, source_target_pairs={{0,56},{1,9},{8,0},{9,17},{16,8},{17,25},{24,16},{25,33},{32,24},{... | collective-permute-start | bytes 196616 | tf_op jit(solution)/shard_map/ppermute | solution.py:33
  70.8 7.2 %collective-permute-start.9 = (f32[256,128]{1,0:T(8,128)S(1)}, f32[256,128]{1,0:T(8,128)S(1)}, u32[]{:S(2)}, u32[]{:S(2)}) collective-permute-start(f32[256,128]{1,0:T(8,128)S(1)} %get-tuple-element.22), channel_id=1, source_target_pairs={{0,48},{1,17},{8,56},{9,25},{16,0},{17,33},{24,8},{25,41},{32,16},... | collective-permute-start | bytes 393224 | tf_op jit(solution)/shard_map/ppermute | solution.py:33
  73.3 5.9 %collective-permute-start.10 = (f32[256,128]{1,0:T(8,128)S(1)}, f32[256,128]{1,0:T(8,128)S(1)}, u32[]{:S(2)}, u32[]{:S(2)}) collective-permute-start(f32[256,128]{1,0:T(8,128)S(1)} %get-tuple-element.23), channel_id=1, source_target_pairs={{0,56},{1,9},{8,0},{9,17},{16,8},{17,25},{24,16},{25,33},{32,24},{... | collective-permute-start | bytes 393224 | tf_op jit(solution)/shard_map/ppermute | solution.py:33
  75.8 9.9 %collective-permute-start.8 = (f32[256,128]{1,0:T(8,128)S(1)}, f32[256,128]{1,0:T(8,128)S(1)}, u32[]{:S(2)}, u32[]{:S(2)}) collective-permute-start(f32[256,128]{1,0:T(8,128)S(1)} %shard_map.117), channel_id=1, source_target_pairs={{0,40},{1,25},{8,48},{9,33},{16,56},{17,41},{24,0},{25,49},{32,8},... | collective-permute-start | bytes 393224 | tf_op jit(solution)/shard_map/ppermute | solution.py:33
  85.8 1.3 %collective-permute-start.11 = (f32[128,128]{1,0:T(8,128)S(1)}, f32[128,128]{1,0:T(8,128)S(1)}, u32[]{:S(2)}, u32[]{:S(2)}) collective-permute-start(f32[128,128]{1,0:T(8,128)S(1)} %get-tuple-element.26), channel_id=1, source_target_pairs={{0,1},{1,0},{2,3},{3,2},{4,5},{5,4},{6,7},{7,6},{8,9},{9,8},{10,11... | collective-permute-start | bytes 196616 | tf_op jit(solution)/shard_map/ppermute | solution.py:25

commit v6 on v5

--- a/solution.py
+++ b/solution.py
@@ -54,7 +54,7 @@
     for z in range(NZ):
         for c in range(NC):
             places = [place ^ (FLIP * c) for place in range(NX * NY)]
-            groups.append([((p // NY * NZ + z) * NY + p % NY) * NC + c for p in places])
+            groups.append([((p % NX * NZ + z) * NY + p // NX) * NC + c for p in places])
     return lax.all_to_all(
         parts, ("hst", "z", "y", "core"), split_axis=0, concat_axis=0, tiled=True, axis_index_groups=groups
     )
@@ -177,12 +177,12 @@
     for x, c in enumerate((c0, c1, c2, c3)):
         total = base[x] + pool_part(terms, c[HALF_ROWS:])
         for y in range(NY):
-            out[(x * NY + y) ^ flip] = total[:, y * SB : (y + 1) * SB].T
+            out[(y * NX + x) ^ flip] = total[:, y * SB : (y + 1) * SB].T
 
 
 def cross_kernel(parts, u, v, bias, cot, crossed, out):
     flip = own_flip()
-    x = [sum(parts[(t * NY + y) ^ flip] for y in range(1, NY)) + parts[(t * NY) ^ flip] for t in range(NX)]
+    x = [sum(parts[(y * NX + t) ^ flip] for y in range(1, NY)) + parts[t ^ flip] for t in range(NX)]
     base_x = jnp.concatenate(x, axis=1)
     low = jnp.dot(base_x.astype(BF16), u[...], preferred_element_type=F32).astype(BF16)
     scale = jnp.dot(low, v[...], preferred_element_type=F32) + bias[...]
@@ -196,7 +196,7 @@
     )
     for t in range(NX):
         for y in range(NY):
-            out[(t * NY + y) ^ flip] = grad_x[:, t * E : (t + 1) * E]
+            out[(y * NX + t) ^ flip] = grad_x[:, t * E : (t + 1) * E]
 
 
 def rows_grads(rows, terms, counts):
@@ -211,7 +211,7 @@
     flip = own_flip()
     for x in range(NX):
         for y in range(NY):
-            terms[x, y * SB : (y + 1) * SB] = split_terms(g[(x * NY + y) ^ flip])
+            terms[x, y * SB : (y + 1) * SB] = split_terms(g[(y * NX + x) ^ flip])
     out[...] = rows_grads(slice(HALF_ROWS, NC * HALF_ROWS), terms, (c0, c1, c2, c3))
 
 

time: 88.3 us -> 88.1 us (level)
  no operation moved by 1% of the time
where the time goes in v6:
time: 88.1 us; the launch traced here: 87.9 us
  blocking collectives  39.8 us (45%)
  starting transfers between devices  19.8 us (22%)
  waiting for transfers between devices  13 us (15%)
  Pallas kernels  12.7 us (14%)
  other arithmetic  0.95 us (1%)
    all_to_all x2, blocking collectives, exchange(): lax.all_to_all(parts, ('hst', 'z', 'y', 'core'), split_axis=0, concat_axi...  39.8 us
    ppermute x8, starting transfers between devices, move_ways(): return lax.ppermute(array, (axis, 'core'), pairs)  12.6 us
    ppermute x8, waiting for transfers between devices, move_ways(): return lax.ppermute(array, (axis, 'core'), pairs)  11.1 us
    pallas_call x11, Pallas kernels, call(): pl.pallas_call(kernel, in_specs=[vm] * len(operands), out_specs=[vm] * le...  7.46 us
    ppermute x4, starting transfers between devices, move(): return lax.ppermute(array, axis, [(i, (i + step) % n) for i in range(n)])  7.22 us
    pallas_call x4, Pallas kernels, counts_of(): pl.pallas_call(lambda s, v, *rest: counts_kernel(s, v, rest[-1]), grid=(1...  5.24 us
    ppermute x4, waiting for transfers between devices, move(): return lax.ppermute(array, axis, [(i, (i + step) % n) for i in range(n)])  1.88 us
  transfers between devices with their start and end apart: 12, of which 10 were waited for; matrix products, arithmetic and copies ran while one was open for 1% of the time, Pallas kernels for 9%

profile of v6, /device:TPU:1, one launch (start us, length us, event | category | flops | bytes accessed | tf_op | source)
XLA Modules:
  0.0 87.9 jit_solution(14490160804009069136)
XLA Ops:
  0.6 3.3 %collective-permute-start = (f32[128,128]{1,0:T(8,128)}, f32[128,128]{1,0:T(8,128)S(1)}, u32[]{:S(2)}, u32[]{:S(2)}) collective-permute-start(f32[128,128]{1,0:T(8,128)} %bitcast.100), channel_id=1, source_target_pairs={{0,1},{1,0},{2,3},{3,2},{4,5},{5,4},{6,7},{7,6},{8,9},{9,8},{10,11... | collective-permute-start | bytes 196616 | tf_op jit(solution)/shard_map/ppermute | solution.py:25
  5.1 4.8 %collective-permute-start.3 = (f32[256,128]{1,0:T(8,128)S(1)}, f32[256,128]{1,0:T(8,128)S(1)}, u32[]{:S(2)}, u32[]{:S(2)}) collective-permute-start(f32[256,128]{1,0:T(8,128)S(1)} %shard_map.104.pair.rows), channel_id=1, source_target_pairs={{0,24},{1,41},{8,32},{9,49},{16,40},{17,57},{24,48},{25,1},{32,56}... | collective-permute-start | bytes 393224 | tf_op jit(solution)/shard_map/ppermute | solution.py:33
  10.6 1.0 %fusion.4 = (f32[4,4,8,128]{3,2,1,0:T(8,128)S(1)}, s32[4,4,8,128]{3,2,1,0:T(8,128)S(1)}) fusion(s32[4,8,4,2,8,128]{5,4,3,2,1,0:T(8,128)} %bitcast.103, s32[]{:T(128)S(6)} %select_n.26, s32[]{:T(128)S(6)} %select_n.27, s32[4,8,4,2,8,128]{5,4,3,2,1,0:T(8,128)} %bitcast.104, s32[]{:T(128)S(6)} %axis_index.35, s32[]{:T(128)S(6)} %sub.23, s32[]{:T(128)S(6)} %axis_index.33, ...), kind=kLoop, calls=%fused_computation.7 | loop fusion | flops 557056 | bytes 262168 | tf_op jit(solution)/shard_map/convert_element_type | solution.py:86
  11.6 1.3 %shard_map.106.refs_1_.c1 = bf16[2048,512]{1,0:T(8,128)(2,1)S(1)} custom-call(s32[4,4,8,128]{3,2,1,0:T(8,128)S(1)} %get-tuple-element.30.s, f32[4,4,8,128]{3,2,1,0:T(8,128)S(1)} %get-tuple-element.29.v), custom_call_target="tpu_custom_call" | custom-call | bytes 1024 | tf_op jit(solution)/shard_map/pallas_call | solution.py:113
  12.9 1.3 %shard_map.105.refs_0_.c0 = bf16[2048,512]{1,0:T(8,128)(2,1)S(1)} custom-call(s32[4,4,8,128]{3,2,1,0:T(8,128)S(1)} %get-tuple-element.30.s, f32[4,4,8,128]{3,2,1,0:T(8,128)S(1)} %get-tuple-element.29.v), custom_call_target="tpu_custom_call" | custom-call | bytes 1024 | tf_op jit(solution)/shard_map/pallas_call | solution.py:113
  14.2 1.4 %collective-permute-done.3.three = f32[256,128]{1,0:T(8,128)S(1)} collective-permute-done((f32[256,128]{1,0:T(8,128)S(1)}, f32[256,128]{1,0:T(8,128)S(1)}, u32[]{:S(2)}, u32[]{:S(2)}) %collective-permute-start.3) | collective-permute-done | bytes 131104 | tf_op jit(solution)/shard_map/ppermute | solution.py:33
  16.0 1.3 %shard_map.109.refs_3_.c3 = bf16[2048,512]{1,0:T(8,128)(2,1)S(1)} custom-call(s32[4,4,8,128]{3,2,1,0:T(8,128)S(1)} %get-tuple-element.30.s, f32[4,4,8,128]{3,2,1,0:T(8,128)S(1)} %get-tuple-element.29.v, f32[128,128]{1,0:T(8,128)S(1)} %shard_map.107.rest_0_), custom_call_target="tpu_custom_call" | custom-call | bytes 1024 | tf_op jit(solution)/shard_map/pallas_call | solution.py:113
  17.3 1.3 %shard_map.108.refs_2_.c2 = bf16[2048,512]{1,0:T(8,128)(2,1)S(1)} custom-call(s32[4,4,8,128]{3,2,1,0:T(8,128)S(1)} %get-tuple-element.30.s, f32[4,4,8,128]{3,2,1,0:T(8,128)S(1)} %get-tuple-element.29.v, f32[128,128]{1,0:T(8,128)S(1)} %shard_map.107.rest_0_), custom_call_target="tpu_custom_call" | custom-call | bytes 1024 | tf_op jit(solution)/shard_map/pallas_call | solution.py:113
  19.7 2.6 %collective-permute-start.5 = (f32[1024,128]{1,0:T(8,128)S(1)}, f32[1024,128]{1,0:T(8,128)S(1)}, u32[]{:S(2)}, u32[]{:S(2)}) collective-permute-start(f32[1024,128]{1,0:T(8,128)S(1)} %shard_map.110.rows), channel_id=1, source_target_pairs={{0,1},{1,0},{2,3},{3,2},{4,5},{5,4},{6,7},{7,6},{8,9},{9,8},{10,11... | collective-permute-start | bytes 1572872 | tf_op jit(solution)/shard_map/ppermute | solution.py:25
  22.3 1.3 %shard_map.111.base = f32[4,128,512]{2,1,0:T(8,128)S(1)} custom-call(f32[1024,128]{1,0:T(8,128)S(1)} %shard_map.110.rows, bf16[2048,512]{1,0:T(8,128)(2,1)S(1)} %shard_map.105.refs_0_.c0, bf16[2048,512]{1,0:T(8,128)(2,1)S(1)} %shard_map.106.refs_1_.c1, bf16[2048,512]{1,0:T(8,128)(2,1)S(1)} %shard_map.108.refs_2_.c2, bf16[2048,512]{1,0:T(8,128)(2,1)S(1)} %shard_map.109.refs_3_.c3), custom_call_target="tpu_custom_call" | custom-call | bytes 1024 | tf_op jit(solution)/shard_map/pallas_call | solution.py:38
  23.8 1.4 %shard_map.112 = f32[16,128,128]{2,1,0:T(8,128)S(1)} custom-call(f32[1024,128]{1,0:T(8,128)S(1)} %collective-permute-done.5.rows, f32[4,128,512]{2,1,0:T(8,128)S(1)} %shard_map.111.base, bf16[2048,512]{1,0:T(8,128)(2,1)S(1)} %shard_map.105.refs_0_.c0, bf16[2048,512]{1,0:T(8,128)(2,1)S(1)} %shard_map.106.refs_1_.c1, ...), custom_call_target="tpu_custom_call" | custom-call | bytes 1024 | tf_op jit(solution)/shard_map/pallas_call | solution.py:38
  25.3 20.7 %all_to_all.10.parts = f32[16,128,128]{2,1,0:T(8,128)S(1)} all-to-all(f32[16,128,128]{2,1,0:T(8,128)S(1)} %shard_map.112), channel_id=1, replica_groups={{0,64,128,192,2,66,130,194,4,68,132,196,6,70,134,198},{133,197,5,69,135..., dimensions={0} | all-to-all | bytes 2097152 | tf_op jit(solution)/shard_map/all_to_all | solution.py:58
  46.1 1.3 %shard_map.113 = (bf16[128,512]{1,0:T(8,128)(2,1)}, f32[16,128,128]{2,1,0:T(8,128)S(1)}) custom-call(f32[16,128,128]{2,1,0:T(8,128)S(1)} %all_to_all.10.parts, bf16[512,512]{1,0:T(8,128)(2,1)S(1)} %copy-done, bf16[512,512]{1,0:T(8,128)(2,1)S(1)} %copy-done.1, f32[1,512]{1,0:T(1,128)S(1)} %bitcast.102, bf16[128,512]{1,0:T(8,128)(2,1)S(1)} %copy-done.2), custom_call_target="tpu_custom_call" | custom-call | bytes 1024 | tf_op jit(solution)/shard_map/pallas_call | solution.py:38
  47.3 19.1 %all_to_all.11.g = f32[16,128,128]{2,1,0:T(8,128)S(1)} all-to-all(f32[16,128,128]{2,1,0:T(8,128)S(1)} %get-tuple-element.17), channel_id=1, replica_groups={{0,64,128,192,2,66,130,194,4,68,132,196,6,70,134,198},{133,197,5,69,135..., dimensions={0} | all-to-all | bytes 2097152 | tf_op jit(solution)/shard_map/all_to_all | solution.py:58
  66.4 1.3 %shard_map.114 = (f32[1024,128]{1,0:T(8,128)S(1)}, bf16[4,512,256]{2,1,0:T(8,128)(2,1)S(1)}) custom-call(f32[16,128,128]{2,1,0:T(8,128)S(1)} %all_to_all.11.g, bf16[2048,512]{1,0:T(8,128)(2,1)S(1)} %shard_map.105.refs_0_.c0, bf16[2048,512]{1,0:T(8,128)(2,1)S(1)} %shard_map.106.refs_1_.c1, bf16[2048,512]{1,0:T(8,128)(2,1)S(1)} %shard_map.108.refs_2_.c2, ...), custom_call_target="tpu_custom_call" | custom-call | bytes 1024 | tf_op jit(solution)/shard_map/pallas_call | solution.py:38
  67.6 1.0 %collective-permute-start.6 = (f32[1024,128]{1,0:T(8,128)S(1)}, f32[1024,128]{1,0:T(8,128)S(1)}, u32[]{:S(2)}, u32[]{:S(2)}) collective-permute-start(f32[1024,128]{1,0:T(8,128)S(1)} %get-tuple-element.19), channel_id=1, source_target_pairs={{0,1},{1,0},{2,3},{3,2},{4,5},{5,4},{6,7},{7,6},{8,9},{9,8},{10,11... | collective-permute-start | bytes 1572872 | tf_op jit(solution)/shard_map/ppermute | solution.py:25
  68.7 1.2 %shard_map.115.a = f32[1024,128]{1,0:T(8,128)S(1)} custom-call(bf16[4,512,256]{2,1,0:T(8,128)(2,1)S(1)} %get-tuple-element.18.terms, bf16[2048,512]{1,0:T(8,128)(2,1)S(1)} %shard_map.105.refs_0_.c0, bf16[2048,512]{1,0:T(8,128)(2,1)S(1)} %shard_map.106.refs_1_.c1, bf16[2048,512]{1,0:T(8,128)(2,1)S(1)} %shard_map.108.refs_2_.c2, ...), custom_call_target="tpu_custom_call" | custom-call | bytes 1024 | tf_op jit(solution)/shard_map/pallas_call | solution.py:38
  70.6 2.5 %collective-permute-start.9 = (f32[256,128]{1,0:T(8,128)S(1)}, f32[256,128]{1,0:T(8,128)S(1)}, u32[]{:S(2)}, u32[]{:S(2)}) collective-permute-start(f32[256,128]{1,0:T(8,128)S(1)} %get-tuple-element.22), channel_id=1, source_target_pairs={{0,48},{1,17},{8,56},{9,25},{16,0},{17,33},{24,8},{25,41},{32,16},... | collective-permute-start | bytes 393224 | tf_op jit(solution)/shard_map/ppermute | solution.py:33
  73.2 2.5 %collective-permute-start.10 = (f32[256,128]{1,0:T(8,128)S(1)}, f32[256,128]{1,0:T(8,128)S(1)}, u32[]{:S(2)}, u32[]{:S(2)}) collective-permute-start(f32[256,128]{1,0:T(8,128)S(1)} %get-tuple-element.23), channel_id=1, source_target_pairs={{0,56},{1,9},{8,0},{9,17},{16,8},{17,25},{24,16},{25,33},{32,24},{... | collective-permute-start | bytes 393224 | tf_op jit(solution)/shard_map/ppermute | solution.py:33
  75.7 1.2 %collective-permute-start.8 = (f32[256,128]{1,0:T(8,128)S(1)}, f32[256,128]{1,0:T(8,128)S(1)}, u32[]{:S(2)}, u32[]{:S(2)}) collective-permute-start(f32[256,128]{1,0:T(8,128)S(1)} %shard_map.117), channel_id=1, source_target_pairs={{0,40},{1,25},{8,48},{9,33},{16,56},{17,41},{24,0},{25,49},{32,8},... | collective-permute-start | bytes 393224 | tf_op jit(solution)/shard_map/ppermute | solution.py:33
  76.9 1.0 %collective-permute-done.9.two = f32[256,128]{1,0:T(8,128)S(1)} collective-permute-done((f32[256,128]{1,0:T(8,128)S(1)}, f32[256,128]{1,0:T(8,128)S(1)}, u32[]{:S(2)}, u32[]{:S(2)}) %collective-permute-start.9) | collective-permute-done | bytes 131104 | tf_op jit(solution)/shard_map/ppermute | solution.py:33
  77.8 1.2 %collective-permute-done.10.one = f32[256,128]{1,0:T(8,128)S(1)} collective-permute-done((f32[256,128]{1,0:T(8,128)S(1)}, f32[256,128]{1,0:T(8,128)S(1)}, u32[]{:S(2)}, u32[]{:S(2)}) %collective-permute-start.10) | collective-permute-done | bytes 131104 | tf_op jit(solution)/shard_map/ppermute | solution.py:33
  79.0 6.6 %collective-permute-done.8.three = f32[256,128]{1,0:T(8,128)S(1)} collective-permute-done((f32[256,128]{1,0:T(8,128)S(1)}, f32[256,128]{1,0:T(8,128)S(1)}, u32[]{:S(2)}, u32[]{:S(2)}) %collective-permute-start.8) | collective-permute-done | bytes 131104 | tf_op jit(solution)/shard_map/ppermute | solution.py:33
  85.9 1.1 %collective-permute-done.11.b = f32[128,128]{1,0:T(8,128)S(1)} collective-permute-done((f32[128,128]{1,0:T(8,128)S(1)}, f32[128,128]{1,0:T(8,128)S(1)}, u32[]{:S(2)}, u32[]{:S(2)}) %collective-permute-start.11) | collective-permute-done | bytes 65568 | tf_op jit(solution)/shard_map/ppermute | solution.py:25
  (32 shorter events, 5.5 us)
Async XLA Ops:
  0.6 4.4 %collective-permute-start = (f32[128,128]{1,0:T(8,128)}, f32[128,128]{1,0:T(8,128)S(1)}, u32[]{:S(2)}, u32[]{:S(2)}) collective-permute-start(f32[128,128]{1,0:T(8,128)} %bitcast.100), channel_id=1, source_target_pairs={{0,1},{1,0},{2,3},{3,2},{4,5},{5,4},{6,7},{7,6},{8,9},{9,8},{10,11... | collective-permute-start | bytes 196616 | tf_op jit(solution)/shard_map/ppermute | solution.py:25
  4.0 0.8 copy-start.3
  5.1 10.5 %collective-permute-start.3 = (f32[256,128]{1,0:T(8,128)S(1)}, f32[256,128]{1,0:T(8,128)S(1)}, u32[]{:S(2)}, u32[]{:S(2)}) collective-permute-start(f32[256,128]{1,0:T(8,128)S(1)} %shard_map.104.pair.rows), channel_id=1, source_target_pairs={{0,24},{1,41},{8,32},{9,49},{16,40},{17,57},{24,48},{25,1},{32,56}... | collective-permute-start | bytes 393224 | tf_op jit(solution)/shard_map/ppermute | solution.py:33
  9.9 8.8 %collective-permute-start.2 = (f32[256,128]{1,0:T(8,128)S(1)}, f32[256,128]{1,0:T(8,128)S(1)}, u32[]{:S(2)}, u32[]{:S(2)}) collective-permute-start(f32[256,128]{1,0:T(8,128)S(1)} %shard_map.104.pair.rows), channel_id=1, source_target_pairs={{0,16},{1,49},{8,24},{9,57},{16,32},{17,1},{24,40},{25,9},{32,48},... | collective-permute-start | bytes 393224 | tf_op jit(solution)/shard_map/ppermute | solution.py:33
  10.2 8.7 %collective-permute-start.1 = (f32[256,128]{1,0:T(8,128)S(1)}, f32[256,128]{1,0:T(8,128)S(1)}, u32[]{:S(2)}, u32[]{:S(2)}) collective-permute-start(f32[256,128]{1,0:T(8,128)S(1)} %shard_map.104.pair.rows), channel_id=1, source_target_pairs={{0,8},{1,57},{8,16},{9,1},{16,24},{17,9},{24,32},{25,17},{32,40},{... | collective-permute-start | bytes 393224 | tf_op jit(solution)/shard_map/ppermute | solution.py:33
  15.6 4.1 %collective-permute-start.4 = (f32[128,128]{1,0:T(8,128)S(1)}, f32[128,128]{1,0:T(8,128)S(1)}, u32[]{:S(2)}, u32[]{:S(2)}) collective-permute-start(f32[128,128]{1,0:T(8,128)S(1)} %shard_map.107.rest_0_), channel_id=1, source_target_pairs={{0,8},{1,57},{8,16},{9,1},{16,24},{17,9},{24,32},{25,17},{32,40},{... | collective-permute-start | bytes 196616 | tf_op jit(solution)/shard_map/ppermute | solution.py:33
  19.7 4.2 %collective-permute-start.5 = (f32[1024,128]{1,0:T(8,128)S(1)}, f32[1024,128]{1,0:T(8,128)S(1)}, u32[]{:S(2)}, u32[]{:S(2)}) collective-permute-start(f32[1024,128]{1,0:T(8,128)S(1)} %shard_map.110.rows), channel_id=1, source_target_pairs={{0,1},{1,0},{2,3},{3,2},{4,5},{5,4},{6,7},{7,6},{8,9},{9,8},{10,11... | collective-permute-start | bytes 1572872 | tf_op jit(solution)/shard_map/ppermute | solution.py:25
  25.3 20.8 %copy-start = (bf16[512,512]{1,0:T(8,128)(2,1)S(1)}, bf16[512,512]{1,0:T(8,128)(2,1)}, u32[]{:S(2)}) copy-start(bf16[512,512]{1,0:T(8,128)(2,1)} %u.1) | copy-start | bytes 1572868
  25.3 20.8 %copy-start.1 = (bf16[512,512]{1,0:T(8,128)(2,1)S(1)}, bf16[512,512]{1,0:T(8,128)(2,1)}, u32[]{:S(2)}) copy-start(bf16[512,512]{1,0:T(8,128)(2,1)} %v.1) | copy-start | bytes 1572868
  25.3 20.8 %copy-start.2 = (bf16[128,512]{1,0:T(8,128)(2,1)S(1)}, bf16[128,512]{1,0:T(8,128)(2,1)}, u32[]{:S(2)}) copy-start(bf16[128,512]{1,0:T(8,128)(2,1)} %cot.1) | copy-start | bytes 393220
  25.3 20.8 %copy-start.4 = (f32[512]{0:T(512)S(1)}, f32[512]{0:T(512)}, u32[]{:S(2)}) copy-start(f32[512]{0:T(512)} %param.14) | copy-start | bytes 6148
  67.6 2.6 %collective-permute-start.6 = (f32[1024,128]{1,0:T(8,128)S(1)}, f32[1024,128]{1,0:T(8,128)S(1)}, u32[]{:S(2)}, u32[]{:S(2)}) collective-permute-start(f32[1024,128]{1,0:T(8,128)S(1)} %get-tuple-element.19), channel_id=1, source_target_pairs={{0,1},{1,0},{2,3},{3,2},{4,5},{5,4},{6,7},{7,6},{8,9},{9,8},{10,11... | collective-permute-start | bytes 1572872 | tf_op jit(solution)/shard_map/ppermute | solution.py:25
  68.7 18.3 %copy-start.5 = (f32[1,128]{1,0:T(1,128)S(1)}, f32[1,128]{1,0:T(1,128)}, u32[]{:S(2)}) copy-start(f32[1,128]{1,0:T(1,128)} %accum.1) | copy-start | bytes 1540
  70.3 5.4 %collective-permute-start.7 = (f32[128,128]{1,0:T(8,128)S(1)}, f32[128,128]{1,0:T(8,128)S(1)}, u32[]{:S(2)}, u32[]{:S(2)}) collective-permute-start(f32[128,128]{1,0:T(8,128)S(1)} %get-tuple-element.21), channel_id=1, source_target_pairs={{0,56},{1,9},{8,0},{9,17},{16,8},{17,25},{24,16},{25,33},{32,24},{... | collective-permute-start | bytes 196616 | tf_op jit(solution)/shard_map/ppermute | solution.py:33
  70.6 7.2 %collective-permute-start.9 = (f32[256,128]{1,0:T(8,128)S(1)}, f32[256,128]{1,0:T(8,128)S(1)}, u32[]{:S(2)}, u32[]{:S(2)}) collective-permute-start(f32[256,128]{1,0:T(8,128)S(1)} %get-tuple-element.22), channel_id=1, source_target_pairs={{0,48},{1,17},{8,56},{9,25},{16,0},{17,33},{24,8},{25,41},{32,16},... | collective-permute-start | bytes 393224 | tf_op jit(solution)/shard_map/ppermute | solution.py:33
  73.2 5.9 %collective-permute-start.10 = (f32[256,128]{1,0:T(8,128)S(1)}, f32[256,128]{1,0:T(8,128)S(1)}, u32[]{:S(2)}, u32[]{:S(2)}) collective-permute-start(f32[256,128]{1,0:T(8,128)S(1)} %get-tuple-element.23), channel_id=1, source_target_pairs={{0,56},{1,9},{8,0},{9,17},{16,8},{17,25},{24,16},{25,33},{32,24},{... | collective-permute-start | bytes 393224 | tf_op jit(solution)/shard_map/ppermute | solution.py:33
  75.7 9.9 %collective-permute-start.8 = (f32[256,128]{1,0:T(8,128)S(1)}, f32[256,128]{1,0:T(8,128)S(1)}, u32[]{:S(2)}, u32[]{:S(2)}) collective-permute-start(f32[256,128]{1,0:T(8,128)S(1)} %shard_map.117), channel_id=1, source_target_pairs={{0,40},{1,25},{8,48},{9,33},{16,56},{17,41},{24,0},{25,49},{32,8},... | collective-permute-start | bytes 393224 | tf_op jit(solution)/shard_map/ppermute | solution.py:33
  85.6 1.3 %collective-permute-start.11 = (f32[128,128]{1,0:T(8,128)S(1)}, f32[128,128]{1,0:T(8,128)S(1)}, u32[]{:S(2)}, u32[]{:S(2)}) collective-permute-start(f32[128,128]{1,0:T(8,128)S(1)} %get-tuple-element.26), channel_id=1, source_target_pairs={{0,1},{1,0},{2,3},{3,2},{4,5},{5,4},{6,7},{7,6},{8,9},{9,8},{10,11... | collective-permute-start | bytes 196616 | tf_op jit(solution)/shard_map/ppermute | solution.py:25

commit v7 on v6

--- a/solution.py
+++ b/solution.py
@@ -255,9 +255,11 @@
     other = move(own, "core", 1)
     (held,) = call(copy_kernel, [((RB, E), F32)], own)
     (pair,) = call(pair_kernel, [((2 * RB, E), F32)], held, other)
-    three, two, one = (move_ways(pair, "z", s) for s in (3, 2, 1))
+    three = move_ways(pair, "z", 3)
     entries = entries_of(row_ids, sketch_bits)
     counts = [counts_of(entries, x) for x in range(2)]
+    (later,) = call_after(copy_kernel, [(2 * RB, E)], (pair,), counts)
+    two, one = (move_ways(later, "z", s) for s in (2, 1))
     (onward,) = call_after(onward_kernel, [(RB, E)], (three,), counts)
     four = move_ways(onward, "z", 1)
     counts = counts + [counts_of(entries, x, onward) for x in range(2, NX)]

time: 88.1 us -> 86.5 us (0.982)
  starting transfers between devices: 19.8 us -> 16.7 us
  waiting for transfers between devices: 13 us -> 14 us
    ppermute x8, starting transfers between devices: 12.6 us -> 10.8 us  [move_ways(): return lax.ppermute(array, (axis, 'core'), pairs)]
    ppermute x4, starting transfers between devices: 7.22 us -> 5.95 us  [move(): return lax.ppermute(array, axis, [(i, (i + step) % n) for i in range(n)])]
    ppermute x8, waiting for transfers between devices: 11.1 us -> 12 us  [move_ways(): return lax.ppermute(array, (axis, 'core'), pairs)]
  transfers between devices with their start and end apart: 12 -> 12, of which waited for: 10 -> 12; matrix products, arithmetic and copies ran while one was open for 1% -> 1% of each run, Pallas kernels for 9% -> 9%
where the time goes in v7:
time: 86.5 us; the launch traced here: 86 us
  blocking collectives  39.8 us (46%)
  starting transfers between devices  16.7 us (19%)
  waiting for transfers between devices  14 us (16%)
  Pallas kernels  12.8 us (15%)
  other arithmetic  0.95 us (1%)
  local copies, waits for them, and re-layouts  0.87 us (1%)
    all_to_all x2, blocking collectives, exchange(): lax.all_to_all(parts, ('hst', 'z', 'y', 'core'), split_axis=0, concat_axi...  39.8 us
    ppermute x8, waiting for transfers between devices, move_ways(): return lax.ppermute(array, (axis, 'core'), pairs)  12 us
    ppermute x8, starting transfers between devices, move_ways(): return lax.ppermute(array, (axis, 'core'), pairs)  10.8 us
    pallas_call x11, Pallas kernels, call(): pl.pallas_call(kernel, in_specs=[vm] * len(operands), out_specs=[vm] * le...  7.46 us
    ppermute x4, starting transfers between devices, move(): return lax.ppermute(array, axis, [(i, (i + step) % n) for i in range(n)])  5.95 us
    pallas_call x4, Pallas kernels, counts_of(): pl.pallas_call(lambda s, v, *rest: counts_kernel(s, v, rest[-1]), grid=(1...  5.24 us
    ppermute x4, waiting for transfers between devices, move(): return lax.ppermute(array, axis, [(i, (i + step) % n) for i in range(n)])  2 us
  transfers between devices with their start and end apart: 12, of which 12 were waited for; matrix products, arithmetic and copies ran while one was open for 1% of the time, Pallas kernels for 9%

profile of v7, /device:TPU:1, one launch (start us, length us, event | category | flops | bytes accessed | tf_op | source)
XLA Modules:
  0.0 86.0 jit_solution(13889958766446629578)
XLA Ops:
  0.6 3.3 %collective-permute-start = (f32[128,128]{1,0:T(8,128)}, f32[128,128]{1,0:T(8,128)S(1)}, u32[]{:S(2)}, u32[]{:S(2)}) collective-permute-start(f32[128,128]{1,0:T(8,128)} %bitcast.100), channel_id=1, source_target_pairs={{0,1},{1,0},{2,3},{3,2},{4,5},{5,4},{6,7},{7,6},{8,9},{9,8},{10,11... | collective-permute-start | bytes 196616 | tf_op jit(solution)/shard_map/ppermute | solution.py:25
  5.1 4.8 %collective-permute-start.3 = (f32[256,128]{1,0:T(8,128)S(1)}, f32[256,128]{1,0:T(8,128)S(1)}, u32[]{:S(2)}, u32[]{:S(2)}) collective-permute-start(f32[256,128]{1,0:T(8,128)S(1)} %shard_map.104.a.pair.rows), channel_id=1, source_target_pairs={{0,24},{1,41},{8,32},{9,49},{16,40},{17,57},{24,48},{25,1},{32,56}... | collective-permute-start | bytes 393224 | tf_op jit(solution)/shard_map/ppermute | solution.py:33
  10.8 1.3 %shard_map.106.refs_1_.c1 = bf16[2048,512]{1,0:T(8,128)(2,1)S(1)} custom-call(s32[4,4,8,128]{3,2,1,0:T(8,128)S(1)} %get-tuple-element.30.s, f32[4,4,8,128]{3,2,1,0:T(8,128)S(1)} %get-tuple-element.29.v), custom_call_target="tpu_custom_call" | custom-call | bytes 1024 | tf_op jit(solution)/shard_map/pallas_call | solution.py:113
  12.2 1.3 %shard_map.105.refs_0_.c0 = bf16[2048,512]{1,0:T(8,128)(2,1)S(1)} custom-call(s32[4,4,8,128]{3,2,1,0:T(8,128)S(1)} %get-tuple-element.30.s, f32[4,4,8,128]{3,2,1,0:T(8,128)S(1)} %get-tuple-element.29.v), custom_call_target="tpu_custom_call" | custom-call | bytes 1024 | tf_op jit(solution)/shard_map/pallas_call | solution.py:113
  14.6 1.4 %collective-permute-start.4 = (f32[128,128]{1,0:T(8,128)S(1)}, f32[128,128]{1,0:T(8,128)S(1)}, u32[]{:S(2)}, u32[]{:S(2)}) collective-permute-start(f32[128,128]{1,0:T(8,128)S(1)} %shard_map.108.rest_0_), channel_id=1, source_target_pairs={{0,8},{1,57},{8,16},{9,1},{16,24},{17,9},{24,32},{25,17},{32,40},{... | collective-permute-start | bytes 196616 | tf_op jit(solution)/shard_map/ppermute | solution.py:33
  16.0 1.3 %shard_map.110.refs_3_.c3 = bf16[2048,512]{1,0:T(8,128)(2,1)S(1)} custom-call(s32[4,4,8,128]{3,2,1,0:T(8,128)S(1)} %get-tuple-element.30.s, f32[4,4,8,128]{3,2,1,0:T(8,128)S(1)} %get-tuple-element.29.v, f32[128,128]{1,0:T(8,128)S(1)} %shard_map.108.rest_0_), custom_call_target="tpu_custom_call" | custom-call | bytes 1024 | tf_op jit(solution)/shard_map/pallas_call | solution.py:113
  17.3 1.3 %shard_map.109.refs_2_.c2 = bf16[2048,512]{1,0:T(8,128)(2,1)S(1)} custom-call(s32[4,4,8,128]{3,2,1,0:T(8,128)S(1)} %get-tuple-element.30.s, f32[4,4,8,128]{3,2,1,0:T(8,128)S(1)} %get-tuple-element.29.v, f32[128,128]{1,0:T(8,128)S(1)} %shard_map.108.rest_0_), custom_call_target="tpu_custom_call" | custom-call | bytes 1024 | tf_op jit(solution)/shard_map/pallas_call | solution.py:113
  18.7 1.1 %collective-permute-done.2.two = f32[256,128]{1,0:T(8,128)S(1)} collective-permute-done((f32[256,128]{1,0:T(8,128)S(1)}, f32[256,128]{1,0:T(8,128)S(1)}, u32[]{:S(2)}, u32[]{:S(2)}) %collective-permute-start.2) | collective-permute-done | bytes 131104 | tf_op jit(solution)/shard_map/ppermute | solution.py:33
  19.8 1.1 %collective-permute-done.1.one = f32[256,128]{1,0:T(8,128)S(1)} collective-permute-done((f32[256,128]{1,0:T(8,128)S(1)}, f32[256,128]{1,0:T(8,128)S(1)}, u32[]{:S(2)}, u32[]{:S(2)}) %collective-permute-start.1) | collective-permute-done | bytes 131104 | tf_op jit(solution)/shard_map/ppermute | solution.py:33
  21.7 1.5 %collective-permute-start.5 = (f32[1024,128]{1,0:T(8,128)S(1)}, f32[1024,128]{1,0:T(8,128)S(1)}, u32[]{:S(2)}, u32[]{:S(2)}) collective-permute-start(f32[1024,128]{1,0:T(8,128)S(1)} %shard_map.111.rows), channel_id=1, source_target_pairs={{0,1},{1,0},{2,3},{3,2},{4,5},{5,4},{6,7},{7,6},{8,9},{9,8},{10,11... | collective-permute-start | bytes 1572872 | tf_op jit(solution)/shard_map/ppermute | solution.py:25
  23.2 1.3 %shard_map.112.base = f32[4,128,512]{2,1,0:T(8,128)S(1)} custom-call(f32[1024,128]{1,0:T(8,128)S(1)} %shard_map.111.rows, bf16[2048,512]{1,0:T(8,128)(2,1)S(1)} %shard_map.105.refs_0_.c0, bf16[2048,512]{1,0:T(8,128)(2,1)S(1)} %shard_map.106.refs_1_.c1, bf16[2048,512]{1,0:T(8,128)(2,1)S(1)} %shard_map.109.refs_2_.c2, bf16[2048,512]{1,0:T(8,128)(2,1)S(1)} %shard_map.110.refs_3_.c3), custom_call_target="tpu_custom_call" | custom-call | bytes 1024 | tf_op jit(solution)/shard_map/pallas_call | solution.py:38
  24.7 1.4 %shard_map.113 = f32[16,128,128]{2,1,0:T(8,128)S(1)} custom-call(f32[1024,128]{1,0:T(8,128)S(1)} %collective-permute-done.5.rows, f32[4,128,512]{2,1,0:T(8,128)S(1)} %shard_map.112.base, bf16[2048,512]{1,0:T(8,128)(2,1)S(1)} %shard_map.105.refs_0_.c0, bf16[2048,512]{1,0:T(8,128)(2,1)S(1)} %shard_map.106.refs_1_.c1, ...), custom_call_target="tpu_custom_call" | custom-call | bytes 1024 | tf_op jit(solution)/shard_map/pallas_call | solution.py:38
  26.2 20.8 %all_to_all.10.parts = f32[16,128,128]{2,1,0:T(8,128)S(1)} all-to-all(f32[16,128,128]{2,1,0:T(8,128)S(1)} %shard_map.113), channel_id=1, replica_groups={{0,64,128,192,2,66,130,194,4,68,132,196,6,70,134,198},{133,197,5,69,135..., dimensions={0} | all-to-all | bytes 2097152 | tf_op jit(solution)/shard_map/all_to_all | solution.py:58
  46.9 1.3 %shard_map.114 = (bf16[128,512]{1,0:T(8,128)(2,1)}, f32[16,128,128]{2,1,0:T(8,128)S(1)}) custom-call(f32[16,128,128]{2,1,0:T(8,128)S(1)} %all_to_all.10.parts, bf16[512,512]{1,0:T(8,128)(2,1)S(1)} %copy-done, bf16[512,512]{1,0:T(8,128)(2,1)S(1)} %copy-done.1, f32[1,512]{1,0:T(1,128)S(1)} %bitcast.102, bf16[128,512]{1,0:T(8,128)(2,1)S(1)} %copy-done.2), custom_call_target="tpu_custom_call" | custom-call | bytes 1024 | tf_op jit(solution)/shard_map/pallas_call | solution.py:38
  48.2 19.1 %all_to_all.11.g = f32[16,128,128]{2,1,0:T(8,128)S(1)} all-to-all(f32[16,128,128]{2,1,0:T(8,128)S(1)} %get-tuple-element.17), channel_id=1, replica_groups={{0,64,128,192,2,66,130,194,4,68,132,196,6,70,134,198},{133,197,5,69,135..., dimensions={0} | all-to-all | bytes 2097152 | tf_op jit(solution)/shard_map/all_to_all | solution.py:58
  67.3 1.3 %shard_map.115 = (f32[1024,128]{1,0:T(8,128)S(1)}, bf16[4,512,256]{2,1,0:T(8,128)(2,1)S(1)}) custom-call(f32[16,128,128]{2,1,0:T(8,128)S(1)} %all_to_all.11.g, bf16[2048,512]{1,0:T(8,128)(2,1)S(1)} %shard_map.105.refs_0_.c0, bf16[2048,512]{1,0:T(8,128)(2,1)S(1)} %shard_map.106.refs_1_.c1, bf16[2048,512]{1,0:T(8,128)(2,1)S(1)} %shard_map.109.refs_2_.c2, ...), custom_call_target="tpu_custom_call" | custom-call | bytes 1024 | tf_op jit(solution)/shard_map/pallas_call | solution.py:38
  68.5 1.0 %collective-permute-start.6 = (f32[1024,128]{1,0:T(8,128)S(1)}, f32[1024,128]{1,0:T(8,128)S(1)}, u32[]{:S(2)}, u32[]{:S(2)}) collective-permute-start(f32[1024,128]{1,0:T(8,128)S(1)} %get-tuple-element.19), channel_id=1, source_target_pairs={{0,1},{1,0},{2,3},{3,2},{4,5},{5,4},{6,7},{7,6},{8,9},{9,8},{10,11... | collective-permute-start | bytes 1572872 | tf_op jit(solution)/shard_map/ppermute | solution.py:25
  69.5 1.2 %shard_map.116.a = f32[1024,128]{1,0:T(8,128)S(1)} custom-call(bf16[4,512,256]{2,1,0:T(8,128)(2,1)S(1)} %get-tuple-element.18.terms, bf16[2048,512]{1,0:T(8,128)(2,1)S(1)} %shard_map.105.refs_0_.c0, bf16[2048,512]{1,0:T(8,128)(2,1)S(1)} %shard_map.106.refs_1_.c1, bf16[2048,512]{1,0:T(8,128)(2,1)S(1)} %shard_map.109.refs_2_.c2, ...), custom_call_target="tpu_custom_call" | custom-call | bytes 1024 | tf_op jit(solution)/shard_map/pallas_call | solution.py:38
  72.1 1.1 %collective-permute-start.9 = (f32[256,128]{1,0:T(8,128)S(1)}, f32[256,128]{1,0:T(8,128)S(1)}, u32[]{:S(2)}, u32[]{:S(2)}) collective-permute-start(f32[256,128]{1,0:T(8,128)S(1)} %get-tuple-element.22), channel_id=1, source_target_pairs={{0,48},{1,17},{8,56},{9,25},{16,0},{17,33},{24,8},{25,41},{32,16},... | collective-permute-start | bytes 393224 | tf_op jit(solution)/shard_map/ppermute | solution.py:33
  73.2 1.0 %collective-permute-start.10 = (f32[256,128]{1,0:T(8,128)S(1)}, f32[256,128]{1,0:T(8,128)S(1)}, u32[]{:S(2)}, u32[]{:S(2)}) collective-permute-start(f32[256,128]{1,0:T(8,128)S(1)} %get-tuple-element.23), channel_id=1, source_target_pairs={{0,56},{1,9},{8,0},{9,17},{16,8},{17,25},{24,16},{25,33},{32,24},{... | collective-permute-start | bytes 393224 | tf_op jit(solution)/shard_map/ppermute | solution.py:33
  74.2 1.3 %collective-permute-done.7.four = f32[128,128]{1,0:T(8,128)S(1)} collective-permute-done((f32[128,128]{1,0:T(8,128)S(1)}, f32[128,128]{1,0:T(8,128)S(1)}, u32[]{:S(2)}, u32[]{:S(2)}) %collective-permute-start.7) | collective-permute-done | bytes 65568 | tf_op jit(solution)/shard_map/ppermute | solution.py:33
  76.2 3.4 %collective-permute-done.9.two = f32[256,128]{1,0:T(8,128)S(1)} collective-permute-done((f32[256,128]{1,0:T(8,128)S(1)}, f32[256,128]{1,0:T(8,128)S(1)}, u32[]{:S(2)}, u32[]{:S(2)}) %collective-permute-start.9) | collective-permute-done | bytes 131104 | tf_op jit(solution)/shard_map/ppermute | solution.py:33
  80.3 3.4 %collective-permute-done.8.three = f32[256,128]{1,0:T(8,128)S(1)} collective-permute-done((f32[256,128]{1,0:T(8,128)S(1)}, f32[256,128]{1,0:T(8,128)S(1)}, u32[]{:S(2)}, u32[]{:S(2)}) %collective-permute-start.8) | collective-permute-done | bytes 131104 | tf_op jit(solution)/shard_map/ppermute | solution.py:33
  83.8 1.2 %collective-permute-done.11.b = f32[128,128]{1,0:T(8,128)S(1)} collective-permute-done((f32[128,128]{1,0:T(8,128)S(1)}, f32[128,128]{1,0:T(8,128)S(1)}, u32[]{:S(2)}, u32[]{:S(2)}) %collective-permute-start.11) | collective-permute-done | bytes 65568 | tf_op jit(solution)/shard_map/ppermute | solution.py:25
  (33 shorter events, 7.9 us)
Async XLA Ops:
  0.6 4.4 %collective-permute-start = (f32[128,128]{1,0:T(8,128)}, f32[128,128]{1,0:T(8,128)S(1)}, u32[]{:S(2)}, u32[]{:S(2)}) collective-permute-start(f32[128,128]{1,0:T(8,128)} %bitcast.100), channel_id=1, source_target_pairs={{0,1},{1,0},{2,3},{3,2},{4,5},{5,4},{6,7},{7,6},{8,9},{9,8},{10,11... | collective-permute-start | bytes 196616 | tf_op jit(solution)/shard_map/ppermute | solution.py:25
  4.0 0.8 copy-start.3
  5.1 9.5 %collective-permute-start.3 = (f32[256,128]{1,0:T(8,128)S(1)}, f32[256,128]{1,0:T(8,128)S(1)}, u32[]{:S(2)}, u32[]{:S(2)}) collective-permute-start(f32[256,128]{1,0:T(8,128)S(1)} %shard_map.104.a.pair.rows), channel_id=1, source_target_pairs={{0,24},{1,41},{8,32},{9,49},{16,40},{17,57},{24,48},{25,1},{32,56}... | collective-permute-start | bytes 393224 | tf_op jit(solution)/shard_map/ppermute | solution.py:33
  13.5 6.3 %collective-permute-start.2 = (f32[256,128]{1,0:T(8,128)S(1)}, f32[256,128]{1,0:T(8,128)S(1)}, u32[]{:S(2)}, u32[]{:S(2)}) collective-permute-start(f32[256,128]{1,0:T(8,128)S(1)} %shard_map.107), channel_id=1, source_target_pairs={{0,16},{1,49},{8,24},{9,57},{16,32},{17,1},{24,40},{25,9},{32,48},... | collective-permute-start | bytes 393224 | tf_op jit(solution)/shard_map/ppermute | solution.py:33
  13.8 7.1 %collective-permute-start.1 = (f32[256,128]{1,0:T(8,128)S(1)}, f32[256,128]{1,0:T(8,128)S(1)}, u32[]{:S(2)}, u32[]{:S(2)}) collective-permute-start(f32[256,128]{1,0:T(8,128)S(1)} %shard_map.107), channel_id=1, source_target_pairs={{0,8},{1,57},{8,16},{9,1},{16,24},{17,9},{24,32},{25,17},{32,40},{... | collective-permute-start | bytes 393224 | tf_op jit(solution)/shard_map/ppermute | solution.py:33
  14.6 7.0 %collective-permute-start.4 = (f32[128,128]{1,0:T(8,128)S(1)}, f32[128,128]{1,0:T(8,128)S(1)}, u32[]{:S(2)}, u32[]{:S(2)}) collective-permute-start(f32[128,128]{1,0:T(8,128)S(1)} %shard_map.108.rest_0_), channel_id=1, source_target_pairs={{0,8},{1,57},{8,16},{9,1},{16,24},{17,9},{24,32},{25,17},{32,40},{... | collective-permute-start | bytes 196616 | tf_op jit(solution)/shard_map/ppermute | solution.py:33
  21.7 3.0 %collective-permute-start.5 = (f32[1024,128]{1,0:T(8,128)S(1)}, f32[1024,128]{1,0:T(8,128)S(1)}, u32[]{:S(2)}, u32[]{:S(2)}) collective-permute-start(f32[1024,128]{1,0:T(8,128)S(1)} %shard_map.111.rows), channel_id=1, source_target_pairs={{0,1},{1,0},{2,3},{3,2},{4,5},{5,4},{6,7},{7,6},{8,9},{9,8},{10,11... | collective-permute-start | bytes 1572872 | tf_op jit(solution)/shard_map/ppermute | solution.py:25
  26.1 20.8 %copy-start = (bf16[512,512]{1,0:T(8,128)(2,1)S(1)}, bf16[512,512]{1,0:T(8,128)(2,1)}, u32[]{:S(2)}) copy-start(bf16[512,512]{1,0:T(8,128)(2,1)} %u.1) | copy-start | bytes 1572868
  26.1 20.8 %copy-start.1 = (bf16[512,512]{1,0:T(8,128)(2,1)S(1)}, bf16[512,512]{1,0:T(8,128)(2,1)}, u32[]{:S(2)}) copy-start(bf16[512,512]{1,0:T(8,128)(2,1)} %v.1) | copy-start | bytes 1572868
  26.1 20.8 %copy-start.2 = (bf16[128,512]{1,0:T(8,128)(2,1)S(1)}, bf16[128,512]{1,0:T(8,128)(2,1)}, u32[]{:S(2)}) copy-start(bf16[128,512]{1,0:T(8,128)(2,1)} %cot.1) | copy-start | bytes 393220
  26.2 20.8 %copy-start.4 = (f32[512]{0:T(512)S(1)}, f32[512]{0:T(512)}, u32[]{:S(2)}) copy-start(f32[512]{0:T(512)} %param.14) | copy-start | bytes 6148
  68.5 2.6 %collective-permute-start.6 = (f32[1024,128]{1,0:T(8,128)S(1)}, f32[1024,128]{1,0:T(8,128)S(1)}, u32[]{:S(2)}, u32[]{:S(2)}) collective-permute-start(f32[1024,128]{1,0:T(8,128)S(1)} %get-tuple-element.19), channel_id=1, source_target_pairs={{0,1},{1,0},{2,3},{3,2},{4,5},{5,4},{6,7},{7,6},{8,9},{9,8},{10,11... | collective-permute-start | bytes 1572872 | tf_op jit(solution)/shard_map/ppermute | solution.py:25
  69.5 15.5 %copy-start.5 = (f32[1,128]{1,0:T(1,128)S(1)}, f32[1,128]{1,0:T(1,128)}, u32[]{:S(2)}) copy-start(f32[1,128]{1,0:T(1,128)} %accum.1) | copy-start | bytes 1540
  71.1 4.4 %collective-permute-start.7 = (f32[128,128]{1,0:T(8,128)S(1)}, f32[128,128]{1,0:T(8,128)S(1)}, u32[]{:S(2)}, u32[]{:S(2)}) collective-permute-start(f32[128,128]{1,0:T(8,128)S(1)} %get-tuple-element.21), channel_id=1, source_target_pairs={{0,56},{1,9},{8,0},{9,17},{16,8},{17,25},{24,16},{25,33},{32,24},{... | collective-permute-start | bytes 196616 | tf_op jit(solution)/shard_map/ppermute | solution.py:33
  72.1 7.4 %collective-permute-start.9 = (f32[256,128]{1,0:T(8,128)S(1)}, f32[256,128]{1,0:T(8,128)S(1)}, u32[]{:S(2)}, u32[]{:S(2)}) collective-permute-start(f32[256,128]{1,0:T(8,128)S(1)} %get-tuple-element.22), channel_id=1, source_target_pairs={{0,48},{1,17},{8,56},{9,25},{16,0},{17,33},{24,8},{25,41},{32,16},... | collective-permute-start | bytes 393224 | tf_op jit(solution)/shard_map/ppermute | solution.py:33
  73.2 7.1 %collective-permute-start.10 = (f32[256,128]{1,0:T(8,128)S(1)}, f32[256,128]{1,0:T(8,128)S(1)}, u32[]{:S(2)}, u32[]{:S(2)}) collective-permute-start(f32[256,128]{1,0:T(8,128)S(1)} %get-tuple-element.23), channel_id=1, source_target_pairs={{0,56},{1,9},{8,0},{9,17},{16,8},{17,25},{24,16},{25,33},{32,24},{... | collective-permute-start | bytes 393224 | tf_op jit(solution)/shard_map/ppermute | solution.py:33
  75.6 8.1 %collective-permute-start.8 = (f32[256,128]{1,0:T(8,128)S(1)}, f32[256,128]{1,0:T(8,128)S(1)}, u32[]{:S(2)}, u32[]{:S(2)}) collective-permute-start(f32[256,128]{1,0:T(8,128)S(1)} %shard_map.118), channel_id=1, source_target_pairs={{0,40},{1,25},{8,48},{9,33},{16,56},{17,41},{24,0},{25,49},{32,8},... | collective-permute-start | bytes 393224 | tf_op jit(solution)/shard_map/ppermute | solution.py:33
  83.7 1.3 %collective-permute-start.11 = (f32[128,128]{1,0:T(8,128)S(1)}, f32[128,128]{1,0:T(8,128)S(1)}, u32[]{:S(2)}, u32[]{:S(2)}) collective-permute-start(f32[128,128]{1,0:T(8,128)S(1)} %get-tuple-element.26), channel_id=1, source_target_pairs={{0,1},{1,0},{2,3},{3,2},{4,5},{5,4},{6,7},{7,6},{8,9},{9,8},{10,11... | collective-permute-start | bytes 196616 | tf_op jit(solution)/shard_map/ppermute | solution.py:25
